TPU v7x, 128 devices: a whole 4x4x4 slice. The times are simulated.
128 devices in a mesh: seq: 32 (over z, y, x_lo), dp: 4 (over x_hi, core).
Axes of the slice: x: 4 (x_hi: 2, x_lo: 2; x = x_hi * 2 + x_lo), y: 4, z: 4, core: 2. Of those that a mesh axis runs over, the one named last changes fastest.
Arguments:
- clips: bfloat16 [4, 32, 256, 1152], P('dp', 'seq'), may hold values from -6 to 6
- cotangent: bfloat16 [4, 32, 256, 1152], P('dp', 'seq'), may hold values from -6 to 6
- w_qkv_space: bfloat16 [1152, 1728], replicated, may hold values from -0.1875 to 0.1875
- w_out_space: bfloat16 [1152, 576], replicated, may hold values from -0.25 to 0.25
- w_qkv_time: bfloat16 [1152, 1728], replicated, may hold values from -0.1875 to 0.1875
- w_out_time: bfloat16 [1152, 576], replicated, may hold values from -0.25 to 0.25
Outputs:
- mixed: bfloat16 [4, 32, 256, 1152], P('dp', 'seq')
- grad_clips: bfloat16 [4, 32, 256, 1152], P('dp', 'seq')
- grad_qkv_space: float32 [1152, 1728], P(('seq', 'dp'))
- grad_out_space: float32 [1152, 576], P(('seq', 'dp'))
- grad_qkv_time: float32 [1152, 1728], P(('seq', 'dp'))
- grad_out_time: float32 [1152, 576], P(('seq', 'dp'))
All inputs are finite; a program needn't handle non-finite values.
Results may differ from a plain program's by a relative error of at most 0.022.
Values may be sent and summed in bfloat16 or wider, within the bound.
No kernel may reach another device: no remote copies, remote signals or barrier semaphores. Data moves between devices by JAX's collectives and lax.ppermute only.
A program may use at most 128 MiB of HBM per device.

v0:
```python
import functools
import math

import jax
import jax.numpy as jnp
import numpy as np
from jax import lax
from jax.experimental import pallas as pl
from jax.experimental.pallas import tpu as pltpu
from jax.sharding import Mesh
from jax.sharding import PartitionSpec as P

HEADS = 8
HEAD_DIM = 72
HK = HEADS * HEAD_DIM
EPS = 1e-06
LANES = 128
F32 = jnp.float32
BF16 = jnp.bfloat16


def windows():
    out = []
    for head in range(HEADS):
        low, high = head * HEAD_DIM, (head + 1) * HEAD_DIM
        start = low // LANES * LANES
        stop = min(-(-high // LANES) * LANES, HK)
        out.append((low, high, start, stop))
    return out


def dot_nn(a, b):
    return lax.dot_general(a, b, (((1,), (0,)), ((), ())), preferred_element_type=F32)


def dot_nt(a, b):
    return lax.dot_general(a, b, (((1,), (1,)), ((), ())), preferred_element_type=F32)


def dot_tn(a, b):
    return lax.dot_general(a, b, (((0,), (0,)), ((), ())), preferred_element_type=F32)


def norm_parts(tokens):
    center = tokens - jnp.mean(tokens, axis=-1, keepdims=True)
    spread = jnp.mean(center * center, axis=-1, keepdims=True)
    rate = lax.rsqrt(spread + EPS)
    return center * rate, rate


def norm_back(grad, normed, rate):
    first = jnp.mean(grad, axis=-1, keepdims=True)
    second = jnp.mean(grad * normed, axis=-1, keepdims=True)
    return rate * (grad - first - normed * second)


def split_qkv(qkv):
    return qkv[:, :HK], qkv[:, HK : 2 * HK], qkv[:, 2 * HK :]


class HeadSum:
    def __init__(self):
        self.slabs = [None] * -(-HK // LANES)

    def put(self, head, piece):
        low, high, start, stop = windows()[head]
        for slab in range(start // LANES, -(-stop // LANES)):
            left, right = slab * LANES, min((slab + 1) * LANES, HK)
            part = piece[:, left - start : right - start]
            held = self.slabs[slab]
            if held is not None:
                lane = left + lax.broadcasted_iota(jnp.int32, part.shape, 1)
                part = jnp.where((lane >= low) & (lane < high), part, held)
            self.slabs[slab] = part

    def whole(self, dtype):
        return jnp.concatenate([slab.astype(dtype) for slab in self.slabs], axis=1)


def head_part(array, head):
    low, high, start, stop = windows()[head]
    part = array[:, start:stop]
    lane = start + lax.broadcasted_iota(jnp.int32, part.shape, 1)
    return jnp.where((lane >= low) & (lane < high), part, jnp.zeros_like(part))


def head_window(array, head):
    _, _, start, stop = windows()[head]
    return array[:, start:stop]


def probs_t(query, keys, head, keep):
    scores = dot_nt(head_part(keys, head), head_window(query, head)) * HEAD_DIM ** (-0.5)
    if keep is not None:
        scores = jnp.where(keep, scores, -1e30)
    peak = jnp.max(scores, axis=0, keepdims=True)
    weights = jnp.exp(scores - peak)
    return weights / jnp.sum(weights, axis=0, keepdims=True)


def same_patch(count, patches):
    row = lax.broadcasted_iota(jnp.int32, (count, count), 0)
    col = lax.broadcasted_iota(jnp.int32, (count, count), 1)
    return lax.rem(row, patches) == lax.rem(col, patches)


def space_forward(x_ref, cot_ref, w_qkv_ref, w_out_ref, w_time_ref, send_ref, qkv_ref, attn_ref, normed_ref):
    x = x_ref[...].astype(F32)
    normed = norm_parts(x)[0].astype(BF16)
    normed_ref[...] = normed
    qkv = dot_nt(normed, w_qkv_ref[...]).astype(BF16)
    qkv_ref[...] = qkv
    query, keys, values = split_qkv(qkv)
    mix = HeadSum()
    for head in range(HEADS):
        weights = probs_t(query, keys, head, None).astype(BF16)
        mix.put(head, dot_tn(weights, head_window(values, head)))
    attn = mix.whole(BF16)
    attn_ref[...] = attn
    width = x.shape[1]
    send_ref[:, :width] = (x + dot_nn(attn, w_out_ref[...])).astype(BF16)
    send_ref[:, width:] = dot_nt(cot_ref[...], w_time_ref[...]).astype(BF16)


def attention_back(query, keys, values, dmix, keep, forward):
    mix, dq, dk, dv = HeadSum(), HeadSum(), HeadSum(), HeadSum()
    for head in range(HEADS):
        weights = probs_t(query, keys, head, keep)
        rounded = weights.astype(BF16)
        if forward:
            mix.put(head, dot_tn(rounded, head_window(values, head)))
        dprobs = dot_nt(head_part(values, head), head_window(dmix, head)).astype(BF16).astype(F32)
        total = jnp.sum(weights * dprobs, axis=0, keepdims=True)
        dscores = (weights * (dprobs - total) * HEAD_DIM ** (-0.5)).astype(BF16)
        dv.put(head, dot_nn(rounded, head_window(dmix, head)))
        dk.put(head, dot_nn(dscores, head_window(query, head)))
        dq.put(head, dot_tn(dscores, head_window(keys, head)))
    dqkv = jnp.concatenate([dq.whole(BF16), dk.whole(BF16), dv.whole(BF16)], axis=1)
    return (mix.whole(BF16) if forward else None), dqkv


def time_both(patches, recv_ref, w_qkv_ref, back_ref, normed_ref, dqkv_ref):
    width = w_qkv_ref.shape[1]
    hidden = recv_ref[:, :width].astype(F32)
    normed, rate = norm_parts(hidden)
    rounded = normed.astype(BF16)
    normed_ref[...] = rounded
    qkv = dot_nt(rounded, w_qkv_ref[...]).astype(BF16)
    query, keys, values = split_qkv(qkv)
    keep = same_patch(hidden.shape[0], patches)
    attn, dqkv = attention_back(query, keys, values, recv_ref[:, width:], keep, True)
    dqkv_ref[...] = dqkv
    back_ref[:, width:] = attn
    dnormed = dot_nn(dqkv, w_qkv_ref[...]).astype(BF16).astype(F32)
    back_ref[:, :width] = norm_back(dnormed, normed, rate).astype(BF16)


def space_backward(
    core_ref, cot_ref, recv_ref, qkv_ref, attn_ref, w_out_ref, dhidden_ref, dqkv_ref, keep_ref, send_ref
):
    width = cot_ref.shape[1]
    dhidden = cot_ref[...] + recv_ref[:, :width]
    dhidden_ref[...] = dhidden
    dattn = dot_nt(dhidden, w_out_ref[...]).astype(BF16)
    query, keys, values = split_qkv(qkv_ref[...])
    dqkv = attention_back(query, keys, values, dattn, None, False)[1]
    dqkv_ref[...] = dqkv
    pair_up(core_ref[0], dqkv, attn_ref[...], keep_ref, send_ref)


def space_finish(x_ref, dhidden_ref, dqkv_ref, w_qkv_ref, grad_ref):
    normed, rate = norm_parts(x_ref[...].astype(F32))
    dnormed = dot_nn(dqkv_ref[...], w_qkv_ref[...]).astype(BF16).astype(F32)
    dres = norm_back(dnormed, normed, rate).astype(BF16)
    grad_ref[...] = dhidden_ref[...] + dres


def call(kernel, outs, *args, flops=0):
    size = sum(a.size * a.dtype.itemsize for a in args) + sum(math.prod(shape) * 2 for shape, _ in outs)
    shapes = [jax.ShapeDtypeStruct(shape, dtype) for shape, dtype in outs]
    return pl.pallas_call(
        kernel,
        out_shape=shapes,
        in_specs=[
            pl.BlockSpec(memory_space=pltpu.SMEM if a.dtype == jnp.int32 else pltpu.VMEM) for a in args
        ],
        out_specs=[pl.BlockSpec(memory_space=pltpu.VMEM)] * len(outs),
        compiler_params=pltpu.CompilerParams(vmem_limit_bytes=8 * 1024 * 1024),
        cost_estimate=pl.CostEstimate(flops=flops, bytes_accessed=size, transcendentals=0),
    )(*args)


def permutation(width, chips):
    rows = width // chips
    table = np.zeros((3, chips, 8, width), np.float32)
    for chip in range(chips):
        for lane in range(8):
            table[0, chip, lane, chip * rows + lane] = 1
            table[1, chip, lane, chip * rows + 8 + lane] = 1
        for lane in range(6):
            table[2, chip, lane, chip * rows + 16 + lane % 2] = 1
    return table.reshape(3 * chips * 8, width).astype(jnp.bfloat16)


def transpose_rows(perm_ref, tokens_ref, out_ref):
    out_ref[...] = dot_nt(perm_ref[...], tokens_ref[...]).astype(BF16)


def mix_out(send_ref, recv_ref, w_out_ref, mixed_ref):
    width = w_out_ref.shape[1]
    mixed = send_ref[:, :width].astype(F32) + dot_nn(recv_ref[:, width:], w_out_ref[...])
    mixed_ref[...] = mixed.astype(BF16)


def pair_up(core, dqkv, attn, keep_ref, send_ref):
    second = jnp.concatenate([dqkv[:, 2 * HK :], attn], axis=1)
    first = dqkv[:, : 2 * HK]
    keep_ref[...] = jnp.where(core == 0, first, second)
    send_ref[...] = jnp.where(core == 0, second, first)


def time_pair(core_ref, dqkv_ref, recv_ref, keep_ref, send_ref):
    pair_up(core_ref[0], dqkv_ref[...], recv_ref[:, recv_ref.shape[1] - HK :], keep_ref, send_ref)


def weight_terms(core_ref, in_own, in_got, out_own, out_got, own_ref, got_ref, chunk_ref):
    block = in_own.shape[0] // 3
    low, high = HK // LANES * LANES, -(-HK // LANES) * LANES
    width = own_ref.shape[1]
    third = width // 3

    def fill(second_own, second_got):
        for part in range(3):
            rows = pl.ds(part * block, block)
            left = dot_nn(in_own[rows, :], own_ref[:, :high]) + dot_nn(in_got[rows, :], got_ref[:, :high])
            right = dot_nn(second_own[rows, :], own_ref[:, low:]) + dot_nn(
                second_got[rows, :], got_ref[:, low:]
            )
            lane = low + lax.broadcasted_iota(jnp.int32, (block, high - low), 1)
            middle = jnp.where(lane < HK, left[:, low:], right[:, : high - low])
            whole = jnp.concatenate([left[:, :low], middle, right[:, high - low :]], axis=1)
            if part < 2:
                chunk_ref[:, part * width : (part + 1) * width] = whole.astype(BF16)
            else:
                row = lax.rem(lax.broadcasted_iota(jnp.int32, (block, third), 0), 8)
                rest = jnp.where(
                    row < 2,
                    whole[:, :third],
                    jnp.where(row < 4, whole[:, third : 2 * third], whole[:, 2 * third :]),
                )
                chunk_ref[:, 2 * width :] = rest.astype(BF16)

    @pl.when(core_ref[0] == 0)
    def _():
        fill(in_own, in_got)

    @pl.when(core_ref[0] != 0)
    def _():
        fill(out_own, out_got)


def add_chunks(scale, core_ref, chunk_ref, keep_ref, send_ref):
    count, lanes = chunk_ref.shape
    total = chunk_ref[:16, :].astype(F32)
    for start in range(16, count, 16):
        total = total + chunk_ref[start : start + 16, :].astype(F32)
    total = (total[:8] + total[8:]) * scale
    width = keep_ref.shape[1]
    third = width // 3
    first, second, rest = total[:, :width], total[:, width : 2 * width], total[:, 2 * width :]
    last = jnp.concatenate([rest[0:2], rest[2:4], rest[4:6]], axis=1)
    low = jnp.concatenate([first, second[:1]], axis=0)
    high = jnp.concatenate([second[1:], last], axis=0)
    core = core_ref[0]
    keep_ref[...] = jnp.where(core == 0, low, high)
    send_ref[...] = jnp.where(core == 0, high, low)


def place_rows(core_ref, keep_ref, got_ref, qkv_ref, out_ref):
    core = core_ref[0]
    keep, got = keep_ref[...], got_ref[...]
    first = jnp.where(core == 0, keep, got)
    second = jnp.where(core == 0, got, keep)
    qkv_ref[:, : 2 * HK] = first
    qkv_ref[:, 2 * HK :] = second[:, :HK]
    out_ref[...] = second[:, HK:]


SEQ = ("z", "y", "xl")
CHIPS = ("z", "y", "xl", "xh")


def on_device(clips, cotangent, w_qkv_space, w_out_space, w_qkv_time, w_out_time):
    patches, width = clips.shape[2], clips.shape[3]
    frames = lax.axis_size(SEQ)
    chips = lax.axis_size(CHIPS)
    own_patches = patches // frames
    count = patches
    qkv_cols = w_qkv_space.shape[1]
    w_qkv_space, w_out_space = w_qkv_space.T, w_out_space.T
    w_qkv_time, w_out_time = w_qkv_time.T, w_out_time.T
    scale = 1.0 / math.sqrt(count * frames * lax.axis_size(("xh", "c")))
    core = lax.axis_index("c").astype(jnp.int32).reshape(1)
    x = clips.reshape(count, width)
    top = cotangent.reshape(count, width)
    perm = jnp.asarray(permutation(width, chips))
    pairs = [(0, 1), (1, 0)]

    def swap(array):
        return lax.ppermute(array, "c", pairs)

    def exchange(array, axes, parts):
        lanes = array.shape[1]
        array = lax.all_to_all(
            array.reshape(parts, -1, lanes), axes, split_axis=0, concat_axis=0, tiled=True
        )
        return array.reshape(-1, lanes)

    def rows_of(tokens):
        out = call(transpose_rows, [((perm.shape[0], count), BF16)], perm, tokens, flops=10**9)[0]
        return out, swap(out)

    send, qkv_space, attn_space, normed_space = call(
        space_forward,
        [((count, width + HK), BF16), ((count, qkv_cols), BF16), ((count, HK), BF16), ((count, width), BF16)],
        x, top, w_qkv_space, w_out_space, w_out_time, flops=3 * 10**9,
    )
    recv = exchange(send, SEQ, frames)
    back, normed_time, dqkv_time = call(
        functools.partial(time_both, own_patches),
        [((count, width + HK), BF16), ((count, width), BF16), ((count, qkv_cols), BF16)],
        recv, w_qkv_time, flops=5 * 10**9,
    )
    recv = exchange(back, SEQ, frames)
    rows_norm_space = rows_of(normed_space)
    rows_top = rows_of(top)
    rows_norm_time = rows_of(normed_time)
    half = ((count, width), BF16)
    keep, give = call(time_pair, [half, half], core, dqkv_time, recv)
    chunk_shape = ((8 * chips, 2 * width + width // 3), BF16)
    terms_time = call(
        weight_terms, [chunk_shape], core, *rows_norm_time, *rows_top, keep, swap(give),
        flops=2 * 10**9,
    )[0]
    got_time = exchange(terms_time, CHIPS, chips)
    dhidden, dqkv_space, keep, give = call(
        space_backward, [half, ((count, qkv_cols), BF16), half, half],
        core, top, recv, qkv_space, attn_space, w_out_space, flops=3 * 10**9,
    )
    rows_dhidden = rows_of(dhidden)
    terms_space = call(
        weight_terms, [chunk_shape], core, *rows_norm_space, *rows_dhidden, keep, swap(give), flops=2 * 10**9
    )[0]
    got_space = exchange(terms_space, CHIPS, chips)
    grad_clips = call(
        space_finish, [half], x, dhidden, dqkv_space, w_qkv_space, flops=10**9
    )[0]
    mixed = call(mix_out, [half], send, recv, w_out_time, flops=10**9)[0]

    def finish(got):
        rows = width // chips // 2
        own, other = call(
            functools.partial(add_chunks, scale), [((rows, width), F32), ((rows, width), F32)], core, got
        )
        return call(
            place_rows, [((rows, qkv_cols), F32), ((rows, HK), F32)], core, own, swap(other)
        )

    grad_qkv_time, grad_out_time = finish(got_time)
    grad_qkv_space, grad_out_space = finish(got_space)
    return (
        mixed.reshape(clips.shape),
        grad_clips.reshape(clips.shape),
        grad_qkv_space,
        grad_out_space,
        grad_qkv_time,
        grad_out_time,
    )


def solution(mesh):
    fine = Mesh(mesh.devices.reshape(4, 4, 2, 2, 2), ("z", "y", "xl", "xh", "c"))
    tokens = P(("xh", "c"), SEQ, None, None)
    rows = P(("z", "y", "xl", "xh", "c"), None)
    return jax.shard_map(
        on_device,
        mesh=fine,
        in_specs=(tokens, tokens, P(), P(), P(), P()),
        out_specs=(tokens, tokens, rows, rows, rows, rows),
        check_vma=False,
    )
```

profile of v0, /device:TPU:1, one launch (start us, length us, event | category | flops | bytes accessed | tf_op | source)
XLA Modules:
  0.0 173.1 jit_solution(14509879165574476339)
XLA Ops:
  0.6 2.1 %copy-done.1 = bf16[1152,1728]{0,1:T(8,128)(2,1)S(1)} copy-done((bf16[1152,1728]{0,1:T(8,128)(2,1)S(1)}, bf16[1152,1728]{0,1:T(8,128)(2,1)}, u32[]{:S(2)}) %copy-start.1) | copy-done | bytes 3981336
  2.8 1.3 copy-done.9
  6.2 1.3 copy-done.26
  7.5 4.1 %shard_map.118 = (bf16[256,1728]{1,0:T(8,128)(2,1)S(1)}, bf16[256,1728]{1,0:T(8,128)(2,1)S(1)}, bf16[256,576]{1,0:T(8,128)(2,1)S(1)}, bf16[256,1152]{1,0:T(8,128)(2,1)S(1)}) custom-call(bf16[256,1152]{1,0:T(8,128)(2,1)S(1)} %bitcast.30, bf16[256,1152]{1,0:T(8,128)(2,1)S(1)} %bitcast.27, bf16[1728,1152]{1,0:T(8,128)(2,1)S(1)} %bitcast.18, ...), custom_call_target="tpu_custom_call" | custom-call | flops 3000000000 | bytes 10469376 | tf_op jit(solution)/shard_map/pallas_call | solution.py:181
  12.7 24.9 %all_to_all.20 = bf16[32,8,1728]{2,1,0:T(8,128)(2,1)S(1)} all-to-all(bf16[32,8,1728]{2,1,0:T(8,128)(2,1)S(1)} %bitcast.20), channel_id=1, replica_groups=mesh['z'=4,'y'=4,'xl'=2,'xh'=2,'c'=2] {'z','y','xl'}, dimensions={0} | all-to-all | bytes 1769472 | tf_op jit(solution)/shard_map/all_to_all | solution.py:314
  37.6 6.6 %shard_map.119 = (bf16[256,1728]{1,0:T(8,128)(2,1)S(1)}, bf16[256,1152]{1,0:T(8,128)(2,1)S(1)}, bf16[256,1728]{1,0:T(8,128)(2,1)S(1)}) custom-call(bf16[256,1728]{1,0:T(8,128)(2,1)S(1)} %bitcast.26, bf16[1728,1152]{1,0:T(8,128)(2,1)S(1)} %bitcast.32), custom_call_target="tpu_custom_call" | custom-call | flops 5000000000 | bytes 7225344 | tf_op jit(solution)/shard_map/pallas_call | solution.py:181
  47.0 4.6 %all-to-all-start.1 = ((bf16[32,8,1728]{2,1,0:T(8,128)(2,1)}), bf16[32,8,1728]{2,1,0:T(8,128)(2,1)}, u32[]{:S(2)}, u32[]{:S(2)}) async-start(bf16[32,8,1728]{2,1,0:T(8,128)(2,1)} %bitcast.25), calls=%async_computation.1 | async-start | bytes 1835008 | tf_op jit(solution)/shard_map/all_to_all | solution.py:314
  52.7 2.1 %shard_map.129.out_own = bf16[1536,256]{1,0:T(8,128)(2,1)} custom-call(bf16[1536,1152]{1,0:T(8,128)(2,1)S(1)} %copy-done, bf16[256,1152]{1,0:T(8,128)(2,1)S(1)} %bitcast.28), custom_call_target="tpu_custom_call" | custom-call | flops 1000000000 | bytes 4915200 | tf_op jit(solution)/shard_map/pallas_call | solution.py:181
  54.8 2.1 %collective-permute-start.5 = (bf16[1536,256]{1,0:T(8,128)(2,1)}, bf16[1536,256]{1,0:T(8,128)(2,1)}, u32[]{:S(2)}, u32[]{:S(2)}) collective-permute-start(bf16[1536,256]{1,0:T(8,128)(2,1)} %shard_map.129.out_own), channel_id=1, source_target_pairs={{0,1},{1,0},{2,3},{3,2},{4,5},{5,4},{6,7},{7,6},{8,9},{9,8},{10,11... | collective-permute-start | bytes 2359304 | tf_op jit(solution)/shard_map/ppermute | solution.py:310
  56.9 2.1 %shard_map.128.in_own = bf16[1536,256]{1,0:T(8,128)(2,1)} custom-call(bf16[1536,1152]{1,0:T(8,128)(2,1)S(1)} %copy-done, bf16[256,1152]{1,0:T(8,128)(2,1)S(1)} %copy-done.24), custom_call_target="tpu_custom_call" | custom-call | flops 1000000000 | bytes 4915200 | tf_op jit(solution)/shard_map/pallas_call | solution.py:181
  59.0 6.8 %all-to-all-done.1 = bf16[32,8,1728]{2,1,0:T(8,128)(2,1)} async-done(((bf16[32,8,1728]{2,1,0:T(8,128)(2,1)}), bf16[32,8,1728]{2,1,0:T(8,128)(2,1)}, u32[]{:S(2)}, u32[]{:S(2)}) %all-to-all-start.1) | async-done | bytes 884768 | tf_op jit(solution)/shard_map/all_to_all | solution.py:314
  67.1 1.3 shard_map.130
  68.4 3.2 %collective-permute-start.6 = (bf16[256,1152]{1,0:T(8,128)(2,1)S(1)}, bf16[256,1152]{1,0:T(8,128)(2,1)S(1)}, u32[]{:S(2)}, u32[]{:S(2)}) collective-permute-start(bf16[256,1152]{1,0:T(8,128)(2,1)S(1)} %get-tuple-element.43), channel_id=1, source_target_pairs={{0,1},{1,0},{2,3},{3,2},{4,5},{5,4},{6,7},{7,6},{8,9},{9,8},{10,11... | collective-permute-start | bytes 1769480 | tf_op jit(solution)/shard_map/ppermute | solution.py:310
  71.7 1.6 collective-permute-done.6.got_ref
  73.3 4.5 %shard_map.131 = bf16[512,2688]{1,0:T(8,128)(2,1)S(1)} custom-call(s32[1]{0:T(128)} %bitcast.11.core_ref, bf16[1536,256]{1,0:T(8,128)(2,1)} %shard_map.128.in_own, bf16[1536,256]{1,0:T(8,128)(2,1)} %collective-permute-done.4.in_got, bf16[1536,256]{1,0:T(8,128)(2,1)} %shard_map.129.out_own, bf16[1536,256]{1,0:T(8,128)(2,1)} %collective-permute-done.5.out_got, ...), custom_call_target="tpu_custom_call" | custom-call | flops 2000000000 | bytes 7077892 | tf_op jit(solution)/shard_map/pallas_call | solution.py:181
  77.8 1.5 copy-done.5
  79.3 6.1 %all-to-all-start.3 = ((bf16[64,8,2688]{2,1,0:T(8,128)(2,1)}), bf16[64,8,2688]{2,1,0:T(8,128)(2,1)}, u32[]{:S(2)}, u32[]{:S(2)}) async-start(bf16[64,8,2688]{2,1,0:T(8,128)(2,1)} %bitcast.21), calls=%async_computation.3 | async-start | bytes 5505024 | tf_op jit(solution)/shard_map/all_to_all | solution.py:314
  88.8 5.1 %shard_map.121 = (bf16[256,1152]{1,0:T(8,128)(2,1)S(1)}, bf16[256,1728]{1,0:T(8,128)(2,1)S(1)}, bf16[256,1152]{1,0:T(8,128)(2,1)S(1)}, bf16[256,1152]{1,0:T(8,128)(2,1)S(1)}) custom-call(s32[1]{0:T(128)} %bitcast.11.core_ref, bf16[256,1152]{1,0:T(8,128)(2,1)S(1)} %bitcast.29, bf16[256,1728]{1,0:T(8,128)(2,1)} %bitcast.9.recv_ref, ...), custom_call_target="tpu_custom_call" | custom-call | flops 3000000000 | bytes 6635524 | tf_op jit(solution)/shard_map/pallas_call | solution.py:181
  93.9 1.2 shard_map.124.out_own
  95.8 2.6 %collective-permute-done.2.got_ref = bf16[256,1152]{1,0:T(8,128)(2,1)S(1)} collective-permute-done((bf16[256,1152]{1,0:T(8,128)(2,1)S(1)}, bf16[256,1152]{1,0:T(8,128)(2,1)S(1)}, u32[]{:S(2)}, u32[]{:S(2)}) %collective-permute-start.2) | collective-permute-done | bytes 589856 | tf_op jit(solution)/shard_map/ppermute | solution.py:310
  98.4 2.7 %shard_map.125 = bf16[512,2688]{1,0:T(8,128)(2,1)S(1)} custom-call(s32[1]{0:T(128)} %bitcast.11.core_ref, bf16[1536,256]{1,0:T(8,128)(2,1)S(1)} %shard_map.123.in_own, bf16[1536,256]{1,0:T(8,128)(2,1)S(1)} %collective-permute-done.in_got, bf16[1536,256]{1,0:T(8,128)(2,1)S(1)} %shard_map.124.out_own, bf16[1536,256]{1,0:T(8,128)(2,1)S(1)} %collective-permute-done.1.out_got, ...), custom_call_target="tpu_custom_call" | custom-call | flops 2000000000 | bytes 7077892 | tf_op jit(solution)/shard_map/pallas_call | solution.py:181
  101.1 1.6 copy-done.6
  102.6 19.3 %all-to-all-done.3 = bf16[64,8,2688]{2,1,0:T(8,128)(2,1)} async-done(((bf16[64,8,2688]{2,1,0:T(8,128)(2,1)}), bf16[64,8,2688]{2,1,0:T(8,128)(2,1)}, u32[]{:S(2)}, u32[]{:S(2)}) %all-to-all-start.3) | async-done | bytes 2752544 | tf_op jit(solution)/shard_map/all_to_all | solution.py:314
  121.9 6.4 %all-to-all-start.2 = ((bf16[64,8,2688]{2,1,0:T(8,128)(2,1)}), bf16[64,8,2688]{2,1,0:T(8,128)(2,1)S(1)}, u32[]{:S(2)}, u32[]{:S(2)}) async-start(bf16[64,8,2688]{2,1,0:T(8,128)(2,1)} %bitcast.22), calls=%async_computation.2 | async-start | bytes 5505024 | tf_op jit(solution)/shard_map/all_to_all | solution.py:314
  129.6 1.3 copy-done.10
  130.9 2.6 %shard_map.120 = bf16[256,1152]{1,0:T(8,128)(2,1)} custom-call(bf16[256,1728]{1,0:T(8,128)(2,1)S(1)} %copy-done.4, bf16[256,1728]{1,0:T(8,128)(2,1)} %bitcast.9.recv_ref, bf16[576,1152]{1,0:T(8,128)(2,1)S(1)} %bitcast.24), custom_call_target="tpu_custom_call" | custom-call | flops 1000000000 | bytes 3686400 | tf_op jit(solution)/shard_map/pallas_call | solution.py:181
  133.5 2.8 %shard_map.132 = (f32[9,1152]{1,0:T(8,128)S(1)}, f32[9,1152]{1,0:T(8,128)}) custom-call(s32[1]{0:T(128)} %bitcast.11.core_ref, bf16[512,2688]{1,0:T(8,128)(2,1)} %bitcast.16.chunk_ref), custom_call_target="tpu_custom_call" | custom-call | bytes 2793988 | tf_op jit(solution)/shard_map/pallas_call | solution.py:181
  136.4 1.3 collective-permute-start.7
  137.6 27.2 %all-to-all-done.2 = bf16[64,8,2688]{2,1,0:T(8,128)(2,1)S(1)} async-done(((bf16[64,8,2688]{2,1,0:T(8,128)(2,1)}), bf16[64,8,2688]{2,1,0:T(8,128)(2,1)S(1)}, u32[]{:S(2)}, u32[]{:S(2)}) %all-to-all-start.2) | async-done | bytes 2752544 | tf_op jit(solution)/shard_map/all_to_all | solution.py:314
  165.2 1.8 %collective-permute-start.3 = (f32[9,1152]{1,0:T(8,128)S(1)}, f32[9,1152]{1,0:T(8,128)S(1)}, u32[]{:S(2)}, u32[]{:S(2)}) collective-permute-start(f32[9,1152]{1,0:T(8,128)S(1)} %get-tuple-element.37), channel_id=1, source_target_pairs={{0,1},{1,0},{2,3},{3,2},{4,5},{5,4},{6,7},{7,6},{8,9},{9,8},{10,11... | collective-permute-start | bytes 124424 | tf_op jit(solution)/shard_map/ppermute | solution.py:310
  167.0 2.1 %copy-done.2 = bf16[1152,1728]{0,1:T(8,128)(2,1)S(1)} copy-done((bf16[1152,1728]{0,1:T(8,128)(2,1)S(1)}, bf16[1152,1728]{0,1:T(8,128)(2,1)}, u32[]{:S(2)}) %copy-start.2) | copy-done | bytes 3981336
  169.2 2.5 %shard_map.122 = bf16[256,1152]{1,0:T(8,128)(2,1)} custom-call(bf16[256,1152]{1,0:T(8,128)(2,1)S(1)} %bitcast.31, bf16[256,1152]{1,0:T(8,128)(2,1)S(1)} %copy-done.8, bf16[256,1728]{1,0:T(8,128)(2,1)S(1)} %copy-done.12, bf16[1728,1152]{1,0:T(8,128)(2,1)S(1)} %bitcast.19), custom_call_target="tpu_custom_call" | custom-call | flops 1000000000 | bytes 6635520 | tf_op jit(solution)/shard_map/pallas_call | solution.py:181
  (71 shorter events, 15.0 us)
Async XLA Ops:
  0.6 2.1 %copy-start.1 = (bf16[1152,1728]{0,1:T(8,128)(2,1)S(1)}, bf16[1152,1728]{0,1:T(8,128)(2,1)}, u32[]{:S(2)}) copy-start(bf16[1152,1728]{0,1:T(8,128)(2,1)} %param.9) | copy-start | bytes 11943940
  2.8 1.3 copy-start.9
  6.2 1.3 copy-start.26
  7.5 30.0 %copy-start.25 = (bf16[1152,1728]{0,1:T(8,128)(2,1)S(1)}, bf16[1152,1728]{0,1:T(8,128)(2,1)}, u32[]{:S(2)}) copy-start(bf16[1152,1728]{0,1:T(8,128)(2,1)} %param.11) | copy-start | bytes 11943940
  12.6 31.6 %copy-start.3 = (bf16[256,1728]{1,0:T(8,128)(2,1)}, bf16[256,1728]{1,0:T(8,128)(2,1)S(1)}, u32[]{:S(2)}) copy-start(bf16[256,1728]{1,0:T(8,128)(2,1)S(1)} %get-tuple-element.27.send_ref) | copy-start | bytes 2654212
  12.6 31.6 %copy-start.21 = (bf16[256,1152]{1,0:T(8,128)(2,1)}, bf16[256,1152]{1,0:T(8,128)(2,1)S(1)}, u32[]{:S(2)}) copy-start(bf16[256,1152]{1,0:T(8,128)(2,1)S(1)} %get-tuple-element.33.tokens_ref) | copy-start | bytes 1769476
  12.7 31.6 %copy-start.30 = (bf16[256,576]{1,0:T(8,128)(2,1)}, bf16[256,576]{1,0:T(8,128)(2,1)S(1)}, u32[]{:S(2)}) copy-start(bf16[256,576]{1,0:T(8,128)(2,1)S(1)} %get-tuple-element.30.attn_ref) | copy-start | bytes 884740
  37.6 14.0 %copy-start = (bf16[1536,1152]{1,0:T(8,128)(2,1)S(1)}, bf16[1536,1152]{1,0:T(8,128)(2,1)}, u32[]{:S(2)}) copy-start(bf16[1536,1152]{1,0:T(8,128)(2,1)} %constant.6.clone.perm_ref) | copy-start | bytes 10616836
  47.0 18.9 %all-to-all-start.1 = ((bf16[32,8,1728]{2,1,0:T(8,128)(2,1)}), bf16[32,8,1728]{2,1,0:T(8,128)(2,1)}, u32[]{:S(2)}, u32[]{:S(2)}) async-start(bf16[32,8,1728]{2,1,0:T(8,128)(2,1)} %bitcast.25), calls=%async_computation.1 | async-start | bytes 1835008 | tf_op jit(solution)/shard_map/all_to_all | solution.py:314
  52.7 4.2 %copy-start.24 = (bf16[256,1152]{1,0:T(8,128)(2,1)S(1)}, bf16[256,1152]{1,0:T(8,128)(2,1)}, u32[]{:S(2)}) copy-start(bf16[256,1152]{1,0:T(8,128)(2,1)} %copy-done.23) | copy-start | bytes 1769476
  54.8 16.9 %collective-permute-start.5 = (bf16[1536,256]{1,0:T(8,128)(2,1)}, bf16[1536,256]{1,0:T(8,128)(2,1)}, u32[]{:S(2)}, u32[]{:S(2)}) collective-permute-start(bf16[1536,256]{1,0:T(8,128)(2,1)} %shard_map.129.out_own), channel_id=1, source_target_pairs={{0,1},{1,0},{2,3},{3,2},{4,5},{5,4},{6,7},{7,6},{8,9},{9,8},{10,11... | collective-permute-start | bytes 2359304 | tf_op jit(solution)/shard_map/ppermute | solution.py:310
  59.0 12.6 %collective-permute-start.4 = (bf16[1536,256]{1,0:T(8,128)(2,1)}, bf16[1536,256]{1,0:T(8,128)(2,1)}, u32[]{:S(2)}, u32[]{:S(2)}) collective-permute-start(bf16[1536,256]{1,0:T(8,128)(2,1)} %shard_map.128.in_own), channel_id=1, source_target_pairs={{0,1},{1,0},{2,3},{3,2},{4,5},{5,4},{6,7},{7,6},{8,9},{9,8},{10,11... | collective-permute-start | bytes 2359304 | tf_op jit(solution)/shard_map/ppermute | solution.py:310
  68.4 4.9 %collective-permute-start.6 = (bf16[256,1152]{1,0:T(8,128)(2,1)S(1)}, bf16[256,1152]{1,0:T(8,128)(2,1)S(1)}, u32[]{:S(2)}, u32[]{:S(2)}) collective-permute-start(bf16[256,1152]{1,0:T(8,128)(2,1)S(1)} %get-tuple-element.43), channel_id=1, source_target_pairs={{0,1},{1,0},{2,3},{3,2},{4,5},{5,4},{6,7},{7,6},{8,9},{9,8},{10,11... | collective-permute-start | bytes 1769480 | tf_op jit(solution)/shard_map/ppermute | solution.py:310
  77.8 1.5 copy-start.5
  79.3 42.6 %all-to-all-start.3 = ((bf16[64,8,2688]{2,1,0:T(8,128)(2,1)}), bf16[64,8,2688]{2,1,0:T(8,128)(2,1)}, u32[]{:S(2)}, u32[]{:S(2)}) async-start(bf16[64,8,2688]{2,1,0:T(8,128)(2,1)} %bitcast.21), calls=%async_computation.3 | async-start | bytes 5505024 | tf_op jit(solution)/shard_map/all_to_all | solution.py:314
  85.4 3.3 %copy-start.18 = (bf16[1,1,256,1152]{3,2,1,0:T(8,128)(2,1)S(1)}, bf16[1,1,256,1152]{3,2,1,0:T(8,128)(2,1)}, u32[]{:S(2)}) copy-start(bf16[1,1,256,1152]{3,2,1,0:T(8,128)(2,1)} %param.8) | copy-start | bytes 1769476
  86.6 2.2 %copy-start.27 = (bf16[1152,576]{0,1:T(8,128)(2,1)S(1)}, bf16[1152,576]{0,1:T(8,128)(2,1)}, u32[]{:S(2)}) copy-start(bf16[1152,576]{0,1:T(8,128)(2,1)} %param.10) | copy-start | bytes 3981316
  86.6 2.2 %copy-start.29 = (bf16[256,1728]{1,0:T(8,128)(2,1)S(1)}, bf16[256,1728]{1,0:T(8,128)(2,1)}, u32[]{:S(2)}) copy-start(bf16[256,1728]{1,0:T(8,128)(2,1)} %copy-done.28) | copy-start | bytes 2654212
  86.6 2.2 %copy-start.31 = (bf16[256,576]{1,0:T(8,128)(2,1)S(1)}, bf16[256,576]{1,0:T(8,128)(2,1)}, u32[]{:S(2)}) copy-start(bf16[256,576]{1,0:T(8,128)(2,1)} %copy-done.30) | copy-start | bytes 884740
  87.8 7.9 %collective-permute-start = (bf16[1536,256]{1,0:T(8,128)(2,1)S(1)}, bf16[1536,256]{1,0:T(8,128)(2,1)S(1)}, u32[]{:S(2)}, u32[]{:S(2)}) collective-permute-start(bf16[1536,256]{1,0:T(8,128)(2,1)S(1)} %shard_map.123.in_own), channel_id=1, source_target_pairs={{0,1},{1,0},{2,3},{3,2},{4,5},{5,4},{6,7},{7,6},{8,9},{9,8},{10,11... | collective-permute-start | bytes 2359304 | tf_op jit(solution)/shard_map/ppermute | solution.py:310
  93.9 4.5 %copy-start.7 = (bf16[256,1152]{1,0:T(8,128)(2,1)}, bf16[256,1152]{1,0:T(8,128)(2,1)S(1)}, u32[]{:S(2)}) copy-start(bf16[256,1152]{1,0:T(8,128)(2,1)S(1)} %get-tuple-element.31.dhidden_ref.tokens_ref) | copy-start | bytes 1769476
  93.9 4.5 %copy-start.11 = (bf16[256,1728]{1,0:T(8,128)(2,1)}, bf16[256,1728]{1,0:T(8,128)(2,1)S(1)}, u32[]{:S(2)}) copy-start(bf16[256,1728]{1,0:T(8,128)(2,1)S(1)} %get-tuple-element.32.dqkv_ref) | copy-start | bytes 2654212
  95.2 3.2 %collective-permute-start.1 = (bf16[1536,256]{1,0:T(8,128)(2,1)S(1)}, bf16[1536,256]{1,0:T(8,128)(2,1)S(1)}, u32[]{:S(2)}, u32[]{:S(2)}) collective-permute-start(bf16[1536,256]{1,0:T(8,128)(2,1)S(1)} %shard_map.124.out_own), channel_id=1, source_target_pairs={{0,1},{1,0},{2,3},{3,2},{4,5},{5,4},{6,7},{7,6},{8,9},{9,8},{10,11... | collective-permute-start | bytes 2359304 | tf_op jit(solution)/shard_map/ppermute | solution.py:310
  95.4 3.0 %collective-permute-start.2 = (bf16[256,1152]{1,0:T(8,128)(2,1)S(1)}, bf16[256,1152]{1,0:T(8,128)(2,1)S(1)}, u32[]{:S(2)}, u32[]{:S(2)}) collective-permute-start(bf16[256,1152]{1,0:T(8,128)(2,1)S(1)} %get-tuple-element.35), channel_id=1, source_target_pairs={{0,1},{1,0},{2,3},{3,2},{4,5},{5,4},{6,7},{7,6},{8,9},{9,8},{10,11... | collective-permute-start | bytes 1769480 | tf_op jit(solution)/shard_map/ppermute | solution.py:310
  101.0 1.6 copy-start.6
  121.9 42.9 %all-to-all-start.2 = ((bf16[64,8,2688]{2,1,0:T(8,128)(2,1)}), bf16[64,8,2688]{2,1,0:T(8,128)(2,1)S(1)}, u32[]{:S(2)}, u32[]{:S(2)}) async-start(bf16[64,8,2688]{2,1,0:T(8,128)(2,1)} %bitcast.22), calls=%async_computation.2 | async-start | bytes 5505024 | tf_op jit(solution)/shard_map/all_to_all | solution.py:314
  133.5 33.5 %copy-start.8 = (bf16[256,1152]{1,0:T(8,128)(2,1)S(1)}, bf16[256,1152]{1,0:T(8,128)(2,1)}, u32[]{:S(2)}) copy-start(bf16[256,1152]{1,0:T(8,128)(2,1)} %copy-done.7) | copy-start | bytes 1769476
  136.4 35.3 %collective-permute-start.7 = (f32[9,1152]{1,0:T(8,128)}, f32[9,1152]{1,0:T(8,128)S(1)}, u32[]{:S(2)}, u32[]{:S(2)}) collective-permute-start(f32[9,1152]{1,0:T(8,128)} %get-tuple-element.45), channel_id=1, source_target_pairs={{0,1},{1,0},{2,3},{3,2},{4,5},{5,4},{6,7},{7,6},{8,9},{9,8},{10,11... | collective-permute-start | bytes 124424 | tf_op jit(solution)/shard_map/ppermute | solution.py:310
  164.9 2.2 %copy-start.12 = (bf16[256,1728]{1,0:T(8,128)(2,1)S(1)}, bf16[256,1728]{1,0:T(8,128)(2,1)}, u32[]{:S(2)}) copy-start(bf16[256,1728]{1,0:T(8,128)(2,1)} %copy-done.11) | copy-start | bytes 2654212
  164.9 2.2 %copy-start.20 = (bf16[1,1,256,1152]{3,2,1,0:T(8,128)(2,1)S(1)}, bf16[1,1,256,1152]{3,2,1,0:T(8,128)(2,1)}, u32[]{:S(2)}) copy-start(bf16[1,1,256,1152]{3,2,1,0:T(8,128)(2,1)} %param.7) | copy-start | bytes 1769476
  165.2 7.1 %collective-permute-start.3 = (f32[9,1152]{1,0:T(8,128)S(1)}, f32[9,1152]{1,0:T(8,128)S(1)}, u32[]{:S(2)}, u32[]{:S(2)}) collective-permute-start(f32[9,1152]{1,0:T(8,128)S(1)} %get-tuple-element.37), channel_id=1, source_target_pairs={{0,1},{1,0},{2,3},{3,2},{4,5},{5,4},{6,7},{7,6},{8,9},{9,8},{10,11... | collective-permute-start | bytes 124424 | tf_op jit(solution)/shard_map/ppermute | solution.py:310
  167.0 2.1 %copy-start.2 = (bf16[1152,1728]{0,1:T(8,128)(2,1)S(1)}, bf16[1152,1728]{0,1:T(8,128)(2,1)}, u32[]{:S(2)}) copy-start(bf16[1152,1728]{0,1:T(8,128)(2,1)} %param.9) | copy-start | bytes 11943940
  (11 other events, 11.7 us)
where the time goes:
time: 174 us; the launch traced here: 173 us
  waiting for transfers between devices  57.6 us (33%)
  Pallas kernels  40.8 us (23%)
  starting transfers between devices  27.2 us (16%)
  blocking collectives  24.9 us (14%)
  local copies, waits for them, and re-layouts  21.7 us (12%)
    all_to_all x3, waiting for transfers between devices, exchange(): lax.all_to_all(array.reshape(parts, -1, lanes), axes, split_axis=0, conca...  53.3 us
    pallas_call x16, Pallas kernels, call(): pl.pallas_call(kernel, out_shape=shapes, in_specs=[pl.BlockSpec(memory_sp...  40.8 us
    all_to_all x1, blocking collectives, exchange(): lax.all_to_all(array.reshape(parts, -1, lanes), axes, split_axis=0, conca...  24.9 us
    unnamed x64, local copies, waits for them, and re-layouts  21.7 us
    all_to_all x3, starting transfers between devices, exchange(): lax.all_to_all(array.reshape(parts, -1, lanes), axes, split_axis=0, conca...  17.2 us
    ppermute x8, starting transfers between devices, swap(): return lax.ppermute(array, 'c', pairs)  9.97 us
    ppermute x8, waiting for transfers between devices, swap(): return lax.ppermute(array, 'c', pairs)  4.25 us
  transfers between devices with their start and end apart: 11, of which 5 were waited for; matrix products, arithmetic and copies ran while one was open for 0% of the time, Pallas kernels for 14%

commit v1 on v0

--- a/solution.py
+++ b/solution.py
@@ -104,22 +104,39 @@
     return lax.rem(row, patches) == lax.rem(col, patches)
 
 
-def space_forward(x_ref, cot_ref, w_qkv_ref, w_out_ref, w_time_ref, send_ref, qkv_ref, attn_ref, normed_ref):
+def space_forward(
+    x_hbm, cot_hbm, w_qkv_hbm, w_out_hbm, send_ref, qkv_ref, attn_ref, normed_ref, x_ref, w_qkv_ref, w_out_ref, sems
+):
+    width = x_ref.shape[1]
+    load_x = pltpu.make_async_copy(x_hbm, x_ref, sems.at[0])
+    load_x.start()
+    loads = []
+    for part in range(3):
+        rows = pl.ds(part * HK, HK)
+        loads.append(pltpu.make_async_copy(w_qkv_hbm.at[rows, :], w_qkv_ref.at[rows, :], sems.at[1 + part]))
+    load_out = pltpu.make_async_copy(w_out_hbm, w_out_ref, sems.at[4])
+    load_cot = pltpu.make_async_copy(cot_hbm, send_ref.at[:, pl.ds(width, width)], sems.at[5])
+    for load in loads + [load_out, load_cot]:
+        load.start()
+    load_x.wait()
     x = x_ref[...].astype(F32)
     normed = norm_parts(x)[0].astype(BF16)
     normed_ref[...] = normed
-    qkv = dot_nt(normed, w_qkv_ref[...]).astype(BF16)
-    qkv_ref[...] = qkv
-    query, keys, values = split_qkv(qkv)
+    parts = []
+    for part, load in enumerate(loads):
+        load.wait()
+        parts.append(dot_nt(normed, w_qkv_ref[part * HK : (part + 1) * HK, :]).astype(BF16))
+    query, keys, values = parts
+    qkv_ref[...] = jnp.concatenate(parts, axis=1)
     mix = HeadSum()
     for head in range(HEADS):
         weights = probs_t(query, keys, head, None).astype(BF16)
         mix.put(head, dot_tn(weights, head_window(values, head)))
     attn = mix.whole(BF16)
     attn_ref[...] = attn
-    width = x.shape[1]
+    load_out.wait()
     send_ref[:, :width] = (x + dot_nn(attn, w_out_ref[...])).astype(BF16)
-    send_ref[:, width:] = dot_nt(cot_ref[...], w_time_ref[...]).astype(BF16)
+    load_cot.wait()
 
 
 def attention_back(query, keys, values, dmix, keep, forward):
@@ -139,24 +156,37 @@
     return (mix.whole(BF16) if forward else None), dqkv
 
 
-def time_both(patches, recv_ref, w_qkv_ref, back_ref, normed_ref, dqkv_ref):
+def time_both(
+    patches, recv_ref, w_qkv_ref, w_out_ref, back_hbm, normed_hbm, keep_hbm, give_hbm,
+    back_ref, normed_ref, keep_ref, give_ref, sems,
+):
     width = w_qkv_ref.shape[1]
     hidden = recv_ref[:, :width].astype(F32)
     normed, rate = norm_parts(hidden)
     rounded = normed.astype(BF16)
     normed_ref[...] = rounded
+    copies = [pltpu.make_async_copy(normed_ref, normed_hbm, sems.at[0])]
+    copies[0].start()
     qkv = dot_nt(rounded, w_qkv_ref[...]).astype(BF16)
+    dattn = dot_nt(recv_ref[:, width:], w_out_ref[...]).astype(BF16)
     query, keys, values = split_qkv(qkv)
     keep = same_patch(hidden.shape[0], patches)
-    attn, dqkv = attention_back(query, keys, values, recv_ref[:, width:], keep, True)
-    dqkv_ref[...] = dqkv
+    attn, dqkv = attention_back(query, keys, values, dattn, keep, True)
+    pair_up(lax.axis_index("c"), dqkv, attn, keep_ref, give_ref)
     back_ref[:, width:] = attn
+    for source, target in ((keep_ref, keep_hbm), (give_ref, give_hbm)):
+        copies.append(pltpu.make_async_copy(source, target, sems.at[len(copies)]))
+        copies[-1].start()
     dnormed = dot_nn(dqkv, w_qkv_ref[...]).astype(BF16).astype(F32)
     back_ref[:, :width] = norm_back(dnormed, normed, rate).astype(BF16)
+    copies.append(pltpu.make_async_copy(back_ref, back_hbm, sems.at[3]))
+    copies[-1].start()
+    for copy in copies:
+        copy.wait()
 
 
 def space_backward(
-    core_ref, cot_ref, recv_ref, qkv_ref, attn_ref, w_out_ref, dhidden_ref, dqkv_ref, keep_ref, send_ref
+    cot_ref, recv_ref, qkv_ref, attn_ref, w_out_ref, dhidden_ref, dqkv_ref, keep_ref, send_ref
 ):
     width = cot_ref.shape[1]
     dhidden = cot_ref[...] + recv_ref[:, :width]
@@ -165,7 +195,7 @@
     query, keys, values = split_qkv(qkv_ref[...])
     dqkv = attention_back(query, keys, values, dattn, None, False)[1]
     dqkv_ref[...] = dqkv
-    pair_up(core_ref[0], dqkv, attn_ref[...], keep_ref, send_ref)
+    pair_up(lax.axis_index("c"), dqkv, attn_ref[...], keep_ref, send_ref)
 
 
 def space_finish(x_ref, dhidden_ref, dqkv_ref, w_qkv_ref, grad_ref):
@@ -175,17 +205,20 @@
     grad_ref[...] = dhidden_ref[...] + dres
 
 
-def call(kernel, outs, *args, flops=0):
+def call(kernel, outs, *args, flops=0, hbm_in=0, hbm_out=False, vmem_out=False, scratch=(), grant=8):
     size = sum(a.size * a.dtype.itemsize for a in args) + sum(math.prod(shape) * 2 for shape, _ in outs)
-    shapes = [jax.ShapeDtypeStruct(shape, dtype) for shape, dtype in outs]
+    vmem, hbm = pl.BlockSpec(memory_space=pltpu.VMEM), pl.BlockSpec(memory_space=pltpu.HBM)
+    args = [
+        pltpu.with_memory_space_constraint(arg, pltpu.HBM) if place < hbm_in else arg
+        for place, arg in enumerate(args)
+    ]
     return pl.pallas_call(
         kernel,
-        out_shape=shapes,
-        in_specs=[
-            pl.BlockSpec(memory_space=pltpu.SMEM if a.dtype == jnp.int32 else pltpu.VMEM) for a in args
-        ],
-        out_specs=[pl.BlockSpec(memory_space=pltpu.VMEM)] * len(outs),
-        compiler_params=pltpu.CompilerParams(vmem_limit_bytes=8 * 1024 * 1024),
+        out_shape=[pltpu.HBM(*out) if hbm_out else pltpu.VMEM(*out) if vmem_out else jax.ShapeDtypeStruct(*out) for out in outs],
+        in_specs=[hbm if place < hbm_in else vmem for place in range(len(args))],
+        out_specs=[hbm if hbm_out else vmem] * len(outs),
+        scratch_shapes=list(scratch),
+        compiler_params=pltpu.CompilerParams(vmem_limit_bytes=grant * 1024 * 1024),
         cost_estimate=pl.CostEstimate(flops=flops, bytes_accessed=size, transcendentals=0),
     )(*args)
 
@@ -203,7 +236,20 @@
 
 
 def transpose_rows(perm_ref, tokens_ref, out_ref):
-    out_ref[...] = dot_nt(perm_ref[...], tokens_ref[...]).astype(BF16)
+    width = perm_ref.shape[1]
+    tokens = tokens_ref[:, tokens_ref.shape[1] - width :]
+    out_ref[...] = dot_nt(perm_ref[...], tokens).astype(BF16)
+
+
+def stage(from_ref, to_ref, sems):
+    rows = from_ref.shape[0] // 4
+    copies = []
+    for part in range(4):
+        block = pl.ds(part * rows, rows)
+        copies.append(pltpu.make_async_copy(from_ref.at[block, :], to_ref.at[block, :], sems.at[part]))
+        copies[-1].start()
+    for copy in copies:
+        copy.wait()
 
 
 def mix_out(send_ref, recv_ref, w_out_ref, mixed_ref):
@@ -219,13 +265,10 @@
     send_ref[...] = jnp.where(core == 0, second, first)
 
 
-def time_pair(core_ref, dqkv_ref, recv_ref, keep_ref, send_ref):
-    pair_up(core_ref[0], dqkv_ref[...], recv_ref[:, recv_ref.shape[1] - HK :], keep_ref, send_ref)
-
-
-def weight_terms(core_ref, in_own, in_got, out_own, out_got, own_ref, got_ref, chunk_ref):
+def weight_terms(in_own, in_got, out_own, out_got, own_ref, got_ref, chunk_ref):
     block = in_own.shape[0] // 3
     low, high = HK // LANES * LANES, -(-HK // LANES) * LANES
+    core = lax.axis_index("c")
     width = own_ref.shape[1]
     third = width // 3
 
@@ -250,16 +293,16 @@
                 )
                 chunk_ref[:, 2 * width :] = rest.astype(BF16)
 
-    @pl.when(core_ref[0] == 0)
+    @pl.when(core == 0)
     def _():
         fill(in_own, in_got)
 
-    @pl.when(core_ref[0] != 0)
+    @pl.when(core != 0)
     def _():
         fill(out_own, out_got)
 
 
-def add_chunks(scale, core_ref, chunk_ref, keep_ref, send_ref):
+def add_chunks(scale, chunk_ref, keep_ref, send_ref):
     count, lanes = chunk_ref.shape
     total = chunk_ref[:16, :].astype(F32)
     for start in range(16, count, 16):
@@ -271,13 +314,13 @@
     last = jnp.concatenate([rest[0:2], rest[2:4], rest[4:6]], axis=1)
     low = jnp.concatenate([first, second[:1]], axis=0)
     high = jnp.concatenate([second[1:], last], axis=0)
-    core = core_ref[0]
+    core = lax.axis_index("c")
     keep_ref[...] = jnp.where(core == 0, low, high)
     send_ref[...] = jnp.where(core == 0, high, low)
 
 
-def place_rows(core_ref, keep_ref, got_ref, qkv_ref, out_ref):
-    core = core_ref[0]
+def place_rows(keep_ref, got_ref, qkv_ref, out_ref):
+    core = lax.axis_index("c")
     keep, got = keep_ref[...], got_ref[...]
     first = jnp.where(core == 0, keep, got)
     second = jnp.where(core == 0, got, keep)
@@ -300,7 +343,6 @@
     w_qkv_space, w_out_space = w_qkv_space.T, w_out_space.T
     w_qkv_time, w_out_time = w_qkv_time.T, w_out_time.T
     scale = 1.0 / math.sqrt(count * frames * lax.axis_size(("xh", "c")))
-    core = lax.axis_index("c").astype(jnp.int32).reshape(1)
     x = clips.reshape(count, width)
     top = cotangent.reshape(count, width)
     perm = jnp.asarray(permutation(width, chips))
@@ -320,50 +362,77 @@
         out = call(transpose_rows, [((perm.shape[0], count), BF16)], perm, tokens, flops=10**9)[0]
         return out, swap(out)
 
+    half = ((count, width), BF16)
     send, qkv_space, attn_space, normed_space = call(
         space_forward,
-        [((count, width + HK), BF16), ((count, qkv_cols), BF16), ((count, HK), BF16), ((count, width), BF16)],
-        x, top, w_qkv_space, w_out_space, w_out_time, flops=3 * 10**9,
+        [((count, 2 * width), BF16), ((count, qkv_cols), BF16), ((count, HK), BF16), half],
+        x, top, w_qkv_space, w_out_space,
+        flops=3 * 10**9,
+        hbm_in=4,
+        scratch=[
+            pltpu.VMEM((count, width), BF16),
+            pltpu.VMEM((qkv_cols, width), BF16),
+            pltpu.VMEM((HK, width), BF16),
+            pltpu.SemaphoreType.DMA((6,)),
+        ],
+        grant=16,
     )
     recv = exchange(send, SEQ, frames)
-    back, normed_time, dqkv_time = call(
+    back, normed_time, keep, give = call(
         functools.partial(time_both, own_patches),
-        [((count, width + HK), BF16), ((count, width), BF16), ((count, qkv_cols), BF16)],
-        recv, w_qkv_time, flops=5 * 10**9,
-    )
+        [((count, width + HK), BF16), half, half, half],
+        recv, w_qkv_time, w_out_time,
+        flops=5 * 10**9,
+        hbm_out=True,
+        scratch=[
+            pltpu.VMEM((count, width + HK), BF16),
+            pltpu.VMEM((count, width), BF16),
+            pltpu.VMEM((count, width), BF16),
+            pltpu.VMEM((count, width), BF16),
+            pltpu.SemaphoreType.DMA((4,)),
+        ],
+        grant=16,
+    )
+    chunk_shape = ((8 * chips, 2 * width + width // 3), BF16)
+    got_pair = swap(give)
+    rows_norm_time = rows_of(normed_time)
+    rows_top = rows_of(recv)
+    terms_time = call(
+        weight_terms, [chunk_shape], *rows_norm_time, *rows_top, keep, got_pair, flops=2 * 10**9
+    )[0]
     recv = exchange(back, SEQ, frames)
+    recv, terms_time = lax.optimization_barrier((recv, terms_time))
+    got_time = exchange(terms_time, CHIPS, chips)
     rows_norm_space = rows_of(normed_space)
-    rows_top = rows_of(top)
-    rows_norm_time = rows_of(normed_time)
-    half = ((count, width), BF16)
-    keep, give = call(time_pair, [half, half], core, dqkv_time, recv)
-    chunk_shape = ((8 * chips, 2 * width + width // 3), BF16)
-    terms_time = call(
-        weight_terms, [chunk_shape], core, *rows_norm_time, *rows_top, keep, swap(give),
-        flops=2 * 10**9,
-    )[0]
-    got_time = exchange(terms_time, CHIPS, chips)
     dhidden, dqkv_space, keep, give = call(
         space_backward, [half, ((count, qkv_cols), BF16), half, half],
-        core, top, recv, qkv_space, attn_space, w_out_space, flops=3 * 10**9,
-    )
+        top, recv, qkv_space, attn_space, w_out_space, flops=3 * 10**9,
+    )
+    got_pair = swap(give)
     rows_dhidden = rows_of(dhidden)
     terms_space = call(
-        weight_terms, [chunk_shape], core, *rows_norm_space, *rows_dhidden, keep, swap(give), flops=2 * 10**9
+        weight_terms, [chunk_shape], *rows_norm_space, *rows_dhidden, keep, got_pair, flops=2 * 10**9
     )[0]
-    got_space = exchange(terms_space, CHIPS, chips)
     grad_clips = call(
         space_finish, [half], x, dhidden, dqkv_space, w_qkv_space, flops=10**9
     )[0]
     mixed = call(mix_out, [half], send, recv, w_out_time, flops=10**9)[0]
+    terms_space, grad_clips, mixed, got_time = lax.optimization_barrier(
+        (terms_space, grad_clips, mixed, got_time)
+    )
+    terms_space = call(
+        stage, [chunk_shape], terms_space, hbm_in=1, vmem_out=True, scratch=[pltpu.SemaphoreType.DMA((4,))]
+    )[0]
+    got_space = exchange(terms_space, CHIPS, chips)
+    got_time, got_space = lax.optimization_barrier((got_time, got_space))
 
     def finish(got):
         rows = width // chips // 2
         own, other = call(
-            functools.partial(add_chunks, scale), [((rows, width), F32), ((rows, width), F32)], core, got
+            functools.partial(add_chunks, scale), [((rows, width), F32), ((rows, width), F32)], got
         )
         return call(
-            place_rows, [((rows, qkv_cols), F32), ((rows, HK), F32)], core, own, swap(other)
+            place_rows, [((rows, qkv_cols), F32), ((rows, HK), F32)], own, swap(other)
         )
 
     grad_qkv_time, grad_out_time = finish(got_time)

time: 174 us -> 167 us (0.960)
  blocking collectives: 24.9 us -> 69.9 us
  waiting for transfers between devices: 57.6 us -> 24.6 us
  local copies, waits for them, and re-layouts: 21.7 us -> 8.12 us
  starting transfers between devices: 27.2 us -> 18.6 us
  Pallas kernels: 40.8 us -> 44.4 us
    all_to_all x1 -> x2, blocking collectives: 24.9 us -> 69.9 us  [exchange(): lax.all_to_all(array.reshape(parts, -1, lanes), axes, split_axis=0, conca...]
    all_to_all x3 -> x2, waiting for transfers between devices: 53.3 us -> 21.8 us  [exchange(): lax.all_to_all(array.reshape(parts, -1, lanes), axes, split_axis=0, conca...]
    unnamed x64 -> x40, local copies, waits for them, and re-layouts: 21.7 us -> 8.12 us
    all_to_all x3 -> x2, starting transfers between devices: 17.2 us -> 10.7 us  [exchange(): lax.all_to_all(array.reshape(parts, -1, lanes), axes, split_axis=0, conca...]
    pallas_call x16, Pallas kernels: 40.8 us -> 44.4 us  [call(): pl.pallas_call(kernel, out_shape=[pltpu.HBM(*out) if hbm_out else pltpu.V...]
    ppermute x8, starting transfers between devices: 9.97 us -> 7.85 us  [swap(): return lax.ppermute(array, 'c', pairs)]
  transfers between devices with their start and end apart: 11 -> 10, of which waited for: 5 -> 4; matrix products, arithmetic and copies ran while one was open for 0% -> 0% of each run, Pallas kernels for 14% -> 20%
where the time goes in v1:
time: 167 us; the launch traced here: 166 us
  blocking collectives  69.9 us (42%)
  Pallas kernels  44.4 us (27%)
  waiting for transfers between devices  24.6 us (15%)
  starting transfers between devices  18.6 us (11%)
  local copies, waits for them, and re-layouts  8.12 us (5%)
    all_to_all x2, blocking collectives, exchange(): lax.all_to_all(array.reshape(parts, -1, lanes), axes, split_axis=0, conca...  69.9 us
    pallas_call x16, Pallas kernels, call(): pl.pallas_call(kernel, out_shape=[pltpu.HBM(*out) if hbm_out else pltpu.V...  44.4 us
    all_to_all x2, waiting for transfers between devices, exchange(): lax.all_to_all(array.reshape(parts, -1, lanes), axes, split_axis=0, conca...  21.8 us
    all_to_all x2, starting transfers between devices, exchange(): lax.all_to_all(array.reshape(parts, -1, lanes), axes, split_axis=0, conca...  10.7 us
    unnamed x40, local copies, waits for them, and re-layouts  8.12 us
    ppermute x8, starting transfers between devices, swap(): return lax.ppermute(array, 'c', pairs)  7.85 us
  transfers between devices with their start and end apart: 10, of which 4 were waited for; matrix products, arithmetic and copies ran while one was open for 0% of the time, Pallas kernels for 20%

profile of v1, /device:TPU:1, one launch (start us, length us, event | category | flops | bytes accessed | tf_op | source)
XLA Modules:
  0.0 166.4 jit_solution(15463009676267415928)
XLA Ops:
  0.6 5.9 %shard_map.118 = (bf16[256,2304]{1,0:T(8,128)(2,1)S(1)}, bf16[256,1728]{1,0:T(8,128)(2,1)S(1)}, bf16[256,576]{1,0:T(8,128)(2,1)S(1)}, bf16[256,1152]{1,0:T(8,128)(2,1)S(1)}) custom-call(bf16[256,1152]{1,0:T(8,128)(2,1)} %bitcast.26, bf16[256,1152]{1,0:T(8,128)(2,1)} %bitcast.31, bf16[1728,1152]{1,0:T(8,128)(2,1)} %bitcast.21, bf16[576,1152]{1,0:T(8,128)(2,1)} %bitcast.29), custom_call_target="tpu_custom_call" | custom-call | flops 3000000000 | bytes 9437184 | tf_op jit(solution)/shard_map/pallas_call | solution.py:215
  6.6 0.8 copy-done.9
  7.4 0.9 copy-done.16
  8.3 27.8 %all_to_all.20 = bf16[32,8,2304]{2,1,0:T(8,128)(2,1)S(1)} all-to-all(bf16[32,8,2304]{2,1,0:T(8,128)(2,1)S(1)} %bitcast.18), channel_id=1, replica_groups=mesh['z'=4,'y'=4,'xl'=2,'xh'=2,'c'=2] {'z','y','xl'}, dimensions={0} | all-to-all | bytes 2359296 | tf_op jit(solution)/shard_map/all_to_all | solution.py:356
  36.1 2.1 %shard_map.122.out_own = bf16[1536,256]{1,0:T(8,128)(2,1)} custom-call(bf16[1536,1152]{1,0:T(8,128)(2,1)S(1)} %copy-done, bf16[256,2304]{1,0:T(8,128)(2,1)S(1)} %bitcast.19), custom_call_target="tpu_custom_call" | custom-call | flops 1000000000 | bytes 5505024 | tf_op jit(solution)/shard_map/pallas_call | solution.py:215
  38.2 2.1 %collective-permute-start.2 = (bf16[1536,256]{1,0:T(8,128)(2,1)}, bf16[1536,256]{1,0:T(8,128)(2,1)}, u32[]{:S(2)}, u32[]{:S(2)}) collective-permute-start(bf16[1536,256]{1,0:T(8,128)(2,1)} %shard_map.122.out_own), channel_id=1, source_target_pairs={{0,1},{1,0},{2,3},{3,2},{4,5},{5,4},{6,7},{7,6},{8,9},{9,8},{10,11... | collective-permute-start | bytes 2359304 | tf_op jit(solution)/shard_map/ppermute | solution.py:352
  40.3 8.2 %shard_map.120 = (bf16[256,1728]{1,0:T(8,128)(2,1)}, bf16[256,1152]{1,0:T(8,128)(2,1)}, bf16[256,1152]{1,0:T(8,128)(2,1)}, bf16[256,1152]{1,0:T(8,128)(2,1)}) custom-call(bf16[256,2304]{1,0:T(8,128)(2,1)S(1)} %bitcast.20, bf16[1728,1152]{1,0:T(8,128)(2,1)S(1)} %bitcast.28, bf16[576,1152]{1,0:T(8,128)(2,1)S(1)} %bitcast.24), custom_call_target="tpu_custom_call" | custom-call | flops 5000000000 | bytes 9142272 | tf_op jit(solution)/shard_map/pallas_call | solution.py:215
  48.5 1.1 copy-done.11
  49.6 2.1 %shard_map.121.in_own = bf16[1536,256]{1,0:T(8,128)(2,1)} custom-call(bf16[1536,1152]{1,0:T(8,128)(2,1)S(1)} %copy-done, bf16[256,1152]{1,0:T(8,128)(2,1)S(1)} %copy-done.11), custom_call_target="tpu_custom_call" | custom-call | flops 1000000000 | bytes 4915200 | tf_op jit(solution)/shard_map/pallas_call | solution.py:215
  52.4 4.6 %all-to-all-start.1 = ((bf16[32,8,1728]{2,1,0:T(8,128)(2,1)}), bf16[32,8,1728]{2,1,0:T(8,128)(2,1)}, u32[]{:S(2)}, u32[]{:S(2)}) async-start(bf16[32,8,1728]{2,1,0:T(8,128)(2,1)} %bitcast.33), calls=%async_computation.1 | async-start | bytes 1835008 | tf_op jit(solution)/shard_map/all_to_all | solution.py:356
  57.1 2.2 %collective-permute-done.3.got_ref = bf16[256,1152]{1,0:T(8,128)(2,1)S(1)} collective-permute-done((bf16[256,1152]{1,0:T(8,128)(2,1)}, bf16[256,1152]{1,0:T(8,128)(2,1)S(1)}, u32[]{:S(2)}, u32[]{:S(2)}) %collective-permute-start.3) | collective-permute-done | bytes 589856 | tf_op jit(solution)/shard_map/ppermute | solution.py:352
  59.3 1.1 copy-done.15
  60.4 4.5 %shard_map.123 = bf16[512,2688]{1,0:T(8,128)(2,1)S(1)} custom-call(bf16[1536,256]{1,0:T(8,128)(2,1)} %shard_map.121.in_own, bf16[1536,256]{1,0:T(8,128)(2,1)} %collective-permute-done.1.in_got, bf16[1536,256]{1,0:T(8,128)(2,1)} %shard_map.122.out_own, bf16[1536,256]{1,0:T(8,128)(2,1)} %collective-permute-done.2.out_got, bf16[256,1152]{1,0:T(8,128)(2,1)S(1)} %copy-done.15, ...), custom_call_target="tpu_custom_call" | custom-call | flops 2000000000 | bytes 7077888 | tf_op jit(solution)/shard_map/pallas_call | solution.py:215
  64.8 1.5 copy-done.4
  66.4 6.9 %all-to-all-done.1 = bf16[32,8,1728]{2,1,0:T(8,128)(2,1)} async-done(((bf16[32,8,1728]{2,1,0:T(8,128)(2,1)}), bf16[32,8,1728]{2,1,0:T(8,128)(2,1)}, u32[]{:S(2)}, u32[]{:S(2)}) %all-to-all-start.1) | async-done | bytes 884768 | tf_op jit(solution)/shard_map/all_to_all | solution.py:356
  73.3 6.1 %all-to-all-start.2 = ((bf16[64,8,2688]{2,1,0:T(8,128)(2,1)}), bf16[64,8,2688]{2,1,0:T(8,128)(2,1)}, u32[]{:S(2)}, u32[]{:S(2)}) async-start(bf16[64,8,2688]{2,1,0:T(8,128)(2,1)} %bitcast.23), calls=%async_computation.2 | async-start | bytes 5505024 | tf_op jit(solution)/shard_map/all_to_all | solution.py:356
  79.4 1.1 copy-done.10
  80.5 1.2 shard_map.119.in_own
  81.7 1.7 %collective-permute-start = (bf16[1536,256]{1,0:T(8,128)(2,1)S(1)}, bf16[1536,256]{1,0:T(8,128)(2,1)S(1)}, u32[]{:S(2)}, u32[]{:S(2)}) collective-permute-start(bf16[1536,256]{1,0:T(8,128)(2,1)S(1)} %shard_map.119.in_own), channel_id=1, source_target_pairs={{0,1},{1,0},{2,3},{3,2},{4,5},{5,4},{6,7},{7,6},{8,9},{9,8},{10,11... | collective-permute-start | bytes 2359304 | tf_op jit(solution)/shard_map/ppermute | solution.py:352
  83.5 5.1 %shard_map.124 = (bf16[256,1152]{1,0:T(8,128)(2,1)S(1)}, bf16[256,1728]{1,0:T(8,128)(2,1)S(1)}, bf16[256,1152]{1,0:T(8,128)(2,1)S(1)}, bf16[256,1152]{1,0:T(8,128)(2,1)S(1)}) custom-call(bf16[256,1152]{1,0:T(8,128)(2,1)S(1)} %bitcast.32, bf16[256,1728]{1,0:T(8,128)(2,1)} %bitcast.9.recv_ref, bf16[256,1728]{1,0:T(8,128)(2,1)S(1)} %copy-done.17, ...), custom_call_target="tpu_custom_call" | custom-call | flops 3000000000 | bytes 6635520 | tf_op jit(solution)/shard_map/pallas_call | solution.py:215
  88.6 1.2 shard_map.125.out_own
  90.5 2.9 %shard_map.128 = bf16[256,1152]{1,0:T(8,128)(2,1)} custom-call(bf16[256,2304]{1,0:T(8,128)(2,1)S(1)} %copy-done.2, bf16[256,1728]{1,0:T(8,128)(2,1)} %bitcast.9.recv_ref, bf16[576,1152]{1,0:T(8,128)(2,1)S(1)} %bitcast.25), custom_call_target="tpu_custom_call" | custom-call | flops 1000000000 | bytes 3981312 | tf_op jit(solution)/shard_map/pallas_call | solution.py:215
  93.5 2.5 %shard_map.127 = bf16[256,1152]{1,0:T(8,128)(2,1)} custom-call(bf16[256,1152]{1,0:T(8,128)(2,1)S(1)} %bitcast.27, bf16[256,1152]{1,0:T(8,128)(2,1)S(1)} %get-tuple-element.43.tokens_ref.dhidden_ref, bf16[256,1728]{1,0:T(8,128)(2,1)S(1)} %get-tuple-element.46.dqkv_ref, bf16[1728,1152]{1,0:T(8,128)(2,1)S(1)} %bitcast.22), custom_call_target="tpu_custom_call" | custom-call | flops 1000000000 | bytes 6635520 | tf_op jit(solution)/shard_map/pallas_call | solution.py:215
  96.0 2.9 %shard_map.126.from_ref = bf16[512,2688]{1,0:T(8,128)(2,1)S(1)} custom-call(bf16[1536,256]{1,0:T(8,128)(2,1)S(1)} %shard_map.119.in_own, bf16[1536,256]{1,0:T(8,128)(2,1)S(1)} %collective-permute-done.in_got, bf16[1536,256]{1,0:T(8,128)(2,1)S(1)} %shard_map.125.out_own, bf16[1536,256]{1,0:T(8,128)(2,1)S(1)} %collective-permute-done.4.out_got, ...), custom_call_target="tpu_custom_call" | custom-call | flops 2000000000 | bytes 7077888 | tf_op jit(solution)/shard_map/pallas_call | solution.py:215
  98.9 1.6 copy-done.5
  100.5 14.9 %all-to-all-done.2 = bf16[64,8,2688]{2,1,0:T(8,128)(2,1)} async-done(((bf16[64,8,2688]{2,1,0:T(8,128)(2,1)}), bf16[64,8,2688]{2,1,0:T(8,128)(2,1)}, u32[]{:S(2)}, u32[]{:S(2)}) %all-to-all-start.2) | async-done | bytes 2752544 | tf_op jit(solution)/shard_map/all_to_all | solution.py:356
  115.4 1.8 %shard_map.129 = bf16[512,2688]{1,0:T(8,128)(2,1)S(1)} custom-call(bf16[512,2688]{1,0:T(8,128)(2,1)} %copy-done.5), custom_call_target="tpu_custom_call" | custom-call | bytes 5505024 | tf_op jit(solution)/shard_map/pallas_call | solution.py:215
  117.2 42.1 %all_to_all.21 = bf16[64,8,2688]{2,1,0:T(8,128)(2,1)S(1)} all-to-all(bf16[64,8,2688]{2,1,0:T(8,128)(2,1)S(1)} %bitcast.17), channel_id=1, replica_groups=mesh['z'=4,'y'=4,'xl'=2,'xh'=2,'c'=2] {'z','y','xl','xh'}, dimensions={0} | all-to-all | bytes 5505024 | tf_op jit(solution)/shard_map/all_to_all | solution.py:356
  159.7 2.5 %collective-permute-start.6 = (f32[9,1152]{1,0:T(8,128)S(1)}, f32[9,1152]{1,0:T(8,128)S(1)}, u32[]{:S(2)}, u32[]{:S(2)}) collective-permute-start(f32[9,1152]{1,0:T(8,128)S(1)} %get-tuple-element.54), channel_id=1, source_target_pairs={{0,1},{1,0},{2,3},{3,2},{4,5},{5,4},{6,7},{7,6},{8,9},{9,8},{10,11... | collective-permute-start | bytes 124424 | tf_op jit(solution)/shard_map/ppermute | solution.py:352
  162.2 2.1 %shard_map.132 = (f32[9,1152]{1,0:T(8,128)S(1)}, f32[9,1152]{1,0:T(8,128)S(1)}) custom-call(bf16[512,2688]{1,0:T(8,128)(2,1)} %bitcast.11.chunk_ref), custom_call_target="tpu_custom_call" | custom-call | bytes 2793984 | tf_op jit(solution)/shard_map/pallas_call | solution.py:215
  164.5 0.7 shard_map.131
  165.7 0.7 shard_map.133
  (46 shorter events, 2.5 us)
Async XLA Ops:
  0.6 35.5 %copy-start = (bf16[1536,1152]{1,0:T(8,128)(2,1)S(1)}, bf16[1536,1152]{1,0:T(8,128)(2,1)}, u32[]{:S(2)}) copy-start(bf16[1536,1152]{1,0:T(8,128)(2,1)} %constant.2.clone.perm_ref) | copy-start | bytes 10616836
  6.6 0.8 copy-start.9
  7.4 0.9 copy-start.16
  8.3 27.8 %copy-start.18 = (bf16[256,576]{1,0:T(8,128)(2,1)}, bf16[256,576]{1,0:T(8,128)(2,1)S(1)}, u32[]{:S(2)}) copy-start(bf16[256,576]{1,0:T(8,128)(2,1)S(1)} %get-tuple-element.42.attn_ref) | copy-start | bytes 884740
  8.3 29.9 %copy-start.1 = (bf16[256,2304]{1,0:T(8,128)(2,1)}, bf16[256,2304]{1,0:T(8,128)(2,1)S(1)}, u32[]{:S(2)}) copy-start(bf16[256,2304]{1,0:T(8,128)(2,1)S(1)} %get-tuple-element.35.send_ref) | copy-start | bytes 3538948
  36.1 4.2 %copy-start.6 = (bf16[1152,576]{0,1:T(8,128)(2,1)S(1)}, bf16[1152,576]{0,1:T(8,128)(2,1)}, u32[]{:S(2)}) copy-start(bf16[1152,576]{0,1:T(8,128)(2,1)} %param.12) | copy-start | bytes 3981316
  36.1 4.2 %copy-start.12 = (bf16[1152,1728]{0,1:T(8,128)(2,1)S(1)}, bf16[1152,1728]{0,1:T(8,128)(2,1)}, u32[]{:S(2)}) copy-start(bf16[1152,1728]{0,1:T(8,128)(2,1)} %param.11) | copy-start | bytes 11943940
  38.2 21.0 %collective-permute-start.2 = (bf16[1536,256]{1,0:T(8,128)(2,1)}, bf16[1536,256]{1,0:T(8,128)(2,1)}, u32[]{:S(2)}, u32[]{:S(2)}) collective-permute-start(bf16[1536,256]{1,0:T(8,128)(2,1)} %shard_map.122.out_own), channel_id=1, source_target_pairs={{0,1},{1,0},{2,3},{3,2},{4,5},{5,4},{6,7},{7,6},{8,9},{9,8},{10,11... | collective-permute-start | bytes 2359304 | tf_op jit(solution)/shard_map/ppermute | solution.py:352
  48.5 1.1 copy-start.11
  51.7 7.6 %collective-permute-start.1 = (bf16[1536,256]{1,0:T(8,128)(2,1)}, bf16[1536,256]{1,0:T(8,128)(2,1)}, u32[]{:S(2)}, u32[]{:S(2)}) collective-permute-start(bf16[1536,256]{1,0:T(8,128)(2,1)} %shard_map.121.in_own), channel_id=1, source_target_pairs={{0,1},{1,0},{2,3},{3,2},{4,5},{5,4},{6,7},{7,6},{8,9},{9,8},{10,11... | collective-permute-start | bytes 2359304 | tf_op jit(solution)/shard_map/ppermute | solution.py:352
  52.4 20.9 %all-to-all-start.1 = ((bf16[32,8,1728]{2,1,0:T(8,128)(2,1)}), bf16[32,8,1728]{2,1,0:T(8,128)(2,1)}, u32[]{:S(2)}, u32[]{:S(2)}) async-start(bf16[32,8,1728]{2,1,0:T(8,128)(2,1)} %bitcast.33), calls=%async_computation.1 | async-start | bytes 1835008 | tf_op jit(solution)/shard_map/all_to_all | solution.py:356
  57.0 2.3 %collective-permute-start.3 = (bf16[256,1152]{1,0:T(8,128)(2,1)}, bf16[256,1152]{1,0:T(8,128)(2,1)S(1)}, u32[]{:S(2)}, u32[]{:S(2)}) collective-permute-start(bf16[256,1152]{1,0:T(8,128)(2,1)} %get-tuple-element.39), channel_id=1, source_target_pairs={{0,1},{1,0},{2,3},{3,2},{4,5},{5,4},{6,7},{7,6},{8,9},{9,8},{10,11... | collective-permute-start | bytes 1769480 | tf_op jit(solution)/shard_map/ppermute | solution.py:352
  59.3 1.1 copy-start.15
  64.8 1.6 copy-start.4
  73.3 42.1 %all-to-all-start.2 = ((bf16[64,8,2688]{2,1,0:T(8,128)(2,1)}), bf16[64,8,2688]{2,1,0:T(8,128)(2,1)}, u32[]{:S(2)}, u32[]{:S(2)}) async-start(bf16[64,8,2688]{2,1,0:T(8,128)(2,1)} %bitcast.23), calls=%async_computation.2 | async-start | bytes 5505024 | tf_op jit(solution)/shard_map/all_to_all | solution.py:356
  79.4 1.1 copy-start.10
  80.5 3.0 %copy-start.13 = (bf16[1152,576]{0,1:T(8,128)(2,1)S(1)}, bf16[1152,576]{0,1:T(8,128)(2,1)}, u32[]{:S(2)}) copy-start(bf16[1152,576]{0,1:T(8,128)(2,1)} %param.10) | copy-start | bytes 3981316
  80.5 3.0 %copy-start.14 = (bf16[1,1,256,1152]{3,2,1,0:T(8,128)(2,1)S(1)}, bf16[1,1,256,1152]{3,2,1,0:T(8,128)(2,1)}, u32[]{:S(2)}) copy-start(bf16[1,1,256,1152]{3,2,1,0:T(8,128)(2,1)} %param.8) | copy-start | bytes 1769476
  80.5 3.0 %copy-start.17 = (bf16[256,1728]{1,0:T(8,128)(2,1)S(1)}, bf16[256,1728]{1,0:T(8,128)(2,1)}, u32[]{:S(2)}) copy-start(bf16[256,1728]{1,0:T(8,128)(2,1)} %copy-done.16) | copy-start | bytes 2654212
  80.5 3.0 %copy-start.19 = (bf16[256,576]{1,0:T(8,128)(2,1)S(1)}, bf16[256,576]{1,0:T(8,128)(2,1)}, u32[]{:S(2)}) copy-start(bf16[256,576]{1,0:T(8,128)(2,1)} %copy-done.18) | copy-start | bytes 884740
  81.7 14.3 %collective-permute-start = (bf16[1536,256]{1,0:T(8,128)(2,1)S(1)}, bf16[1536,256]{1,0:T(8,128)(2,1)S(1)}, u32[]{:S(2)}, u32[]{:S(2)}) collective-permute-start(bf16[1536,256]{1,0:T(8,128)(2,1)S(1)} %shard_map.119.in_own), channel_id=1, source_target_pairs={{0,1},{1,0},{2,3},{3,2},{4,5},{5,4},{6,7},{7,6},{8,9},{9,8},{10,11... | collective-permute-start | bytes 2359304 | tf_op jit(solution)/shard_map/ppermute | solution.py:352
  88.6 1.9 %copy-start.2 = (bf16[256,2304]{1,0:T(8,128)(2,1)S(1)}, bf16[256,2304]{1,0:T(8,128)(2,1)}, u32[]{:S(2)}) copy-start(bf16[256,2304]{1,0:T(8,128)(2,1)} %copy-done.1) | copy-start | bytes 3538948
  88.6 1.9 %copy-start.7 = (bf16[1152,576]{0,1:T(8,128)(2,1)S(1)}, bf16[1152,576]{0,1:T(8,128)(2,1)}, u32[]{:S(2)}) copy-start(bf16[1152,576]{0,1:T(8,128)(2,1)} %param.12) | copy-start | bytes 3981316
  88.6 4.9 %copy-start.8 = (bf16[1,1,256,1152]{3,2,1,0:T(8,128)(2,1)S(1)}, bf16[1,1,256,1152]{3,2,1,0:T(8,128)(2,1)}, u32[]{:S(2)}) copy-start(bf16[1,1,256,1152]{3,2,1,0:T(8,128)(2,1)} %param.7) | copy-start | bytes 1769476
  89.9 3.6 %copy-start.3 = (bf16[1152,1728]{0,1:T(8,128)(2,1)S(1)}, bf16[1152,1728]{0,1:T(8,128)(2,1)}, u32[]{:S(2)}) copy-start(bf16[1152,1728]{0,1:T(8,128)(2,1)} %param.9) | copy-start | bytes 11943940
  89.9 6.1 %collective-permute-start.4 = (bf16[1536,256]{1,0:T(8,128)(2,1)S(1)}, bf16[1536,256]{1,0:T(8,128)(2,1)S(1)}, u32[]{:S(2)}, u32[]{:S(2)}) collective-permute-start(bf16[1536,256]{1,0:T(8,128)(2,1)S(1)} %shard_map.125.out_own), channel_id=1, source_target_pairs={{0,1},{1,0},{2,3},{3,2},{4,5},{5,4},{6,7},{7,6},{8,9},{9,8},{10,11... | collective-permute-start | bytes 2359304 | tf_op jit(solution)/shard_map/ppermute | solution.py:352
  90.4 5.6 %collective-permute-start.5 = (bf16[256,1152]{1,0:T(8,128)(2,1)S(1)}, bf16[256,1152]{1,0:T(8,128)(2,1)S(1)}, u32[]{:S(2)}, u32[]{:S(2)}) collective-permute-start(bf16[256,1152]{1,0:T(8,128)(2,1)S(1)} %get-tuple-element.45), channel_id=1, source_target_pairs={{0,1},{1,0},{2,3},{3,2},{4,5},{5,4},{6,7},{7,6},{8,9},{9,8},{10,11... | collective-permute-start | bytes 1769480 | tf_op jit(solution)/shard_map/ppermute | solution.py:352
  98.9 1.6 copy-start.5
  159.7 4.8 %collective-permute-start.6 = (f32[9,1152]{1,0:T(8,128)S(1)}, f32[9,1152]{1,0:T(8,128)S(1)}, u32[]{:S(2)}, u32[]{:S(2)}) collective-permute-start(f32[9,1152]{1,0:T(8,128)S(1)} %get-tuple-element.54), channel_id=1, source_target_pairs={{0,1},{1,0},{2,3},{3,2},{4,5},{5,4},{6,7},{7,6},{8,9},{9,8},{10,11... | collective-permute-start | bytes 124424 | tf_op jit(solution)/shard_map/ppermute | solution.py:352
  164.4 1.3 collective-permute-start.7

commit v2 on v1

v2 whole, which is shorter than its diff:
```python
import functools
import math

import jax
import jax.numpy as jnp
import numpy as np
from jax import lax
from jax.experimental import pallas as pl
from jax.experimental.pallas import tpu as pltpu
from jax.sharding import Mesh
from jax.sharding import PartitionSpec as P

HEADS = 8
HEAD_DIM = 72
HK = HEADS * HEAD_DIM
EPS = 1e-06
LANES = 128
F32 = jnp.float32
BF16 = jnp.bfloat16


def windows():
    out = []
    for head in range(HEADS):
        low, high = head * HEAD_DIM, (head + 1) * HEAD_DIM
        start = low // LANES * LANES
        stop = min(-(-high // LANES) * LANES, HK)
        out.append((low, high, start, stop))
    return out


def dot_nn(a, b):
    return lax.dot_general(a, b, (((1,), (0,)), ((), ())), preferred_element_type=F32)


def dot_nt(a, b):
    return lax.dot_general(a, b, (((1,), (1,)), ((), ())), preferred_element_type=F32)


def dot_tn(a, b):
    return lax.dot_general(a, b, (((0,), (0,)), ((), ())), preferred_element_type=F32)


def norm_parts(tokens):
    center = tokens - jnp.mean(tokens, axis=-1, keepdims=True)
    spread = jnp.mean(center * center, axis=-1, keepdims=True)
    rate = lax.rsqrt(spread + EPS)
    return center * rate, rate


def norm_back(grad, normed, rate):
    first = jnp.mean(grad, axis=-1, keepdims=True)
    second = jnp.mean(grad * normed, axis=-1, keepdims=True)
    return rate * (grad - first - normed * second)


def split_qkv(qkv):
    return qkv[:, :HK], qkv[:, HK : 2 * HK], qkv[:, 2 * HK :]


class HeadSum:
    def __init__(self):
        self.slabs = [None] * -(-HK // LANES)

    def put(self, head, piece):
        low, high, start, stop = windows()[head]
        for slab in range(start // LANES, -(-stop // LANES)):
            left, right = slab * LANES, min((slab + 1) * LANES, HK)
            part = piece[:, left - start : right - start]
            held = self.slabs[slab]
            if held is not None:
                lane = left + lax.broadcasted_iota(jnp.int32, part.shape, 1)
                part = jnp.where((lane >= low) & (lane < high), part, held)
            self.slabs[slab] = part

    def whole(self, dtype):
        return jnp.concatenate([slab.astype(dtype) for slab in self.slabs], axis=1)


def head_part(array, head):
    low, high, start, stop = windows()[head]
    part = array[:, start:stop]
    lane = start + lax.broadcasted_iota(jnp.int32, part.shape, 1)
    return jnp.where((lane >= low) & (lane < high), part, jnp.zeros_like(part))


def head_window(array, head):
    _, _, start, stop = windows()[head]
    return array[:, start:stop]


def probs_t(query, keys, head, keep):
    scores = dot_nt(head_part(keys, head), head_window(query, head)) * HEAD_DIM ** (-0.5)
    if keep is not None:
        scores = jnp.where(keep, scores, -1e30)
    peak = jnp.max(scores, axis=0, keepdims=True)
    weights = jnp.exp(scores - peak)
    return weights / jnp.sum(weights, axis=0, keepdims=True)


def same_patch(count, patches):
    row = lax.broadcasted_iota(jnp.int32, (count, count), 0)
    col = lax.broadcasted_iota(jnp.int32, (count, count), 1)
    return lax.rem(row, patches) == lax.rem(col, patches)


def space_forward(
    x_hbm, cot_hbm, w_qkv_hbm, w_out_hbm, send_ref, qkv_hbm, attn_hbm, normed_hbm,
    x_ref, w_qkv_ref, w_out_ref, qkv_ref, attn_ref, normed_ref, sems,
):
    width = x_ref.shape[1]
    load_x = pltpu.make_async_copy(x_hbm, x_ref, sems.at[0])
    load_x.start()
    loads = []
    for part in range(3):
        rows = pl.ds(part * HK, HK)
        loads.append(pltpu.make_async_copy(w_qkv_hbm.at[rows, :], w_qkv_ref.at[rows, :], sems.at[1 + part]))
    load_out = pltpu.make_async_copy(w_out_hbm, w_out_ref, sems.at[4])
    load_cot = pltpu.make_async_copy(cot_hbm, send_ref.at[:, pl.ds(width, width)], sems.at[5])
    for load in loads + [load_out, load_cot]:
        load.start()
    load_x.wait()
    x = x_ref[...].astype(F32)
    normed = norm_parts(x)[0].astype(BF16)
    normed_ref[...] = normed
    store_normed = pltpu.make_async_copy(normed_ref, normed_hbm, sems.at[6])
    store_normed.start()
    parts = []
    for part, load in enumerate(loads):
        load.wait()
        parts.append(dot_nt(normed, w_qkv_ref[part * HK : (part + 1) * HK, :]).astype(BF16))
    query, keys, values = parts
    qkv_ref[...] = jnp.concatenate(parts, axis=1)
    store_qkv = pltpu.make_async_copy(qkv_ref, qkv_hbm, sems.at[7])
    store_qkv.start()
    mix = HeadSum()
    for head in range(HEADS):
        weights = probs_t(query, keys, head, None).astype(BF16)
        mix.put(head, dot_tn(weights, head_window(values, head)))
    attn = mix.whole(BF16)
    attn_ref[...] = attn
    store_attn = pltpu.make_async_copy(attn_ref, attn_hbm, sems.at[8])
    store_attn.start()
    load_out.wait()
    send_ref[:, :width] = (x + dot_nn(attn, w_out_ref[...])).astype(BF16)
    for copy in (load_cot, store_normed, store_qkv, store_attn):
        copy.wait()


def attention_back(query, keys, values, dmix, keep, forward):
    mix, dq, dk, dv = HeadSum(), HeadSum(), HeadSum(), HeadSum()
    for head in range(HEADS):
        weights = probs_t(query, keys, head, keep)
        rounded = weights.astype(BF16)
        if forward:
            mix.put(head, dot_tn(rounded, head_window(values, head)))
        dprobs = dot_nt(head_part(values, head), head_window(dmix, head)).astype(BF16).astype(F32)
        total = jnp.sum(weights * dprobs, axis=0, keepdims=True)
        dscores = (weights * (dprobs - total) * HEAD_DIM ** (-0.5)).astype(BF16)
        dv.put(head, dot_nn(rounded, head_window(dmix, head)))
        dk.put(head, dot_nn(dscores, head_window(query, head)))
        dq.put(head, dot_tn(dscores, head_window(keys, head)))
    dqkv = jnp.concatenate([dq.whole(BF16), dk.whole(BF16), dv.whole(BF16)], axis=1)
    return (mix.whole(BF16) if forward else None), dqkv


def time_both(
    patches, recv_ref, w_qkv_ref, w_out_ref, back_hbm, normed_hbm, top_hbm, keep_hbm, give_hbm,
    back_ref, normed_ref, keep_ref, give_ref, sems,
):
    width = w_qkv_ref.shape[1]
    hidden = recv_ref[:, :width].astype(F32)
    normed, rate = norm_parts(hidden)
    rounded = normed.astype(BF16)
    normed_ref[...] = rounded
    copies = [
        pltpu.make_async_copy(normed_ref, normed_hbm, sems.at[0]),
        pltpu.make_async_copy(recv_ref.at[:, pl.ds(width, width)], top_hbm, sems.at[1]),
    ]
    for copy in copies:
        copy.start()
    qkv = dot_nt(rounded, w_qkv_ref[...]).astype(BF16)
    dattn = dot_nt(recv_ref[:, width:], w_out_ref[...]).astype(BF16)
    query, keys, values = split_qkv(qkv)
    keep = same_patch(hidden.shape[0], patches)
    attn, dqkv = attention_back(query, keys, values, dattn, keep, True)
    pair_up(lax.axis_index("c"), dqkv, attn, keep_ref, give_ref)
    back_ref[:, width:] = attn
    for source, target in ((keep_ref, keep_hbm), (give_ref, give_hbm)):
        copies.append(pltpu.make_async_copy(source, target, sems.at[len(copies)]))
        copies[-1].start()
    dnormed = dot_nn(dqkv, w_qkv_ref[...]).astype(BF16).astype(F32)
    back_ref[:, :width] = norm_back(dnormed, normed, rate).astype(BF16)
    copies.append(pltpu.make_async_copy(back_ref, back_hbm, sems.at[4]))
    copies[-1].start()
    for copy in copies:
        copy.wait()


def space_backward(
    cot_ref, recv_ref, qkv_ref, attn_ref, w_out_ref, dhidden_ref, dqkv_ref, keep_ref, send_ref
):
    width = cot_ref.shape[1]
    dhidden = cot_ref[...] + recv_ref[:, :width]
    dhidden_ref[...] = dhidden
    dattn = dot_nt(dhidden, w_out_ref[...]).astype(BF16)
    query, keys, values = split_qkv(qkv_ref[...])
    dqkv = attention_back(query, keys, values, dattn, None, False)[1]
    dqkv_ref[...] = dqkv
    pair_up(lax.axis_index("c"), dqkv, attn_ref[...], keep_ref, send_ref)


def space_finish(x_ref, dhidden_ref, dqkv_ref, w_qkv_ref, grad_ref):
    normed, rate = norm_parts(x_ref[...].astype(F32))
    dnormed = dot_nn(dqkv_ref[...], w_qkv_ref[...]).astype(BF16).astype(F32)
    dres = norm_back(dnormed, normed, rate).astype(BF16)
    grad_ref[...] = dhidden_ref[...] + dres


def call(kernel, outs, *args, flops=0, hbm_in=0, hbm_out=(), scratch=(), grant=8):
    size = sum(a.size * a.dtype.itemsize for a in args) + sum(math.prod(shape) * 2 for shape, _ in outs)
    vmem, hbm = pl.BlockSpec(memory_space=pltpu.VMEM), pl.BlockSpec(memory_space=pltpu.HBM)
    args = [
        pltpu.with_memory_space_constraint(arg, pltpu.HBM) if place < hbm_in else arg
        for place, arg in enumerate(args)
    ]
    return pl.pallas_call(
        kernel,
        out_shape=[
            pltpu.HBM(*out) if place in hbm_out else jax.ShapeDtypeStruct(*out)
            for place, out in enumerate(outs)
        ],
        in_specs=[hbm if place < hbm_in else vmem for place in range(len(args))],
        out_specs=[hbm if place in hbm_out else vmem for place in range(len(outs))],
        scratch_shapes=list(scratch),
        compiler_params=pltpu.CompilerParams(vmem_limit_bytes=grant * 1024 * 1024),
        cost_estimate=pl.CostEstimate(flops=flops, bytes_accessed=size, transcendentals=0),
    )(*args)


def chunk_rows(chunks, rows, parts):
    table = np.zeros((3, chunks, parts, 8, parts, chunks * rows), np.float32)
    for chunk in range(chunks):
        for part in range(parts):
            for lane in range(8):
                table[0, chunk, part, lane, part, chunk * rows + lane] = 1
                table[1, chunk, part, lane, part, chunk * rows + 8 + lane] = 1
            for lane in range(6):
                table[2, chunk, part, lane, part, chunk * rows + 16 + lane % 2] = 1
    return table.reshape(3 * chunks * parts * 8, parts * chunks * rows).astype(jnp.bfloat16)


def mix_out(send_ref, recv_ref, w_out_ref, mixed_ref):
    width = w_out_ref.shape[1]
    mixed = send_ref[:, :width].astype(F32) + dot_nn(recv_ref[:, width:], w_out_ref[...])
    mixed_ref[...] = mixed.astype(BF16)


def pair_up(core, dqkv, attn, keep_ref, send_ref):
    second = jnp.concatenate([dqkv[:, 2 * HK :], attn], axis=1)
    first = dqkv[:, : 2 * HK]
    keep_ref[...] = jnp.where(core == 0, first, second)
    send_ref[...] = jnp.where(core == 0, second, first)


def weight_terms(lines, in_own, in_got, out_own, out_got, own_ref, got_ref, term_ref, total_ref):
    width = own_ref.shape[1]
    low, high = HK // LANES * LANES, -(-HK // LANES) * LANES
    step = width // 3
    rows = width // (lines * lines)
    core = lax.axis_index("c")

    def product(one, two, left, right):
        return dot_tn(one, own_ref[:, left:right]) + dot_tn(two, got_ref[:, left:right])

    def place(order):
        for first in range(0, lines * lines, 2):
            pair = [total_ref[pl.ds(order(block) * rows, rows), :] for block in (first, first + 1)]
            term_ref[pl.ds(first * rows, 2 * rows), :] = jnp.concatenate(pair, axis=0).astype(BF16)

    @pl.when(core == 0)
    def _():
        for start in range(0, width, step):
            block = slice(start, start + step)
            total_ref[block, :] = product(in_own[:, block], in_got[:, block], 0, width)
        place(lambda block: block)

    @pl.when(core != 0)
    def _():
        for start in range(0, width, step):
            block = slice(start, start + step)
            left = product(in_own[:, block], in_got[:, block], 0, high)
            right = product(out_own[:, block], out_got[:, block], low, width)
            lane = low + lax.broadcasted_iota(jnp.int32, (step, high - low), 1)
            total_ref[block, :low] = left[:, :low]
            total_ref[block, low:high] = jnp.where(lane < HK, left[:, low:], right[:, : high - low])
            total_ref[block, high:] = right[:, high - low :]
        place(lambda block: block % lines * lines + block // lines)


def add_lines(lines, table_ref, time_ref, space_ref, chunk_ref):
    width = time_ref.shape[1]
    third = width // 3
    sums = []
    for ref in (time_ref, space_ref):
        rows = ref.shape[0] // lines
        total = ref[:rows, :].astype(F32)
        for line in range(1, lines):
            total = total + ref[line * rows : (line + 1) * rows, :].astype(F32)
        sums.append(total.astype(BF16))
    sums = jnp.concatenate(sums, axis=0)
    block = table_ref.shape[0] // 3
    for part in range(3):
        whole = dot_nn(table_ref[part * block : (part + 1) * block, :], sums)
        if part < 2:
            chunk_ref[:, part * width : (part + 1) * width] = whole.astype(BF16)
        else:
            row = lax.rem(lax.broadcasted_iota(jnp.int32, (block, third), 0), 8)
            rest = jnp.where(
                row < 2,
                whole[:, :third],
                jnp.where(row < 4, whole[:, third : 2 * third], whole[:, 2 * third :]),
            )
            chunk_ref[:, 2 * width :] = rest.astype(BF16)


def add_chunks(scale, chunk_ref, keep_ref, send_ref):
    count, lanes = chunk_ref.shape
    total = chunk_ref[:16, :].astype(F32)
    for start in range(16, count, 16):
        total = total + chunk_ref[start : start + 16, :].astype(F32)
    total = total * scale
    width = lanes // 7 * 3
    third = width // 3
    core = lax.axis_index("c")
    for part in range(2):
        held = total[8 * part : 8 * part + 8]
        first, second, rest = held[:, :width], held[:, width : 2 * width], held[:, 2 * width :]
        last = jnp.concatenate([rest[0:2], rest[2:4], rest[4:6]], axis=1)
        low = jnp.concatenate([first, second[:1]], axis=0)
        high = jnp.concatenate([second[1:], last], axis=0)
        keep_ref[part] = jnp.where(core == 0, low, high)
        send_ref[part] = jnp.where(core == 0, high, low)


def place_rows(keep_ref, got_ref, qkv_time_ref, out_time_ref, qkv_space_ref, out_space_ref):
    core = lax.axis_index("c")
    for part, (qkv_ref, out_ref) in enumerate(
        ((qkv_time_ref, out_time_ref), (qkv_space_ref, out_space_ref))
    ):
        keep, got = keep_ref[part], got_ref[part]
        first = jnp.where(core == 0, keep, got)
        second = jnp.where(core == 0, got, keep)
        qkv_ref[:, : 2 * HK] = first
        qkv_ref[:, 2 * HK :] = second[:, :HK]
        out_ref[...] = second[:, HK:]


SEQ = ("z", "y", "xl")
ALL = ("z", "y", "xl", "xh", "c")
SIDE = 4


def device(z, y, x, core):
    return ((z * SIDE + y) * SIDE + x) * 2 + core


def line_groups():
    side = range(SIDE)
    groups = [[device(z, y, x, 0) for z in side] for y in side for x in side]
    return groups + [[device(z, y, x, 1) for y in side] for z in side for x in side]


def plane_groups():
    side = range(SIDE)
    groups = [[device(z, y, x, 0) for y in side for x in side] for z in side]
    return groups + [[device(z, y, x, 1) for z in side for x in side] for y in side]


def on_device(clips, cotangent, w_qkv_space, w_out_space, w_qkv_time, w_out_time):
    patches, width = clips.shape[2], clips.shape[3]
    frames = lax.axis_size(SEQ)
    own_patches = patches // frames
    count = patches
    qkv_cols = w_qkv_space.shape[1]
    w_qkv_space, w_out_space = w_qkv_space.T, w_out_space.T
    w_qkv_time, w_out_time = w_qkv_time.T, w_out_time.T
    scale = 1.0 / math.sqrt(count * frames * lax.axis_size(("xh", "c")))
    x = clips.reshape(count, width)
    top = cotangent.reshape(count, width)
    plane = SIDE * SIDE
    rows = width // (plane * SIDE)
    table = jnp.asarray(chunk_rows(plane, rows, 2))
    half = ((count, width), BF16)
    term = ((width, width), BF16)

    def swap(array):
        return lax.ppermute(array, "c", [(0, 1), (1, 0)])

    def exchange(array, axes, parts, groups=None):
        lanes = array.shape[1]
        array = lax.all_to_all(
            array.reshape(parts, -1, lanes),
            axes,
            split_axis=0,
            concat_axis=0,
            tiled=True,
            axis_index_groups=groups,
        )
        return array.reshape(-1, lanes)

    def terms(*args):
        return call(
            functools.partial(weight_terms, SIDE),
            [term],
            *args,
            flops=2 * 10**9,
            scratch=[pltpu.VMEM((width, width), F32)],
            grant=16,
        )[0]

    def buffers(*shapes):
        return [pltpu.VMEM(*shape) for shape in shapes]

    qkv = ((count, qkv_cols), BF16)
    mix = ((count, HK), BF16)
    send, qkv_space, attn_space, normed_space = call(
        space_forward,
        [((count, 2 * width), BF16), qkv, mix, half],
        x, top, w_qkv_space, w_out_space,
        flops=3 * 10**9,
        hbm_in=4,
        hbm_out=(1, 2, 3),
        scratch=buffers(half, ((qkv_cols, width), BF16), ((HK, width), BF16), qkv, mix, half)
        + [pltpu.SemaphoreType.DMA((9,))],
        grant=16,
    )
    recv = exchange(send, SEQ, frames)
    pack = ((count, width + HK), BF16)
    back, normed_time, top_time, keep, give = call(
        functools.partial(time_both, own_patches),
        [pack, half, half, half, half],
        recv, w_qkv_time, w_out_time,
        flops=5 * 10**9,
        hbm_out=(0, 1, 2, 3, 4),
        scratch=buffers(pack, half, half, half) + [pltpu.SemaphoreType.DMA((5,))],
        grant=16,
    )
    terms_time = terms(
        normed_time, swap(normed_time), top_time, swap(top_time), keep, swap(give)
    )
    recv = exchange(back, SEQ, frames)
    recv, terms_time = lax.optimization_barrier((recv, terms_time))
    got_time = exchange(terms_time, ALL, SIDE, line_groups())
    dhidden, dqkv_space, keep, give = call(
        space_backward, [half, qkv, half, half],
        top, recv, qkv_space, attn_space, w_out_space, flops=3 * 10**9,
    )
    terms_space = terms(
        normed_space, swap(normed_space), dhidden, swap(dhidden), keep, swap(give)
    )
    got_space = exchange(terms_space, ALL, SIDE, line_groups())
    grad_clips = call(
        space_finish, [half], x, dhidden, dqkv_space, w_qkv_space, flops=10**9
    )[0]
    mixed = call(mix_out, [half], send, recv, w_out_time, flops=10**9)[0]
    chunks = call(
        functools.partial(add_lines, SIDE),
        [((plane * 16, 2 * width + width // 3), BF16)],
        table, got_time, got_space,
        flops=10**9,
    )[0]
    chunks, grad_clips, mixed = lax.optimization_barrier((chunks, grad_clips, mixed))
    chunks = exchange(chunks, ALL, plane, plane_groups())
    own_rows = ((2, rows // 2, width), F32)
    own, other = call(functools.partial(add_chunks, scale), [own_rows, own_rows], chunks)
    grad_qkv = ((rows // 2, qkv_cols), F32)
    grad_out = ((rows // 2, HK), F32)
    grad_qkv_time, grad_out_time, grad_qkv_space, grad_out_space = call(
        place_rows, [grad_qkv, grad_out, grad_qkv, grad_out], own, swap(other)
    )
    return (
        mixed.reshape(clips.shape),
        grad_clips.reshape(clips.shape),
        grad_qkv_space,
        grad_out_space,
        grad_qkv_time,
        grad_out_time,
    )


def solution(mesh):
    fine = Mesh(mesh.devices.reshape(4, 4, 2, 2, 2), ("z", "y", "xl", "xh", "c"))
    tokens = P(("xh", "c"), SEQ, None, None)
    rows = P(("z", "y", "xl", "xh", "c"), None)
    return jax.shard_map(
        on_device,
        mesh=fine,
        in_specs=(tokens, tokens, P(), P(), P(), P()),
        out_specs=(tokens, tokens, rows, rows, rows, rows),
        check_vma=False,
    )
```

time: 167 us -> 145 us (0.87)
  blocking collectives: 69.9 us -> 53.9 us
  local copies, waits for them, and re-layouts: 8.12 us -> 22.7 us
  Pallas kernels: 44.4 us -> 31.3 us
  waiting for transfers between devices: 24.6 us -> 16.6 us
    all_to_all x2, blocking collectives: 69.9 us -> 53.9 us  [exchange(): lax.all_to_all(array.reshape(parts, -1, lanes), axes, split_axis=0, conca...]
    unnamed x40 -> x50, local copies, waits for them, and re-layouts: 8.12 us -> 22.7 us
    pallas_call x16 -> x10, Pallas kernels: 44.4 us -> 31.3 us  [call(): pl.pallas_call(kernel, out_shape=[pltpu.HBM(*out) if place in hbm_out els...]
    all_to_all x2 -> x3, waiting for transfers between devices: 21.8 us -> 9.91 us  [exchange(): lax.all_to_all(array.reshape(parts, -1, lanes), axes, split_axis=0, conca...]
    ppermute x8 -> x7, waiting for transfers between devices: 2.75 us -> 6.71 us  [swap(): return lax.ppermute(array, 'c', [(0, 1), (1, 0)])]
    all_to_all x2 -> x3, starting transfers between devices: 10.7 us -> 12.9 us  [exchange(): lax.all_to_all(array.reshape(parts, -1, lanes), axes, split_axis=0, conca...]
    ppermute x8 -> x7, starting transfers between devices: 7.85 us -> 6.07 us  [swap(): return lax.ppermute(array, 'c', [(0, 1), (1, 0)])]
  transfers between devices with their start and end apart: 10 -> 10, of which waited for: 4 -> 8; matrix products, arithmetic and copies ran while one was open for 0% -> 0% of each run, Pallas kernels for 20% -> 8%
where the time goes in v2:
time: 145 us; the launch traced here: 144 us
  blocking collectives  53.9 us (37%)
  Pallas kernels  31.3 us (22%)
  local copies, waits for them, and re-layouts  22.7 us (16%)
  starting transfers between devices  18.9 us (13%)
  waiting for transfers between devices  16.6 us (11%)
    all_to_all x2, blocking collectives, exchange(): lax.all_to_all(array.reshape(parts, -1, lanes), axes, split_axis=0, conca...  53.9 us
    pallas_call x10, Pallas kernels, call(): pl.pallas_call(kernel, out_shape=[pltpu.HBM(*out) if place in hbm_out els...  31.3 us
    unnamed x50, local copies, waits for them, and re-layouts  22.7 us
    all_to_all x3, starting transfers between devices, exchange(): lax.all_to_all(array.reshape(parts, -1, lanes), axes, split_axis=0, conca...  12.9 us
    all_to_all x3, waiting for transfers between devices, exchange(): lax.all_to_all(array.reshape(parts, -1, lanes), axes, split_axis=0, conca...  9.91 us
    ppermute x7, waiting for transfers between devices, swap(): return lax.ppermute(array, 'c', [(0, 1), (1, 0)])  6.71 us
    ppermute x7, starting transfers between devices, swap(): return lax.ppermute(array, 'c', [(0, 1), (1, 0)])  6.07 us
  transfers between devices with their start and end apart: 10, of which 8 were waited for; matrix products, arithmetic and copies ran while one was open for 0% of the time, Pallas kernels for 8%

profile of v2, /device:TPU:1, one launch (start us, length us, event | category | flops | bytes accessed | tf_op | source)
XLA Modules:
  0.0 144.2 jit_solution(17355095542403445522)
XLA Ops:
  0.7 6.3 %shard_map.118 = (bf16[256,2304]{1,0:T(8,128)(2,1)S(1)}, bf16[256,1728]{1,0:T(8,128)(2,1)}, bf16[256,576]{1,0:T(8,128)(2,1)}, bf16[256,1152]{1,0:T(8,128)(2,1)}) custom-call(bf16[256,1152]{1,0:T(8,128)(2,1)} %bitcast.31, bf16[256,1152]{1,0:T(8,128)(2,1)} %bitcast.36, bf16[1728,1152]{1,0:T(8,128)(2,1)} %bitcast.22, bf16[576,1152]{1,0:T(8,128)(2,1)} %bitcast.34), custom_call_target="tpu_custom_call" | custom-call | flops 3000000000 | bytes 9437184 | tf_op jit(solution)/shard_map/pallas_call | solution.py:227
  6.9 27.8 %all_to_all.25 = bf16[32,8,2304]{2,1,0:T(8,128)(2,1)S(1)} all-to-all(bf16[32,8,2304]{2,1,0:T(8,128)(2,1)S(1)} %bitcast.21), channel_id=1, replica_groups=mesh['z'=4,'y'=4,'xl'=2,'xh'=2,'c'=2] {'z','y','xl'}, dimensions={0} | all-to-all | bytes 2359296 | tf_op jit(solution)/shard_map/all_to_all | solution.py:402
  35.8 8.4 %shard_map.119 = (bf16[256,1728]{1,0:T(8,128)(2,1)}, bf16[256,1152]{1,0:T(8,128)(2,1)}, bf16[256,1152]{1,0:T(8,128)(2,1)}, bf16[256,1152]{1,0:T(8,128)(2,1)}, bf16[256,1152]{1,0:T(8,128)(2,1)}) custom-call(bf16[256,2304]{1,0:T(8,128)(2,1)S(1)} %bitcast.30, bf16[1728,1152]{1,0:T(8,128)(2,1)S(1)} %bitcast.33, bf16[576,1152]{1,0:T(8,128)(2,1)S(1)} %bitcast.28), custom_call_target="tpu_custom_call" | custom-call | flops 5000000000 | bytes 9732096 | tf_op jit(solution)/shard_map/pallas_call | solution.py:227
  44.1 4.2 %all-to-all-start.1 = ((bf16[32,8,1728]{2,1,0:T(8,128)(2,1)}), bf16[32,8,1728]{2,1,0:T(8,128)(2,1)S(1)}, u32[]{:S(2)}, u32[]{:S(2)}) async-start(bf16[32,8,1728]{2,1,0:T(8,128)(2,1)} %bitcast.38), calls=%async_computation.1 | async-start | bytes 1835008 | tf_op jit(solution)/shard_map/all_to_all | solution.py:402
  48.3 1.9 %collective-permute-start.2 = (bf16[256,1152]{1,0:T(8,128)(2,1)}, bf16[256,1152]{1,0:T(8,128)(2,1)S(1)}, u32[]{:S(2)}, u32[]{:S(2)}) collective-permute-start(bf16[256,1152]{1,0:T(8,128)(2,1)} %get-tuple-element.35), channel_id=1, source_target_pairs={{0,1},{1,0},{2,3},{3,2},{4,5},{5,4},{6,7},{7,6},{8,9},{9,8},{10,11... | collective-permute-start | bytes 1769480 | tf_op jit(solution)/shard_map/ppermute | solution.py:398
  50.7 1.3 collective-permute-done.2.got_ref
  53.8 1.1 copy-done.20
  54.8 1.1 copy-done.21
  57.0 2.0 %shard_map.120 = bf16[1152,1152]{1,0:T(8,128)(2,1)S(1)} custom-call(bf16[256,1152]{1,0:T(8,128)(2,1)S(1)} %copy-done.20, bf16[256,1152]{1,0:T(8,128)(2,1)S(1)} %collective-permute-done.in_got, bf16[256,1152]{1,0:T(8,128)(2,1)S(1)} %copy-done.21, bf16[256,1152]{1,0:T(8,128)(2,1)S(1)} %collective-permute-done.1.out_got, bf16[256,1152]{1,0:T(8,128)(2,1)S(1)} %copy-done.22, ...), custom_call_target="tpu_custom_call" | custom-call | flops 2000000000 | bytes 6193152 | tf_op jit(solution)/shard_map/pallas_call | solution.py:227
  59.0 1.5 %copy-done.6 = bf16[1152,1152]{1,0:T(8,128)(2,1)} copy-done((bf16[1152,1152]{1,0:T(8,128)(2,1)}, bf16[1152,1152]{1,0:T(8,128)(2,1)S(1)}, u32[]{:S(2)}) %copy-start.6) | copy-done | bytes 2654232
  60.5 2.3 %all-to-all-done.1 = bf16[32,8,1728]{2,1,0:T(8,128)(2,1)S(1)} async-done(((bf16[32,8,1728]{2,1,0:T(8,128)(2,1)}), bf16[32,8,1728]{2,1,0:T(8,128)(2,1)S(1)}, u32[]{:S(2)}, u32[]{:S(2)}) %all-to-all-start.1) | async-done | bytes 884768 | tf_op jit(solution)/shard_map/all_to_all | solution.py:402
  63.7 3.8 %all-to-all-start.2 = ((bf16[4,288,1152]{2,1,0:T(8,128)(2,1)}), bf16[4,288,1152]{2,1,0:T(8,128)(2,1)S(1)}, u32[]{:S(2)}, u32[]{:S(2)}) async-start(bf16[4,288,1152]{2,1,0:T(8,128)(2,1)} %bitcast.26), calls=%async_computation.2 | async-start | bytes 5308416 | tf_op jit(solution)/shard_map/all_to_all | solution.py:402
  67.5 3.1 %collective-permute-start.3 = (bf16[256,1152]{1,0:T(8,128)(2,1)}, bf16[256,1152]{1,0:T(8,128)(2,1)S(1)}, u32[]{:S(2)}, u32[]{:S(2)}) collective-permute-start(bf16[256,1152]{1,0:T(8,128)(2,1)} %get-tuple-element.37.in_own), channel_id=1, source_target_pairs={{0,1},{1,0},{2,3},{3,2},{4,5},{5,4},{6,7},{7,6},{8,9},{9,8},{10,11... | collective-permute-start | bytes 1769480 | tf_op jit(solution)/shard_map/ppermute | solution.py:398
  70.6 1.2 copy-done.4
  71.8 1.3 copy-done.17
  73.1 1.2 copy-done.23
  75.2 3.9 %shard_map.121 = (bf16[256,1152]{1,0:T(8,128)(2,1)S(1)}, bf16[256,1728]{1,0:T(8,128)(2,1)S(1)}, bf16[256,1152]{1,0:T(8,128)(2,1)S(1)}, bf16[256,1152]{1,0:T(8,128)(2,1)S(1)}) custom-call(bf16[256,1152]{1,0:T(8,128)(2,1)S(1)} %bitcast.37, bf16[256,1728]{1,0:T(8,128)(2,1)S(1)} %bitcast.24, bf16[256,1728]{1,0:T(8,128)(2,1)S(1)} %copy-done.23, ...), custom_call_target="tpu_custom_call" | custom-call | flops 3000000000 | bytes 6635520 | tf_op jit(solution)/shard_map/pallas_call | solution.py:227
  80.7 1.5 %collective-permute-done.5.got_ref = bf16[256,1152]{1,0:T(8,128)(2,1)S(1)} collective-permute-done((bf16[256,1152]{1,0:T(8,128)(2,1)S(1)}, bf16[256,1152]{1,0:T(8,128)(2,1)S(1)}, u32[]{:S(2)}, u32[]{:S(2)}) %collective-permute-start.5) | collective-permute-done | bytes 589856 | tf_op jit(solution)/shard_map/ppermute | solution.py:398
  83.0 2.0 %shard_map.122 = bf16[1152,1152]{1,0:T(8,128)(2,1)S(1)} custom-call(bf16[256,1152]{1,0:T(8,128)(2,1)S(1)} %copy-done.19, bf16[256,1152]{1,0:T(8,128)(2,1)S(1)} %collective-permute-done.3.in_got, bf16[256,1152]{1,0:T(8,128)(2,1)S(1)} %get-tuple-element.41.out_own.dhidden_ref, bf16[256,1152]{1,0:T(8,128)(2,1)S(1)} %collective-permute-done.4.out_got, ...), custom_call_target="tpu_custom_call" | custom-call | flops 2000000000 | bytes 6193152 | tf_op jit(solution)/shard_map/pallas_call | solution.py:227
  85.1 1.5 %copy-done.7 = bf16[1152,1152]{1,0:T(8,128)(2,1)} copy-done((bf16[1152,1152]{1,0:T(8,128)(2,1)}, bf16[1152,1152]{1,0:T(8,128)(2,1)S(1)}, u32[]{:S(2)}) %copy-start.7) | copy-done | bytes 2654232
  87.4 4.9 %all-to-all-start.3 = ((bf16[4,288,1152]{2,1,0:T(8,128)(2,1)}), bf16[4,288,1152]{2,1,0:T(8,128)(2,1)}, u32[]{:S(2)}, u32[]{:S(2)}) async-start(bf16[4,288,1152]{2,1,0:T(8,128)(2,1)} %bitcast.27), calls=%async_computation.3 | async-start | bytes 5308416 | tf_op jit(solution)/shard_map/all_to_all | solution.py:402
  92.4 1.3 copy-done.1
  93.6 1.2 copy-done.5
  94.8 1.3 copy-done.9
  96.1 1.5 %shard_map.125 = bf16[256,1152]{1,0:T(8,128)(2,1)} custom-call(bf16[256,2304]{1,0:T(8,128)(2,1)S(1)} %copy-done.1, bf16[256,1728]{1,0:T(8,128)(2,1)S(1)} %bitcast.25, bf16[576,1152]{1,0:T(8,128)(2,1)S(1)} %bitcast.29), custom_call_target="tpu_custom_call" | custom-call | flops 1000000000 | bytes 3981312 | tf_op jit(solution)/shard_map/pallas_call | solution.py:227
  98.5 1.2 copy-done.12
  100.7 2.5 %shard_map.124 = bf16[256,1152]{1,0:T(8,128)(2,1)} custom-call(bf16[256,1152]{1,0:T(8,128)(2,1)S(1)} %bitcast.32, bf16[256,1152]{1,0:T(8,128)(2,1)S(1)} %copy-done.15, bf16[256,1728]{1,0:T(8,128)(2,1)S(1)} %copy-done.12, bf16[1728,1152]{1,0:T(8,128)(2,1)S(1)} %bitcast.23), custom_call_target="tpu_custom_call" | custom-call | flops 1000000000 | bytes 6635520 | tf_op jit(solution)/shard_map/pallas_call | solution.py:227
  103.2 7.6 %all-to-all-done.3 = bf16[4,288,1152]{2,1,0:T(8,128)(2,1)} async-done(((bf16[4,288,1152]{2,1,0:T(8,128)(2,1)}), bf16[4,288,1152]{2,1,0:T(8,128)(2,1)}, u32[]{:S(2)}, u32[]{:S(2)}) %all-to-all-start.3) | async-done | bytes 2654240 | tf_op jit(solution)/shard_map/all_to_all | solution.py:402
  110.8 1.2 copy-done.10
  112.0 3.7 %shard_map.123 = bf16[256,2688]{1,0:T(8,128)(2,1)S(1)} custom-call(bf16[768,576]{1,0:T(8,128)(2,1)S(1)} %copy-done.10, bf16[1152,1152]{1,0:T(8,128)(2,1)S(1)} %bitcast.18, bf16[1152,1152]{1,0:T(8,128)(2,1)} %bitcast.13.space_ref), custom_call_target="tpu_custom_call" | custom-call | flops 1000000000 | bytes 7569408 | tf_op jit(solution)/shard_map/pallas_call | solution.py:227
  115.7 26.1 %all_to_all.26 = bf16[16,16,2688]{2,1,0:T(8,128)(2,1)S(1)} all-to-all(bf16[16,16,2688]{2,1,0:T(8,128)(2,1)S(1)} %bitcast.20), channel_id=1, replica_groups={{0,2,4,6,8,10,12,14,16,18,20,22,24,26,28,30},{32,34,36,38,40,42,44,46,4..., dimensions={0} | all-to-all | bytes 2752512 | tf_op jit(solution)/shard_map/all_to_all | solution.py:402
  142.1 1.4 collective-permute-done.6.got_ref
  (50 shorter events, 12.4 us)
Async XLA Ops:
  0.6 35.1 %copy-start.8 = (bf16[1152,576]{0,1:T(8,128)(2,1)S(1)}, bf16[1152,576]{0,1:T(8,128)(2,1)}, u32[]{:S(2)}) copy-start(bf16[1152,576]{0,1:T(8,128)(2,1)} %param.12) | copy-start | bytes 3981316
  0.6 35.1 %copy-start.16 = (bf16[1152,1728]{0,1:T(8,128)(2,1)S(1)}, bf16[1152,1728]{0,1:T(8,128)(2,1)}, u32[]{:S(2)}) copy-start(bf16[1152,1728]{0,1:T(8,128)(2,1)} %param.11) | copy-start | bytes 11943940
  34.7 1.0 copy-start
  44.1 18.6 %all-to-all-start.1 = ((bf16[32,8,1728]{2,1,0:T(8,128)(2,1)}), bf16[32,8,1728]{2,1,0:T(8,128)(2,1)S(1)}, u32[]{:S(2)}, u32[]{:S(2)}) async-start(bf16[32,8,1728]{2,1,0:T(8,128)(2,1)} %bitcast.38), calls=%async_computation.1 | async-start | bytes 1835008 | tf_op jit(solution)/shard_map/all_to_all | solution.py:402
  48.3 3.7 %collective-permute-start.2 = (bf16[256,1152]{1,0:T(8,128)(2,1)}, bf16[256,1152]{1,0:T(8,128)(2,1)S(1)}, u32[]{:S(2)}, u32[]{:S(2)}) collective-permute-start(bf16[256,1152]{1,0:T(8,128)(2,1)} %get-tuple-element.35), channel_id=1, source_target_pairs={{0,1},{1,0},{2,3},{3,2},{4,5},{5,4},{6,7},{7,6},{8,9},{9,8},{10,11... | collective-permute-start | bytes 1769480 | tf_op jit(solution)/shard_map/ppermute | solution.py:398
  50.2 2.7 %collective-permute-start = (bf16[256,1152]{1,0:T(8,128)(2,1)}, bf16[256,1152]{1,0:T(8,128)(2,1)S(1)}, u32[]{:S(2)}, u32[]{:S(2)}) collective-permute-start(bf16[256,1152]{1,0:T(8,128)(2,1)} %get-tuple-element.32.in_own), channel_id=1, source_target_pairs={{0,1},{1,0},{2,3},{3,2},{4,5},{5,4},{6,7},{7,6},{8,9},{9,8},{10,11... | collective-permute-start | bytes 1769480 | tf_op jit(solution)/shard_map/ppermute | solution.py:398
  50.3 3.4 %collective-permute-start.1 = (bf16[256,1152]{1,0:T(8,128)(2,1)}, bf16[256,1152]{1,0:T(8,128)(2,1)S(1)}, u32[]{:S(2)}, u32[]{:S(2)}) collective-permute-start(bf16[256,1152]{1,0:T(8,128)(2,1)} %get-tuple-element.33.out_own), channel_id=1, source_target_pairs={{0,1},{1,0},{2,3},{3,2},{4,5},{5,4},{6,7},{7,6},{8,9},{9,8},{10,11... | collective-permute-start | bytes 1769480 | tf_op jit(solution)/shard_map/ppermute | solution.py:398
  53.8 1.1 copy-start.20
  54.8 1.1 copy-start.21
  55.9 1.1 copy-start.22
  59.0 1.5 %copy-start.6 = (bf16[1152,1152]{1,0:T(8,128)(2,1)}, bf16[1152,1152]{1,0:T(8,128)(2,1)S(1)}, u32[]{:S(2)}) copy-start(bf16[1152,1152]{1,0:T(8,128)(2,1)S(1)} %shard_map.120) | copy-start | bytes 7962628
  63.7 6.9 %copy-start.18 = (bf16[1,1,256,1152]{3,2,1,0:T(8,128)(2,1)S(1)}, bf16[1,1,256,1152]{3,2,1,0:T(8,128)(2,1)}, u32[]{:S(2)}) copy-start(bf16[1,1,256,1152]{3,2,1,0:T(8,128)(2,1)} %param.8) | copy-start | bytes 1769476
  63.7 23.7 %all-to-all-start.2 = ((bf16[4,288,1152]{2,1,0:T(8,128)(2,1)}), bf16[4,288,1152]{2,1,0:T(8,128)(2,1)S(1)}, u32[]{:S(2)}, u32[]{:S(2)}) async-start(bf16[4,288,1152]{2,1,0:T(8,128)(2,1)} %bitcast.26), calls=%async_computation.2 | async-start | bytes 5308416 | tf_op jit(solution)/shard_map/all_to_all | solution.py:402
  67.5 13.2 %collective-permute-start.3 = (bf16[256,1152]{1,0:T(8,128)(2,1)}, bf16[256,1152]{1,0:T(8,128)(2,1)S(1)}, u32[]{:S(2)}, u32[]{:S(2)}) collective-permute-start(bf16[256,1152]{1,0:T(8,128)(2,1)} %get-tuple-element.37.in_own), channel_id=1, source_target_pairs={{0,1},{1,0},{2,3},{3,2},{4,5},{5,4},{6,7},{7,6},{8,9},{9,8},{10,11... | collective-permute-start | bytes 1769480 | tf_op jit(solution)/shard_map/ppermute | solution.py:398
  70.6 1.2 copy-start.4
  71.8 1.3 copy-start.17
  73.1 1.2 copy-start.23
  75.2 7.8 %copy-start.19 = (bf16[256,1152]{1,0:T(8,128)(2,1)S(1)}, bf16[256,1152]{1,0:T(8,128)(2,1)}, u32[]{:S(2)}) copy-start(bf16[256,1152]{1,0:T(8,128)(2,1)} %get-tuple-element.37.in_own) | copy-start | bytes 1769476
  79.2 1.0 copy-start.11
  80.2 2.0 %collective-permute-start.5 = (bf16[256,1152]{1,0:T(8,128)(2,1)S(1)}, bf16[256,1152]{1,0:T(8,128)(2,1)S(1)}, u32[]{:S(2)}, u32[]{:S(2)}) collective-permute-start(bf16[256,1152]{1,0:T(8,128)(2,1)S(1)} %get-tuple-element.43), channel_id=1, source_target_pairs={{0,1},{1,0},{2,3},{3,2},{4,5},{5,4},{6,7},{7,6},{8,9},{9,8},{10,11... | collective-permute-start | bytes 1769480 | tf_op jit(solution)/shard_map/ppermute | solution.py:398
  80.2 2.8 %collective-permute-start.4 = (bf16[256,1152]{1,0:T(8,128)(2,1)S(1)}, bf16[256,1152]{1,0:T(8,128)(2,1)S(1)}, u32[]{:S(2)}, u32[]{:S(2)}) collective-permute-start(bf16[256,1152]{1,0:T(8,128)(2,1)S(1)} %get-tuple-element.41.out_own.dhidden_ref), channel_id=1, source_target_pairs={{0,1},{1,0},{2,3},{3,2},{4,5},{5,4},{6,7},{7,6},{8,9},{9,8},{10,11... | collective-permute-start | bytes 1769480 | tf_op jit(solution)/shard_map/ppermute | solution.py:398
  85.1 1.5 %copy-start.7 = (bf16[1152,1152]{1,0:T(8,128)(2,1)}, bf16[1152,1152]{1,0:T(8,128)(2,1)S(1)}, u32[]{:S(2)}) copy-start(bf16[1152,1152]{1,0:T(8,128)(2,1)S(1)} %shard_map.122) | copy-start | bytes 7962628
  87.4 10.2 %copy-start.13 = (bf16[1,1,256,1152]{3,2,1,0:T(8,128)(2,1)S(1)}, bf16[1,1,256,1152]{3,2,1,0:T(8,128)(2,1)}, u32[]{:S(2)}) copy-start(bf16[1,1,256,1152]{3,2,1,0:T(8,128)(2,1)} %param.7) | copy-start | bytes 1769476
  87.4 23.4 %all-to-all-start.3 = ((bf16[4,288,1152]{2,1,0:T(8,128)(2,1)}), bf16[4,288,1152]{2,1,0:T(8,128)(2,1)}, u32[]{:S(2)}, u32[]{:S(2)}) async-start(bf16[4,288,1152]{2,1,0:T(8,128)(2,1)} %bitcast.27), calls=%async_computation.3 | async-start | bytes 5308416 | tf_op jit(solution)/shard_map/all_to_all | solution.py:402
  92.3 1.3 copy-start.1
  93.6 1.2 copy-start.5
  94.8 1.3 copy-start.9
  96.1 2.3 %copy-start.2 = (bf16[1152,1728]{0,1:T(8,128)(2,1)S(1)}, bf16[1152,1728]{0,1:T(8,128)(2,1)}, u32[]{:S(2)}) copy-start(bf16[1152,1728]{0,1:T(8,128)(2,1)} %param.9) | copy-start | bytes 11943940
  98.5 1.2 copy-start.12
  99.6 1.1 copy-start.15
  110.8 1.2 copy-start.10
  142.0 1.5 %collective-permute-start.6 = (f32[2,9,1152]{2,1,0:T(8,128)S(1)}, f32[2,9,1152]{2,1,0:T(8,128)S(1)}, u32[]{:S(2)}, u32[]{:S(2)}) collective-permute-start(f32[2,9,1152]{2,1,0:T(8,128)S(1)} %get-tuple-element.49), channel_id=1, source_target_pairs={{0,1},{1,0},{2,3},{3,2},{4,5},{5,4},{6,7},{7,6},{8,9},{9,8},{10,11... | collective-permute-start | bytes 248840 | tf_op jit(solution)/shard_map/ppermute | solution.py:398
  (3 other events, 2.7 us)

commit v3 on v2

--- a/solution.py
+++ b/solution.py
@@ -197,23 +197,64 @@
         copy.wait()
 
 
+def start_all(copies):
+    for copy in copies:
+        copy.start()
+    return copies
+
+
+def load_all(pairs, sems, first=0):
+    return start_all(
+        [pltpu.make_async_copy(a, b, sems.at[first + place]) for place, (a, b) in enumerate(pairs)]
+    )
+
+
 def space_backward(
-    cot_ref, recv_ref, qkv_ref, attn_ref, w_out_ref, dhidden_ref, dqkv_ref, keep_ref, send_ref
+    cot_hbm, recv_hbm, w_out_hbm, qkv_hbm, attn_hbm, dhidden_hbm, dqkv_hbm, keep_ref, send_ref,
+    cot_ref, dres_ref, w_out_ref, qkv_ref, attn_ref, dhidden_ref, dqkv_ref, sems,
 ):
     width = cot_ref.shape[1]
-    dhidden = cot_ref[...] + recv_ref[:, :width]
+    loads = load_all(
+        [
+            (cot_hbm, cot_ref),
+            (recv_hbm.at[:, pl.ds(0, width)], dres_ref),
+            (w_out_hbm, w_out_ref),
+            (qkv_hbm, qkv_ref),
+            (attn_hbm, attn_ref),
+        ],
+        sems,
+    )
+    loads[0].wait()
+    loads[1].wait()
+    dhidden = cot_ref[...] + dres_ref[...]
     dhidden_ref[...] = dhidden
+    stores = load_all([(dhidden_ref, dhidden_hbm)], sems, 5)
+    loads[2].wait()
     dattn = dot_nt(dhidden, w_out_ref[...]).astype(BF16)
+    loads[3].wait()
     query, keys, values = split_qkv(qkv_ref[...])
     dqkv = attention_back(query, keys, values, dattn, None, False)[1]
     dqkv_ref[...] = dqkv
+    stores += load_all([(dqkv_ref, dqkv_hbm)], sems, 6)
+    loads[4].wait()
     pair_up(lax.axis_index("c"), dqkv, attn_ref[...], keep_ref, send_ref)
-
-
-def space_finish(x_ref, dhidden_ref, dqkv_ref, w_qkv_ref, grad_ref):
+    for store in stores:
+        store.wait()
+
+
+def space_finish(
+    x_hbm, dhidden_hbm, dqkv_hbm, w_qkv_hbm, grad_ref, x_ref, dhidden_ref, dqkv_ref, w_qkv_ref, sems
+):
+    loads = load_all(
+        [(x_hbm, x_ref), (dqkv_hbm, dqkv_ref), (w_qkv_hbm, w_qkv_ref), (dhidden_hbm, dhidden_ref)], sems
+    )
+    loads[0].wait()
     normed, rate = norm_parts(x_ref[...].astype(F32))
+    loads[1].wait()
+    loads[2].wait()
     dnormed = dot_nn(dqkv_ref[...], w_qkv_ref[...]).astype(BF16).astype(F32)
     dres = norm_back(dnormed, normed, rate).astype(BF16)
+    loads[3].wait()
     grad_ref[...] = dhidden_ref[...] + dres
 
 
@@ -234,25 +275,40 @@
         out_specs=[hbm if place in hbm_out else vmem for place in range(len(outs))],
         scratch_shapes=list(scratch),
         compiler_params=pltpu.CompilerParams(vmem_limit_bytes=grant * 1024 * 1024),
-        cost_estimate=pl.CostEstimate(flops=flops, bytes_accessed=size, transcendentals=0),
+        cost_estimate=pl.CostEstimate(flops=flops // 1000, bytes_accessed=size // 1000, transcendentals=0),
     )(*args)
 
 
-def chunk_rows(chunks, rows, parts):
-    table = np.zeros((3, chunks, parts, 8, parts, chunks * rows), np.float32)
+def chunk_rows(chunks, rows, part):
+    table = np.zeros((3, chunks, 2, 8, chunks * rows), np.float32)
     for chunk in range(chunks):
-        for part in range(parts):
-            for lane in range(8):
-                table[0, chunk, part, lane, part, chunk * rows + lane] = 1
-                table[1, chunk, part, lane, part, chunk * rows + 8 + lane] = 1
-            for lane in range(6):
-                table[2, chunk, part, lane, part, chunk * rows + 16 + lane % 2] = 1
-    return table.reshape(3 * chunks * parts * 8, parts * chunks * rows).astype(jnp.bfloat16)
-
-
-def mix_out(send_ref, recv_ref, w_out_ref, mixed_ref):
-    width = w_out_ref.shape[1]
-    mixed = send_ref[:, :width].astype(F32) + dot_nn(recv_ref[:, width:], w_out_ref[...])
+        for lane in range(8):
+            table[0, chunk, part, lane, chunk * rows + lane] = 1
+            table[1, chunk, part, lane, chunk * rows + 8 + lane] = 1
+        for lane in range(6):
+            table[2, chunk, part, lane, chunk * rows + 16 + lane % 2] = 1
+    return table.reshape(3 * chunks * 16, chunks * rows).astype(jnp.bfloat16)
+
+
+def mix_out(
+    x_hbm, attn_hbm, w_space_hbm, recv_hbm, w_time_hbm, mixed_ref,
+    x_ref, attn_ref, w_space_ref, time_ref, w_time_ref, sems,
+):
+    width = x_ref.shape[1]
+    loads = load_all(
+        [
+            (x_hbm, x_ref),
+            (attn_hbm, attn_ref),
+            (w_space_hbm, w_space_ref),
+            (recv_hbm.at[:, pl.ds(width, HK)], time_ref),
+            (w_time_hbm, w_time_ref),
+        ],
+        sems,
+    )
+    for load in loads:
+        load.wait()
+    hidden = (x_ref[...].astype(F32) + dot_nn(attn_ref[...], w_space_ref[...])).astype(BF16)
+    mixed = hidden.astype(F32) + dot_nn(time_ref[...], w_time_ref[...])
     mixed_ref[...] = mixed.astype(BF16)
 
 
@@ -263,65 +319,71 @@
     send_ref[...] = jnp.where(core == 0, second, first)
 
 
-def weight_terms(lines, in_own, in_got, out_own, out_got, own_ref, got_ref, term_ref, total_ref):
+def weight_terms(lines, in_own, in_got, out_own, out_got, own_ref, got_ref, *refs):
+    parts, total_ref = refs[:-1], refs[-1]
     width = own_ref.shape[1]
     low, high = HK // LANES * LANES, -(-HK // LANES) * LANES
-    step = width // 3
+    size = width // 3
     rows = width // (lines * lines)
     core = lax.axis_index("c")
 
     def product(one, two, left, right):
         return dot_tn(one, own_ref[:, left:right]) + dot_tn(two, got_ref[:, left:right])
 
-    def place(order):
-        for first in range(0, lines * lines, 2):
-            pair = [total_ref[pl.ds(order(block) * rows, rows), :] for block in (first, first + 1)]
-            term_ref[pl.ds(first * rows, 2 * rows), :] = jnp.concatenate(pair, axis=0).astype(BF16)
+    def place(me, order):
+        for step, part_ref in enumerate(parts):
+            line = lax.rem(me + step, lines)
+            blocks = []
+            for block in range(lines):
+                start = pl.multiple_of(order(block, line) * rows, 8)
+                blocks.append(total_ref[pl.ds(start, rows), :])
+            part_ref[...] = jnp.concatenate(blocks, axis=0).astype(BF16)
 
     @pl.when(core == 0)
     def _():
-        for start in range(0, width, step):
-            block = slice(start, start + step)
+        for start in range(0, width, size):
+            block = slice(start, start + size)
             total_ref[block, :] = product(in_own[:, block], in_got[:, block], 0, width)
-        place(lambda block: block)
+        place(lax.axis_index("z"), lambda block, line: line * lines + block)
 
     @pl.when(core != 0)
     def _():
-        for start in range(0, width, step):
-            block = slice(start, start + step)
+        for start in range(0, width, size):
+            block = slice(start, start + size)
             left = product(in_own[:, block], in_got[:, block], 0, high)
             right = product(out_own[:, block], out_got[:, block], low, width)
-            lane = low + lax.broadcasted_iota(jnp.int32, (step, high - low), 1)
+            lane = low + lax.broadcasted_iota(jnp.int32, (size, high - low), 1)
             total_ref[block, :low] = left[:, :low]
             total_ref[block, low:high] = jnp.where(lane < HK, left[:, low:], right[:, : high - low])
             total_ref[block, high:] = right[:, high - low :]
-        place(lambda block: block % lines * lines + block // lines)
-
-
-def add_lines(lines, table_ref, time_ref, space_ref, chunk_ref):
-    width = time_ref.shape[1]
+        place(lax.axis_index("y"), lambda block, line: block * lines + line)
+
+
+def add_lines(table_ref, *refs):
+    got, chunk_ref = refs[:4], refs[-1]
+    width = got[0].shape[1]
     third = width // 3
-    sums = []
-    for ref in (time_ref, space_ref):
-        rows = ref.shape[0] // lines
-        total = ref[:rows, :].astype(F32)
-        for line in range(1, lines):
-            total = total + ref[line * rows : (line + 1) * rows, :].astype(F32)
-        sums.append(total.astype(BF16))
-    sums = jnp.concatenate(sums, axis=0)
+    total = got[0][...].astype(F32)
+    for ref in got[1:4]:
+        total = total + ref[...].astype(F32)
+    total = total.astype(BF16)
     block = table_ref.shape[0] // 3
     for part in range(3):
-        whole = dot_nn(table_ref[part * block : (part + 1) * block, :], sums)
-        if part < 2:
-            chunk_ref[:, part * width : (part + 1) * width] = whole.astype(BF16)
-        else:
+        whole = dot_nn(table_ref[part * block : (part + 1) * block, :], total)
+        place = slice(part * width, min((part + 1) * width, 2 * width + third))
+        if part == 2:
             row = lax.rem(lax.broadcasted_iota(jnp.int32, (block, third), 0), 8)
-            rest = jnp.where(
+            whole = jnp.where(
                 row < 2,
                 whole[:, :third],
                 jnp.where(row < 4, whole[:, third : 2 * third], whole[:, 2 * third :]),
             )
-            chunk_ref[:, 2 * width :] = rest.astype(BF16)
+        whole = whole.astype(BF16)
+        if len(refs) == 6:
+            other = refs[4][:, place]
+            row = lax.rem(lax.broadcasted_iota(jnp.int32, whole.shape, 0), 16)
+            whole = jnp.where(row < 8, other, whole)
+        chunk_ref[:, place] = whole
 
 
 def add_chunks(scale, chunk_ref, keep_ref, send_ref):
@@ -365,10 +427,14 @@
     return ((z * SIDE + y) * SIDE + x) * 2 + core
 
 
-def line_groups():
-    side = range(SIDE)
-    groups = [[device(z, y, x, 0) for z in side] for y in side for x in side]
-    return groups + [[device(z, y, x, 1) for y in side] for z in side for x in side]
+def line_pairs(step):
+    pairs = []
+    for z in range(SIDE):
+        for y in range(SIDE):
+            for x in range(SIDE):
+                pairs.append((device(z, y, x, 0), device((z + step) % SIDE, y, x, 0)))
+                pairs.append((device(z, y, x, 1), device(z, (y + step) % SIDE, x, 1)))
+    return pairs
 
 
 def plane_groups():
@@ -390,9 +456,9 @@
     top = cotangent.reshape(count, width)
     plane = SIDE * SIDE
     rows = width // (plane * SIDE)
-    table = jnp.asarray(chunk_rows(plane, rows, 2))
+    tables = [jnp.asarray(chunk_rows(plane, rows, part)) for part in range(2)]
     half = ((count, width), BF16)
-    term = ((width, width), BF16)
+    quarter = ((width // SIDE, width), BF16)
 
     def swap(array):
         return lax.ppermute(array, "c", [(0, 1), (1, 0)])
@@ -412,12 +478,17 @@
     def terms(*args):
         return call(
             functools.partial(weight_terms, SIDE),
-            [term],
+            [quarter] * SIDE,
             *args,
             flops=2 * 10**9,
             scratch=[pltpu.VMEM((width, width), F32)],
             grant=16,
-        )[0]
+        )
+
+    def along_lines(parts):
+        return [parts[0]] + [
+            lax.ppermute(part, ALL, line_pairs(step)) for step, part in enumerate(parts) if step
+        ]
 
     def buffers(*shapes):
         return [pltpu.VMEM(*shape) for shape in shapes]
@@ -451,25 +522,38 @@
     )
     recv = exchange(back, SEQ, frames)
     recv, terms_time = lax.optimization_barrier((recv, terms_time))
-    got_time = exchange(terms_time, ALL, SIDE, line_groups())
+    got_time = along_lines(terms_time)
+    wide = ((HK, width), BF16)
     dhidden, dqkv_space, keep, give = call(
         space_backward, [half, qkv, half, half],
-        top, recv, qkv_space, attn_space, w_out_space, flops=3 * 10**9,
+        top, recv, w_out_space, qkv_space, attn_space,
+        flops=3 * 10**9,
+        hbm_in=5,
+        hbm_out=(0, 1),
+        scratch=buffers(half, half, wide, qkv, mix, half, qkv) + [pltpu.SemaphoreType.DMA((7,))],
+        grant=20,
     )
     terms_space = terms(
         normed_space, swap(normed_space), dhidden, swap(dhidden), keep, swap(give)
     )
-    got_space = exchange(terms_space, ALL, SIDE, line_groups())
+    got_space = along_lines(terms_space)
     grad_clips = call(
-        space_finish, [half], x, dhidden, dqkv_space, w_qkv_space, flops=10**9
+        space_finish, [half], x, dhidden, dqkv_space, w_qkv_space,
+        flops=10**9,
+        hbm_in=4,
+        scratch=buffers(half, half, qkv, ((qkv_cols, width), BF16)) + [pltpu.SemaphoreType.DMA((4,))],
+        grant=16,
     )[0]
-    mixed = call(mix_out, [half], send, recv, w_out_time, flops=10**9)[0]
-    chunks = call(
-        functools.partial(add_lines, SIDE),
-        [((plane * 16, 2 * width + width // 3), BF16)],
-        table, got_time, got_space,
+    mixed = call(
+        mix_out, [half], x, attn_space, w_out_space, recv, w_out_time,
         flops=10**9,
+        hbm_in=5,
+        scratch=buffers(half, mix, wide, mix, wide) + [pltpu.SemaphoreType.DMA((5,))],
+        grant=16,
     )[0]
+    chunk = [((plane * 16, 2 * width + width // 3), BF16)]
+    chunks = call(add_lines, chunk, tables[0], *got_time, flops=10**9)[0]
+    chunks = call(add_lines, chunk, tables[1], *got_space, chunks, flops=10**9)[0]
     chunks, grad_clips, mixed = lax.optimization_barrier((chunks, grad_clips, mixed))
     chunks = exchange(chunks, ALL, plane, plane_groups())
     own_rows = ((2, rows // 2, width), F32)

time: 145 us -> 129 us (0.89)
  local copies, waits for them, and re-layouts: 22.7 us -> 3.64 us
  Pallas kernels: 31.3 us -> 40.1 us
  waiting for transfers between devices: 16.6 us -> 14.3 us
  starting transfers between devices: 18.9 us -> 16.9 us
    unnamed x50 -> x28, local copies, waits for them, and re-layouts: 22.7 us -> 3.64 us
    pallas_call x10 -> x11, Pallas kernels: 31.3 us -> 40.1 us  [call(): pl.pallas_call(kernel, out_shape=[pltpu.HBM(*out) if place in hbm_out els...]
    all_to_all x3 -> x1, starting transfers between devices: 12.9 us -> 4.78 us  [exchange(): lax.all_to_all(array.reshape(parts, -1, lanes), axes, split_axis=0, conca...]
    all_to_all x3 -> x1, waiting for transfers between devices: 9.91 us -> 3.26 us  [exchange(): lax.all_to_all(array.reshape(parts, -1, lanes), axes, split_axis=0, conca...]
    ppermute x0 -> x6, waiting for transfers between devices: none -> 5.93 us  [along_lines(): lax.ppermute(part, ALL, line_pairs(step))]
    ppermute x0 -> x6, starting transfers between devices: none -> 5.34 us  [along_lines(): lax.ppermute(part, ALL, line_pairs(step))]
    ppermute x7, waiting for transfers between devices: 6.71 us -> 5.15 us  [swap(): return lax.ppermute(array, 'c', [(0, 1), (1, 0)])]
  transfers between devices with their start and end apart: 10 -> 14, of which waited for: 8 -> 8; matrix products, arithmetic and copies ran while one was open for 0% -> 0% of each run, Pallas kernels for 8% -> 18%
where the time goes in v3:
time: 129 us
  blocking collectives  53 us (41%)
  Pallas kernels  40.1 us (31%)
  starting transfers between devices  16.9 us (13%)
  waiting for transfers between devices  14.3 us (11%)
  local copies, waits for them, and re-layouts  3.64 us (3%)
    all_to_all x2, blocking collectives, exchange(): lax.all_to_all(array.reshape(parts, -1, lanes), axes, split_axis=0, conca...  53 us
    pallas_call x11, Pallas kernels, call(): pl.pallas_call(kernel, out_shape=[pltpu.HBM(*out) if place in hbm_out els...  40.1 us
    ppermute x7, starting transfers between devices, swap(): return lax.ppermute(array, 'c', [(0, 1), (1, 0)])  6.82 us
    ppermute x6, waiting for transfers between devices, along_lines(): lax.ppermute(part, ALL, line_pairs(step))  5.93 us
    ppermute x6, starting transfers between devices, along_lines(): lax.ppermute(part, ALL, line_pairs(step))  5.34 us
    ppermute x7, waiting for transfers between devices, swap(): return lax.ppermute(array, 'c', [(0, 1), (1, 0)])  5.15 us
    all_to_all x1, starting transfers between devices, exchange(): lax.all_to_all(array.reshape(parts, -1, lanes), axes, split_axis=0, conca...  4.78 us
    unnamed x28, local copies, waits for them, and re-layouts  3.64 us
  transfers between devices with their start and end apart: 14, of which 8 were waited for; matrix products, arithmetic and copies ran while one was open for 0% of the time, Pallas kernels for 18%

profile of v3, /device:TPU:1, one launch (start us, length us, event | category | flops | bytes accessed | tf_op | source)
XLA Modules:
  0.0 128.9 jit_solution(16199265674638470962)
XLA Ops:
  0.6 6.2 %shard_map.127 = (bf16[256,2304]{1,0:T(8,128)(2,1)S(1)}, bf16[256,1728]{1,0:T(8,128)(2,1)}, bf16[256,576]{1,0:T(8,128)(2,1)}, bf16[256,1152]{1,0:T(8,128)(2,1)}) custom-call(bf16[256,1152]{1,0:T(8,128)(2,1)} %bitcast.26, bf16[256,1152]{1,0:T(8,128)(2,1)} %bitcast.29, bf16[1728,1152]{1,0:T(8,128)(2,1)} %bitcast.21, bf16[576,1152]{1,0:T(8,128)(2,1)} %bitcast.23), custom_call_target="tpu_custom_call" | custom-call | flops 3000000 | bytes 9437 | tf_op jit(solution)/shard_map/pallas_call | solution.py:268
  6.9 27.9 %all_to_all.15 = bf16[32,8,2304]{2,1,0:T(8,128)(2,1)S(1)} all-to-all(bf16[32,8,2304]{2,1,0:T(8,128)(2,1)S(1)} %bitcast.20), channel_id=1, replica_groups=mesh['z'=4,'y'=4,'xl'=2,'xh'=2,'c'=2] {'z','y','xl'}, dimensions={0} | all-to-all | bytes 2359296 | tf_op jit(solution)/shard_map/all_to_all | solution.py:468
  34.8 8.4 %shard_map.128 = (bf16[256,1728]{1,0:T(8,128)(2,1)}, bf16[256,1152]{1,0:T(8,128)(2,1)}, bf16[256,1152]{1,0:T(8,128)(2,1)}, bf16[256,1152]{1,0:T(8,128)(2,1)}, bf16[256,1152]{1,0:T(8,128)(2,1)}) custom-call(bf16[256,2304]{1,0:T(8,128)(2,1)S(1)} %bitcast.18, bf16[1728,1152]{1,0:T(8,128)(2,1)S(1)} %bitcast.19, bf16[576,1152]{1,0:T(8,128)(2,1)S(1)} %bitcast.17), custom_call_target="tpu_custom_call" | custom-call | flops 5000000 | bytes 9732 | tf_op jit(solution)/shard_map/pallas_call | solution.py:268
  43.3 4.8 %all-to-all-start.1 = ((bf16[32,8,1728]{2,1,0:T(8,128)(2,1)}), bf16[32,8,1728]{2,1,0:T(8,128)(2,1)}, u32[]{:S(2)}, u32[]{:S(2)}) async-start(bf16[32,8,1728]{2,1,0:T(8,128)(2,1)} %bitcast.31), calls=%async_computation.1 | async-start | bytes 1835008 | tf_op jit(solution)/shard_map/all_to_all | solution.py:468
  48.1 2.1 %collective-permute-start.1 = (bf16[256,1152]{1,0:T(8,128)(2,1)S(1)}, bf16[256,1152]{1,0:T(8,128)(2,1)S(1)}, u32[]{:S(2)}, u32[]{:S(2)}) collective-permute-start(bf16[256,1152]{1,0:T(8,128)(2,1)S(1)} %copy-done.6), channel_id=1, source_target_pairs={{0,1},{1,0},{2,3},{3,2},{4,5},{5,4},{6,7},{7,6},{8,9},{9,8},{10,11... | collective-permute-start | bytes 1769480 | tf_op jit(solution)/shard_map/ppermute | solution.py:464
  50.3 0.4 collective-permute-start.3
  50.7 1.1 collective-permute-done.1.in_got
  51.8 1.7 %collective-permute-done.2.out_got = bf16[256,1152]{1,0:T(8,128)(2,1)S(1)} collective-permute-done((bf16[256,1152]{1,0:T(8,128)(2,1)S(1)}, bf16[256,1152]{1,0:T(8,128)(2,1)S(1)}, u32[]{:S(2)}, u32[]{:S(2)}) %collective-permute-start.2) | collective-permute-done | bytes 589856 | tf_op jit(solution)/shard_map/ppermute | solution.py:464
  53.7 2.8 %shard_map.129 = (bf16[288,1152]{1,0:T(8,128)(2,1)S(1)}, bf16[288,1152]{1,0:T(8,128)(2,1)S(1)}, bf16[288,1152]{1,0:T(8,128)(2,1)S(1)}, bf16[288,1152]{1,0:T(8,128)(2,1)S(1)}) custom-call(bf16[256,1152]{1,0:T(8,128)(2,1)S(1)} %copy-done.6, bf16[256,1152]{1,0:T(8,128)(2,1)S(1)} %collective-permute-done.1.in_got, bf16[256,1152]{1,0:T(8,128)(2,1)S(1)} %copy-done.7, ...), custom_call_target="tpu_custom_call" | custom-call | flops 2000000 | bytes 6193 | tf_op jit(solution)/shard_map/pallas_call | solution.py:268
  56.5 0.8 copy-done.9
  57.4 0.9 copy-done.11
  58.2 0.8 copy-done.13
  59.1 3.3 %all-to-all-done.1 = bf16[32,8,1728]{2,1,0:T(8,128)(2,1)} async-done(((bf16[32,8,1728]{2,1,0:T(8,128)(2,1)}), bf16[32,8,1728]{2,1,0:T(8,128)(2,1)}, u32[]{:S(2)}, u32[]{:S(2)}) %all-to-all-start.1) | async-done | bytes 884768 | tf_op jit(solution)/shard_map/all_to_all | solution.py:468
  62.3 0.5 collective-permute-start.10
  62.8 3.4 %collective-permute-start = (bf16[256,1152]{1,0:T(8,128)(2,1)S(1)}, bf16[256,1152]{1,0:T(8,128)(2,1)S(1)}, u32[]{:S(2)}, u32[]{:S(2)}) collective-permute-start(bf16[256,1152]{1,0:T(8,128)(2,1)S(1)} %copy-done.5), channel_id=1, source_target_pairs={{0,1},{1,0},{2,3},{3,2},{4,5},{5,4},{6,7},{7,6},{8,9},{9,8},{10,11... | collective-permute-start | bytes 1769480 | tf_op jit(solution)/shard_map/ppermute | solution.py:464
  66.2 7.1 %shard_map.130 = (bf16[256,1152]{1,0:T(8,128)(2,1)}, bf16[256,1728]{1,0:T(8,128)(2,1)}, bf16[256,1152]{1,0:T(8,128)(2,1)S(1)}, bf16[256,1152]{1,0:T(8,128)(2,1)S(1)}) custom-call(bf16[256,1152]{1,0:T(8,128)(2,1)} %bitcast.30, bf16[256,1728]{1,0:T(8,128)(2,1)} %bitcast.9.recv_hbm, bf16[576,1152]{1,0:T(8,128)(2,1)} %bitcast.24, ...), custom_call_target="tpu_custom_call" | custom-call | flops 3000000 | bytes 6635 | tf_op jit(solution)/shard_map/pallas_call | solution.py:268
  73.5 0.5 collective-permute-start.5
  74.0 0.9 collective-permute-start.11
  74.9 0.6 collective-permute-start.9
  75.7 0.6 collective-permute-done.5.got_ref
  76.3 1.1 copy-done.2
  77.4 2.8 %shard_map.131 = (bf16[288,1152]{1,0:T(8,128)(2,1)S(1)}, bf16[288,1152]{1,0:T(8,128)(2,1)S(1)}, bf16[288,1152]{1,0:T(8,128)(2,1)S(1)}, bf16[288,1152]{1,0:T(8,128)(2,1)S(1)}) custom-call(bf16[256,1152]{1,0:T(8,128)(2,1)S(1)} %copy-done.5, bf16[256,1152]{1,0:T(8,128)(2,1)S(1)} %collective-permute-done.in_got, bf16[256,1152]{1,0:T(8,128)(2,1)S(1)} %copy-done.2, ...), custom_call_target="tpu_custom_call" | custom-call | flops 2000000 | bytes 6193 | tf_op jit(solution)/shard_map/pallas_call | solution.py:268
  80.5 2.2 %collective-permute-start.7 = (bf16[288,1152]{1,0:T(8,128)(2,1)S(1)}, bf16[288,1152]{1,0:T(8,128)(2,1)S(1)}, u32[]{:S(2)}, u32[]{:S(2)}) collective-permute-start(bf16[288,1152]{1,0:T(8,128)(2,1)S(1)} %get-tuple-element.60), channel_id=1, source_target_pairs={{0,64},{1,17},{2,66},{3,19},{4,68},{5,21},{6,70},{7,23},{8,72},{9,... | collective-permute-start | bytes 1990664 | tf_op jit(solution)/shard_map/ppermute | solution.py:490
  82.7 0.9 collective-permute-start.8
  83.6 4.1 %shard_map.135 = bf16[256,1152]{1,0:T(8,128)(2,1)} custom-call(bf16[256,1152]{1,0:T(8,128)(2,1)} %bitcast.27, bf16[256,576]{1,0:T(8,128)(2,1)} %get-tuple-element.54.attn_hbm, bf16[576,1152]{1,0:T(8,128)(2,1)} %bitcast.25, bf16[256,1728]{1,0:T(8,128)(2,1)} %bitcast.9.recv_hbm, bf16[576,1152]{1,0:T(8,128)(2,1)} %bitcast.16), custom_call_target="tpu_custom_call" | custom-call | flops 1000000 | bytes 5013 | tf_op jit(solution)/shard_map/pallas_call | solution.py:268
  87.7 5.2 %shard_map.134 = bf16[256,1152]{1,0:T(8,128)(2,1)} custom-call(bf16[256,1152]{1,0:T(8,128)(2,1)} %bitcast.28, bf16[256,1152]{1,0:T(8,128)(2,1)} %get-tuple-element.55.out_own.dhidden_hbm, bf16[256,1728]{1,0:T(8,128)(2,1)} %get-tuple-element.66.dqkv_hbm, bf16[1728,1152]{1,0:T(8,128)(2,1)} %bitcast.22), custom_call_target="tpu_custom_call" | custom-call | flops 1000000 | bytes 6635 | tf_op jit(solution)/shard_map/pallas_call | solution.py:268
  92.9 1.2 shard_map.132.refs_4_
  94.2 5.9 %collective-permute-done.6.refs_1_ = bf16[288,1152]{1,0:T(8,128)(2,1)S(1)} collective-permute-done((bf16[288,1152]{1,0:T(8,128)(2,1)S(1)}, bf16[288,1152]{1,0:T(8,128)(2,1)S(1)}, u32[]{:S(2)}, u32[]{:S(2)}) %collective-permute-start.6) | collective-permute-done | bytes 663584 | tf_op jit(solution)/shard_map/ppermute | solution.py:490
  100.1 1.3 shard_map.133
  101.4 25.1 %all_to_all.16 = bf16[16,16,2688]{2,1,0:T(8,128)(2,1)S(1)} all-to-all(bf16[16,16,2688]{2,1,0:T(8,128)(2,1)S(1)} %bitcast.14), channel_id=1, replica_groups={{0,2,4,6,8,10,12,14,16,18,20,22,24,26,28,30},{32,34,36,38,40,42,44,46,4..., dimensions={0} | all-to-all | bytes 2752512 | tf_op jit(solution)/shard_map/all_to_all | solution.py:468
  126.8 1.3 collective-permute-done.12.got_ref
  128.1 0.7 shard_map.137
  (37 shorter events, 1.4 us)
Async XLA Ops:
  0.6 34.2 %copy-start.1 = (bf16[1152,1728]{0,1:T(8,128)(2,1)S(1)}, bf16[1152,1728]{0,1:T(8,128)(2,1)}, u32[]{:S(2)}) copy-start(bf16[1152,1728]{0,1:T(8,128)(2,1)} %param.12) | copy-start | bytes 11943940
  6.9 27.9 %copy-start = (bf16[1152,576]{0,1:T(8,128)(2,1)S(1)}, bf16[1152,576]{0,1:T(8,128)(2,1)}, u32[]{:S(2)}) copy-start(bf16[1152,576]{0,1:T(8,128)(2,1)} %param.13) | copy-start | bytes 3981316
  43.2 4.8 %copy-start.6 = (bf16[256,1152]{1,0:T(8,128)(2,1)S(1)}, bf16[256,1152]{1,0:T(8,128)(2,1)}, u32[]{:S(2)}) copy-start(bf16[256,1152]{1,0:T(8,128)(2,1)} %get-tuple-element.44.in_own) | copy-start | bytes 1769476
  43.2 7.0 %copy-start.7 = (bf16[256,1152]{1,0:T(8,128)(2,1)S(1)}, bf16[256,1152]{1,0:T(8,128)(2,1)}, u32[]{:S(2)}) copy-start(bf16[256,1152]{1,0:T(8,128)(2,1)} %get-tuple-element.45.out_own) | copy-start | bytes 1769476
  43.3 10.5 %copy-start.8 = (bf16[256,1152]{1,0:T(8,128)(2,1)S(1)}, bf16[256,1152]{1,0:T(8,128)(2,1)}, u32[]{:S(2)}) copy-start(bf16[256,1152]{1,0:T(8,128)(2,1)} %get-tuple-element.46.own_ref) | copy-start | bytes 1769476
  43.3 19.1 %all-to-all-start.1 = ((bf16[32,8,1728]{2,1,0:T(8,128)(2,1)}), bf16[32,8,1728]{2,1,0:T(8,128)(2,1)}, u32[]{:S(2)}, u32[]{:S(2)}) async-start(bf16[32,8,1728]{2,1,0:T(8,128)(2,1)} %bitcast.31), calls=%async_computation.1 | async-start | bytes 1835008 | tf_op jit(solution)/shard_map/all_to_all | solution.py:468
  48.1 3.8 %collective-permute-start.1 = (bf16[256,1152]{1,0:T(8,128)(2,1)S(1)}, bf16[256,1152]{1,0:T(8,128)(2,1)S(1)}, u32[]{:S(2)}, u32[]{:S(2)}) collective-permute-start(bf16[256,1152]{1,0:T(8,128)(2,1)S(1)} %copy-done.6), channel_id=1, source_target_pairs={{0,1},{1,0},{2,3},{3,2},{4,5},{5,4},{6,7},{7,6},{8,9},{9,8},{10,11... | collective-permute-start | bytes 1769480 | tf_op jit(solution)/shard_map/ppermute | solution.py:464
  50.2 3.3 %collective-permute-start.2 = (bf16[256,1152]{1,0:T(8,128)(2,1)S(1)}, bf16[256,1152]{1,0:T(8,128)(2,1)S(1)}, u32[]{:S(2)}, u32[]{:S(2)}) collective-permute-start(bf16[256,1152]{1,0:T(8,128)(2,1)S(1)} %copy-done.7), channel_id=1, source_target_pairs={{0,1},{1,0},{2,3},{3,2},{4,5},{5,4},{6,7},{7,6},{8,9},{9,8},{10,11... | collective-permute-start | bytes 1769480 | tf_op jit(solution)/shard_map/ppermute | solution.py:464
  50.3 3.4 %collective-permute-start.3 = (bf16[256,1152]{1,0:T(8,128)(2,1)}, bf16[256,1152]{1,0:T(8,128)(2,1)S(1)}, u32[]{:S(2)}, u32[]{:S(2)}) collective-permute-start(bf16[256,1152]{1,0:T(8,128)(2,1)} %get-tuple-element.47), channel_id=1, source_target_pairs={{0,1},{1,0},{2,3},{3,2},{4,5},{5,4},{6,7},{7,6},{8,9},{9,8},{10,11... | collective-permute-start | bytes 1769480 | tf_op jit(solution)/shard_map/ppermute | solution.py:464
  53.7 9.1 %copy-start.5 = (bf16[256,1152]{1,0:T(8,128)(2,1)S(1)}, bf16[256,1152]{1,0:T(8,128)(2,1)}, u32[]{:S(2)}) copy-start(bf16[256,1152]{1,0:T(8,128)(2,1)} %get-tuple-element.41.in_own) | copy-start | bytes 1769476
  56.5 0.8 copy-start.9
  57.4 0.9 copy-start.11
  58.2 0.8 copy-start.13
  62.3 20.3 %collective-permute-start.10 = (bf16[288,1152]{1,0:T(8,128)(2,1)}, bf16[288,1152]{1,0:T(8,128)(2,1)S(1)}, u32[]{:S(2)}, u32[]{:S(2)}) collective-permute-start(bf16[288,1152]{1,0:T(8,128)(2,1)} %copy-done.13), channel_id=1, source_target_pairs={{0,64},{1,17},{2,66},{3,19},{4,68},{5,21},{6,70},{7,23},{8,72},{9,... | collective-permute-start | bytes 1990664 | tf_op jit(solution)/shard_map/ppermute | solution.py:490
  62.8 12.0 %collective-permute-start = (bf16[256,1152]{1,0:T(8,128)(2,1)S(1)}, bf16[256,1152]{1,0:T(8,128)(2,1)S(1)}, u32[]{:S(2)}, u32[]{:S(2)}) collective-permute-start(bf16[256,1152]{1,0:T(8,128)(2,1)S(1)} %copy-done.5), channel_id=1, source_target_pairs={{0,1},{1,0},{2,3},{3,2},{4,5},{5,4},{6,7},{7,6},{8,9},{9,8},{10,11... | collective-permute-start | bytes 1769480 | tf_op jit(solution)/shard_map/ppermute | solution.py:464
  66.2 7.7 %copy-start.12 = (bf16[288,1152]{1,0:T(8,128)(2,1)S(1)}, bf16[288,1152]{1,0:T(8,128)(2,1)}, u32[]{:S(2)}) copy-start(bf16[288,1152]{1,0:T(8,128)(2,1)} %copy-done.11) | copy-start | bytes 1990660
  66.2 8.6 %copy-start.10 = (bf16[288,1152]{1,0:T(8,128)(2,1)S(1)}, bf16[288,1152]{1,0:T(8,128)(2,1)}, u32[]{:S(2)}) copy-start(bf16[288,1152]{1,0:T(8,128)(2,1)} %copy-done.9) | copy-start | bytes 1990660
  73.4 2.3 %collective-permute-start.4 = (bf16[256,1152]{1,0:T(8,128)(2,1)}, bf16[256,1152]{1,0:T(8,128)(2,1)S(1)}, u32[]{:S(2)}, u32[]{:S(2)}) collective-permute-start(bf16[256,1152]{1,0:T(8,128)(2,1)} %get-tuple-element.55.out_own.dhidden_hbm), channel_id=1, source_target_pairs={{0,1},{1,0},{2,3},{3,2},{4,5},{5,4},{6,7},{7,6},{8,9},{9,8},{10,11... | collective-permute-start | bytes 1769480 | tf_op jit(solution)/shard_map/ppermute | solution.py:464
  73.5 2.8 %collective-permute-start.5 = (bf16[256,1152]{1,0:T(8,128)(2,1)S(1)}, bf16[256,1152]{1,0:T(8,128)(2,1)S(1)}, u32[]{:S(2)}, u32[]{:S(2)}) collective-permute-start(bf16[256,1152]{1,0:T(8,128)(2,1)S(1)} %get-tuple-element.57), channel_id=1, source_target_pairs={{0,1},{1,0},{2,3},{3,2},{4,5},{5,4},{6,7},{7,6},{8,9},{9,8},{10,11... | collective-permute-start | bytes 1769480 | tf_op jit(solution)/shard_map/ppermute | solution.py:464
  74.0 18.9 %collective-permute-start.11 = (bf16[288,1152]{1,0:T(8,128)(2,1)S(1)}, bf16[288,1152]{1,0:T(8,128)(2,1)S(1)}, u32[]{:S(2)}, u32[]{:S(2)}) collective-permute-start(bf16[288,1152]{1,0:T(8,128)(2,1)S(1)} %copy-done.12), channel_id=1, source_target_pairs={{0,96},{1,25},{2,98},{3,27},{4,100},{5,29},{6,102},{7,31},{8,104},... | collective-permute-start | bytes 1990664 | tf_op jit(solution)/shard_map/ppermute | solution.py:490
  74.9 18.1 %collective-permute-start.9 = (bf16[288,1152]{1,0:T(8,128)(2,1)S(1)}, bf16[288,1152]{1,0:T(8,128)(2,1)S(1)}, u32[]{:S(2)}, u32[]{:S(2)}) collective-permute-start(bf16[288,1152]{1,0:T(8,128)(2,1)S(1)} %copy-done.10), channel_id=1, source_target_pairs={{0,32},{1,9},{2,34},{3,11},{4,36},{5,13},{6,38},{7,15},{8,40},{9,1... | collective-permute-start | bytes 1990664 | tf_op jit(solution)/shard_map/ppermute | solution.py:490
  76.3 1.1 copy-start.2
  80.2 19.9 %collective-permute-start.6 = (bf16[288,1152]{1,0:T(8,128)(2,1)S(1)}, bf16[288,1152]{1,0:T(8,128)(2,1)S(1)}, u32[]{:S(2)}, u32[]{:S(2)}) collective-permute-start(bf16[288,1152]{1,0:T(8,128)(2,1)S(1)} %get-tuple-element.59), channel_id=1, source_target_pairs={{0,32},{1,9},{2,34},{3,11},{4,36},{5,13},{6,38},{7,15},{8,40},{9,1... | collective-permute-start | bytes 1990664 | tf_op jit(solution)/shard_map/ppermute | solution.py:490
  80.5 19.6 %collective-permute-start.7 = (bf16[288,1152]{1,0:T(8,128)(2,1)S(1)}, bf16[288,1152]{1,0:T(8,128)(2,1)S(1)}, u32[]{:S(2)}, u32[]{:S(2)}) collective-permute-start(bf16[288,1152]{1,0:T(8,128)(2,1)S(1)} %get-tuple-element.60), channel_id=1, source_target_pairs={{0,64},{1,17},{2,66},{3,19},{4,68},{5,21},{6,70},{7,23},{8,72},{9,... | collective-permute-start | bytes 1990664 | tf_op jit(solution)/shard_map/ppermute | solution.py:490
  82.7 17.4 %collective-permute-start.8 = (bf16[288,1152]{1,0:T(8,128)(2,1)S(1)}, bf16[288,1152]{1,0:T(8,128)(2,1)S(1)}, u32[]{:S(2)}, u32[]{:S(2)}) collective-permute-start(bf16[288,1152]{1,0:T(8,128)(2,1)S(1)} %get-tuple-element.61), channel_id=1, source_target_pairs={{0,96},{1,25},{2,98},{3,27},{4,100},{5,29},{6,102},{7,31},{8,104},... | collective-permute-start | bytes 1990664 | tf_op jit(solution)/shard_map/ppermute | solution.py:490
  87.7 5.2 %copy-start.4 = (bf16[768,288]{1,0:T(8,128)(2,1)S(1)}, bf16[768,288]{1,0:T(8,128)(2,1)}, u32[]{:S(2)}) copy-start(bf16[768,288]{1,0:T(8,128)(2,1)} %constant.4.clone.table_ref) | copy-start | bytes 1327108
  92.9 7.2 %copy-start.3 = (bf16[768,288]{1,0:T(8,128)(2,1)S(1)}, bf16[768,288]{1,0:T(8,128)(2,1)}, u32[]{:S(2)}) copy-start(bf16[768,288]{1,0:T(8,128)(2,1)} %constant.5.clone.table_ref) | copy-start | bytes 1327108
  126.7 1.5 %collective-permute-start.12 = (f32[2,9,1152]{2,1,0:T(8,128)S(1)}, f32[2,9,1152]{2,1,0:T(8,128)S(1)}, u32[]{:S(2)}, u32[]{:S(2)}) collective-permute-start(f32[2,9,1152]{2,1,0:T(8,128)S(1)} %get-tuple-element.71), channel_id=1, source_target_pairs={{0,1},{1,0},{2,3},{3,2},{4,5},{5,4},{6,7},{7,6},{8,9},{9,8},{10,11... | collective-permute-start | bytes 248840 | tf_op jit(solution)/shard_map/ppermute | solution.py:464

commit v4 on v3

--- a/solution.py
+++ b/solution.py
@@ -89,13 +89,16 @@
     return array[:, start:stop]
 
 
-def probs_t(query, keys, head, keep):
-    scores = dot_nt(head_part(keys, head), head_window(query, head)) * HEAD_DIM ** (-0.5)
+def soft_t(scores, keep):
     if keep is not None:
         scores = jnp.where(keep, scores, -1e30)
     peak = jnp.max(scores, axis=0, keepdims=True)
-    weights = jnp.exp(scores - peak)
-    return weights / jnp.sum(weights, axis=0, keepdims=True)
+    weights = jnp.exp2((scores - peak) * (HEAD_DIM ** (-0.5) * math.log2(math.e)))
+    return weights * (1.0 / jnp.sum(weights, axis=0, keepdims=True))
+
+
+def score_t(query, keys, head):
+    return dot_nt(head_part(keys, head), head_window(query, head))
 
 
 def same_patch(count, patches):
@@ -134,9 +137,11 @@
     store_qkv = pltpu.make_async_copy(qkv_ref, qkv_hbm, sems.at[7])
     store_qkv.start()
     mix = HeadSum()
-    for head in range(HEADS):
-        weights = probs_t(query, keys, head, None).astype(BF16)
-        mix.put(head, dot_tn(weights, head_window(values, head)))
+    for heads in (range(HEADS),):
+        scores = [score_t(query, keys, head) for head in heads]
+        weights = [soft_t(score, None).astype(BF16) for score in scores]
+        for head, weight in zip(heads, weights):
+            mix.put(head, dot_tn(weight, head_window(values, head)))
     attn = mix.whole(BF16)
     attn_ref[...] = attn
     store_attn = pltpu.make_async_copy(attn_ref, attn_hbm, sems.at[8])
@@ -149,17 +154,22 @@
 
 def attention_back(query, keys, values, dmix, keep, forward):
     mix, dq, dk, dv = HeadSum(), HeadSum(), HeadSum(), HeadSum()
-    for head in range(HEADS):
-        weights = probs_t(query, keys, head, keep)
-        rounded = weights.astype(BF16)
-        if forward:
-            mix.put(head, dot_tn(rounded, head_window(values, head)))
-        dprobs = dot_nt(head_part(values, head), head_window(dmix, head)).astype(BF16).astype(F32)
-        total = jnp.sum(weights * dprobs, axis=0, keepdims=True)
-        dscores = (weights * (dprobs - total) * HEAD_DIM ** (-0.5)).astype(BF16)
-        dv.put(head, dot_nn(rounded, head_window(dmix, head)))
-        dk.put(head, dot_nn(dscores, head_window(query, head)))
-        dq.put(head, dot_tn(dscores, head_window(keys, head)))
+    for heads in (range(HEADS),):
+        scores = [score_t(query, keys, head) for head in heads]
+        dprobs = [dot_nt(head_part(values, head), head_window(dmix, head)).astype(BF16) for head in heads]
+        weights = [soft_t(score, keep) for score in scores]
+        rounded = [weight.astype(BF16) for weight in weights]
+        dscores = []
+        for weight, dprob in zip(weights, dprobs):
+            dprob = dprob.astype(F32)
+            total = jnp.sum(weight * dprob, axis=0, keepdims=True)
+            dscores.append((weight * (dprob - total) * HEAD_DIM ** (-0.5)).astype(BF16))
+        for place, head in enumerate(heads):
+            if forward:
+                mix.put(head, dot_tn(rounded[place], head_window(values, head)))
+            dv.put(head, dot_nn(rounded[place], head_window(dmix, head)))
+            dk.put(head, dot_nn(dscores[place], head_window(query, head)))
+            dq.put(head, dot_tn(dscores[place], head_window(keys, head)))
     dqkv = jnp.concatenate([dq.whole(BF16), dk.whole(BF16), dv.whole(BF16)], axis=1)
     return (mix.whole(BF16) if forward else None), dqkv
 
@@ -210,8 +220,9 @@
 
 
 def space_backward(
-    cot_hbm, recv_hbm, w_out_hbm, qkv_hbm, attn_hbm, dhidden_hbm, dqkv_hbm, keep_ref, send_ref,
-    cot_ref, dres_ref, w_out_ref, qkv_ref, attn_ref, dhidden_ref, dqkv_ref, sems,
+    cot_hbm, recv_hbm, w_out_hbm, qkv_hbm, attn_hbm, normed_hbm,
+    dhidden_ref, dqkv_ref, keep_ref, send_ref, normed_ref,
+    cot_ref, dres_ref, w_out_ref, qkv_ref, attn_ref, sems,
 ):
     width = cot_ref.shape[1]
     loads = load_all(
@@ -221,6 +232,7 @@
             (w_out_hbm, w_out_ref),
             (qkv_hbm, qkv_ref),
             (attn_hbm, attn_ref),
+            (normed_hbm, normed_ref),
         ],
         sems,
     )
@@ -228,33 +240,24 @@
     loads[1].wait()
     dhidden = cot_ref[...] + dres_ref[...]
     dhidden_ref[...] = dhidden
-    stores = load_all([(dhidden_ref, dhidden_hbm)], sems, 5)
     loads[2].wait()
     dattn = dot_nt(dhidden, w_out_ref[...]).astype(BF16)
     loads[3].wait()
     query, keys, values = split_qkv(qkv_ref[...])
     dqkv = attention_back(query, keys, values, dattn, None, False)[1]
     dqkv_ref[...] = dqkv
-    stores += load_all([(dqkv_ref, dqkv_hbm)], sems, 6)
     loads[4].wait()
     pair_up(lax.axis_index("c"), dqkv, attn_ref[...], keep_ref, send_ref)
-    for store in stores:
-        store.wait()
-
-
-def space_finish(
-    x_hbm, dhidden_hbm, dqkv_hbm, w_qkv_hbm, grad_ref, x_ref, dhidden_ref, dqkv_ref, w_qkv_ref, sems
-):
-    loads = load_all(
-        [(x_hbm, x_ref), (dqkv_hbm, dqkv_ref), (w_qkv_hbm, w_qkv_ref), (dhidden_hbm, dhidden_ref)], sems
-    )
+    loads[5].wait()
+
+
+def space_finish(x_hbm, w_qkv_hbm, dhidden_ref, dqkv_ref, grad_ref, x_ref, w_qkv_ref, sems):
+    loads = load_all([(x_hbm, x_ref), (w_qkv_hbm, w_qkv_ref)], sems)
     loads[0].wait()
     normed, rate = norm_parts(x_ref[...].astype(F32))
     loads[1].wait()
-    loads[2].wait()
     dnormed = dot_nn(dqkv_ref[...], w_qkv_ref[...]).astype(BF16).astype(F32)
     dres = norm_back(dnormed, normed, rate).astype(BF16)
-    loads[3].wait()
     grad_ref[...] = dhidden_ref[...] + dres
 
 
@@ -524,24 +527,24 @@
     recv, terms_time = lax.optimization_barrier((recv, terms_time))
     got_time = along_lines(terms_time)
     wide = ((HK, width), BF16)
-    dhidden, dqkv_space, keep, give = call(
-        space_backward, [half, qkv, half, half],
-        top, recv, w_out_space, qkv_space, attn_space,
+    dhidden, dqkv_space, keep, give, normed_space = call(
+        space_backward, [half, qkv, half, half, half],
+        top, recv, w_out_space, qkv_space, attn_space, normed_space,
         flops=3 * 10**9,
-        hbm_in=5,
-        hbm_out=(0, 1),
-        scratch=buffers(half, half, wide, qkv, mix, half, qkv) + [pltpu.SemaphoreType.DMA((7,))],
+        hbm_in=6,
+        scratch=buffers(half, half, wide, qkv, mix) + [pltpu.SemaphoreType.DMA((6,))],
         grant=20,
     )
+    keep, got_time[1], got_time[3] = lax.optimization_barrier((keep, got_time[1], got_time[3]))
     terms_space = terms(
         normed_space, swap(normed_space), dhidden, swap(dhidden), keep, swap(give)
     )
     got_space = along_lines(terms_space)
     grad_clips = call(
-        space_finish, [half], x, dhidden, dqkv_space, w_qkv_space,
+        space_finish, [half], x, w_qkv_space, dhidden, dqkv_space,
         flops=10**9,
-        hbm_in=4,
-        scratch=buffers(half, half, qkv, ((qkv_cols, width), BF16)) + [pltpu.SemaphoreType.DMA((4,))],
+        hbm_in=2,
+        scratch=buffers(half, ((qkv_cols, width), BF16)) + [pltpu.SemaphoreType.DMA((2,))],
         grant=16,
     )[0]
     mixed = call(

time: 129 us -> 125 us (0.969)
  Pallas kernels: 40.1 us -> 36 us
  blocking collectives: 53 us -> 49.3 us
  waiting for transfers between devices: 14.3 us -> 18 us
  local copies, waits for them, and re-layouts: 3.64 us -> 1.71 us
  starting transfers between devices: 16.9 us -> 18.7 us
    pallas_call x11, Pallas kernels: 40.1 us -> 36 us  [call(): pl.pallas_call(kernel, out_shape=[pltpu.HBM(*out) if place in hbm_out els...]
    all_to_all x2, blocking collectives: 53 us -> 49.3 us  [exchange(): lax.all_to_all(array.reshape(parts, -1, lanes), axes, split_axis=0, conca...]
    unnamed x28 -> x18, local copies, waits for them, and re-layouts: 3.64 us -> 1.71 us
    ppermute x7, starting transfers between devices: 6.82 us -> 8.66 us  [swap(): return lax.ppermute(array, 'c', [(0, 1), (1, 0)])]
    ppermute x6, waiting for transfers between devices: 5.93 us -> 7.56 us  [along_lines(): lax.ppermute(part, ALL, line_pairs(step))]
  transfers between devices with their start and end apart: 14 -> 14, of which waited for: 8 -> 10; matrix products, arithmetic and copies ran while one was open for 0% -> 0% of each run, Pallas kernels for 18% -> 17%
where the time goes in v4:
time: 125 us
  blocking collectives  49.3 us (39%)
  Pallas kernels  36 us (29%)
  starting transfers between devices  18.7 us (15%)
  waiting for transfers between devices  18 us (14%)
  local copies, waits for them, and re-layouts  1.71 us (1%)
    all_to_all x2, blocking collectives, exchange(): lax.all_to_all(array.reshape(parts, -1, lanes), axes, split_axis=0, conca...  49.3 us
    pallas_call x11, Pallas kernels, call(): pl.pallas_call(kernel, out_shape=[pltpu.HBM(*out) if place in hbm_out els...  36 us
    ppermute x7, starting transfers between devices, swap(): return lax.ppermute(array, 'c', [(0, 1), (1, 0)])  8.66 us
    ppermute x6, waiting for transfers between devices, along_lines(): lax.ppermute(part, ALL, line_pairs(step))  7.56 us
    ppermute x7, waiting for transfers between devices, swap(): return lax.ppermute(array, 'c', [(0, 1), (1, 0)])  6.34 us
    ppermute x6, starting transfers between devices, along_lines(): lax.ppermute(part, ALL, line_pairs(step))  5.27 us
    all_to_all x1, starting transfers between devices, exchange(): lax.all_to_all(array.reshape(parts, -1, lanes), axes, split_axis=0, conca...  4.78 us
    all_to_all x1, waiting for transfers between devices, exchange(): lax.all_to_all(array.reshape(parts, -1, lanes), axes, split_axis=0, conca...  4.14 us
  transfers between devices with their start and end apart: 14, of which 10 were waited for; matrix products, arithmetic and copies ran while one was open for 0% of the time, Pallas kernels for 17%

profile of v4, /device:TPU:1, one launch (start us, length us, event | category | flops | bytes accessed | tf_op | source)
XLA Modules:
  0.0 124.6 jit_solution(6926204122070724605)
XLA Ops:
  0.6 5.8 %shard_map.127 = (bf16[256,2304]{1,0:T(8,128)(2,1)S(1)}, bf16[256,1728]{1,0:T(8,128)(2,1)}, bf16[256,576]{1,0:T(8,128)(2,1)}, bf16[256,1152]{1,0:T(8,128)(2,1)}) custom-call(bf16[256,1152]{1,0:T(8,128)(2,1)} %bitcast.26, bf16[256,1152]{1,0:T(8,128)(2,1)} %bitcast.29, bf16[1728,1152]{1,0:T(8,128)(2,1)} %bitcast.21, bf16[576,1152]{1,0:T(8,128)(2,1)} %bitcast.23), custom_call_target="tpu_custom_call" | custom-call | flops 3000000 | bytes 9437 | tf_op jit(solution)/shard_map/pallas_call | solution.py:271
  6.5 27.9 %all_to_all.15 = bf16[32,8,2304]{2,1,0:T(8,128)(2,1)S(1)} all-to-all(bf16[32,8,2304]{2,1,0:T(8,128)(2,1)S(1)} %bitcast.20), channel_id=1, replica_groups=mesh['z'=4,'y'=4,'xl'=2,'xh'=2,'c'=2] {'z','y','xl'}, dimensions={0} | all-to-all | bytes 2359296 | tf_op jit(solution)/shard_map/all_to_all | solution.py:471
  34.4 7.0 %shard_map.128 = (bf16[256,1728]{1,0:T(8,128)(2,1)}, bf16[256,1152]{1,0:T(8,128)(2,1)}, bf16[256,1152]{1,0:T(8,128)(2,1)}, bf16[256,1152]{1,0:T(8,128)(2,1)}, bf16[256,1152]{1,0:T(8,128)(2,1)}) custom-call(bf16[256,2304]{1,0:T(8,128)(2,1)S(1)} %bitcast.18, bf16[1728,1152]{1,0:T(8,128)(2,1)S(1)} %bitcast.19, bf16[576,1152]{1,0:T(8,128)(2,1)S(1)} %bitcast.17), custom_call_target="tpu_custom_call" | custom-call | flops 5000000 | bytes 9732 | tf_op jit(solution)/shard_map/pallas_call | solution.py:271
  41.5 4.8 %all-to-all-start.1 = ((bf16[32,8,1728]{2,1,0:T(8,128)(2,1)}), bf16[32,8,1728]{2,1,0:T(8,128)(2,1)}, u32[]{:S(2)}, u32[]{:S(2)}) async-start(bf16[32,8,1728]{2,1,0:T(8,128)(2,1)} %bitcast.31), calls=%async_computation.1 | async-start | bytes 1835008 | tf_op jit(solution)/shard_map/all_to_all | solution.py:471
  46.3 2.1 %collective-permute-start = (bf16[256,1152]{1,0:T(8,128)(2,1)S(1)}, bf16[256,1152]{1,0:T(8,128)(2,1)S(1)}, u32[]{:S(2)}, u32[]{:S(2)}) collective-permute-start(bf16[256,1152]{1,0:T(8,128)(2,1)S(1)} %copy-done.4), channel_id=1, source_target_pairs={{0,1},{1,0},{2,3},{3,2},{4,5},{5,4},{6,7},{7,6},{8,9},{9,8},{10,11... | collective-permute-start | bytes 1769480 | tf_op jit(solution)/shard_map/ppermute | solution.py:467
  48.9 1.1 collective-permute-done.in_got
  50.0 1.7 %collective-permute-done.1.out_got = bf16[256,1152]{1,0:T(8,128)(2,1)S(1)} collective-permute-done((bf16[256,1152]{1,0:T(8,128)(2,1)S(1)}, bf16[256,1152]{1,0:T(8,128)(2,1)S(1)}, u32[]{:S(2)}, u32[]{:S(2)}) %collective-permute-start.1) | collective-permute-done | bytes 589856 | tf_op jit(solution)/shard_map/ppermute | solution.py:467
  51.9 2.8 %shard_map.129 = (bf16[288,1152]{1,0:T(8,128)(2,1)S(1)}, bf16[288,1152]{1,0:T(8,128)(2,1)S(1)}, bf16[288,1152]{1,0:T(8,128)(2,1)S(1)}, bf16[288,1152]{1,0:T(8,128)(2,1)S(1)}) custom-call(bf16[256,1152]{1,0:T(8,128)(2,1)S(1)} %copy-done.4, bf16[256,1152]{1,0:T(8,128)(2,1)S(1)} %collective-permute-done.in_got, bf16[256,1152]{1,0:T(8,128)(2,1)S(1)} %copy-done.5, ...), custom_call_target="tpu_custom_call" | custom-call | flops 2000000 | bytes 6193 | tf_op jit(solution)/shard_map/pallas_call | solution.py:271
  54.8 0.8 copy-done.7
  55.6 0.8 copy-done.8
  56.4 4.1 %all-to-all-done.1 = bf16[32,8,1728]{2,1,0:T(8,128)(2,1)} async-done(((bf16[32,8,1728]{2,1,0:T(8,128)(2,1)}), bf16[32,8,1728]{2,1,0:T(8,128)(2,1)}, u32[]{:S(2)}, u32[]{:S(2)}) %all-to-all-start.1) | async-done | bytes 884768 | tf_op jit(solution)/shard_map/all_to_all | solution.py:471
  60.6 0.6 collective-permute-start.5
  61.2 2.1 %collective-permute-start.6 = (bf16[288,1152]{1,0:T(8,128)(2,1)}, bf16[288,1152]{1,0:T(8,128)(2,1)S(1)}, u32[]{:S(2)}, u32[]{:S(2)}) collective-permute-start(bf16[288,1152]{1,0:T(8,128)(2,1)} %copy-done.7), channel_id=1, source_target_pairs={{0,96},{1,25},{2,98},{3,27},{4,100},{5,29},{6,102},{7,31},{8,104},... | collective-permute-start | bytes 1990664 | tf_op jit(solution)/shard_map/ppermute | solution.py:493
  63.2 5.2 %shard_map.130 = (bf16[256,1152]{1,0:T(8,128)(2,1)S(1)}, bf16[256,1728]{1,0:T(8,128)(2,1)S(1)}, bf16[256,1152]{1,0:T(8,128)(2,1)S(1)}, bf16[256,1152]{1,0:T(8,128)(2,1)S(1)}, bf16[256,1152]{1,0:T(8,128)(2,1)S(1)}) custom-call(bf16[256,1152]{1,0:T(8,128)(2,1)} %bitcast.30, bf16[256,1728]{1,0:T(8,128)(2,1)} %bitcast.9.recv_hbm, bf16[576,1152]{1,0:T(8,128)(2,1)} %bitcast.24, ...), custom_call_target="tpu_custom_call" | custom-call | flops 3000000 | bytes 7815 | tf_op jit(solution)/shard_map/pallas_call | solution.py:271
  68.4 3.8 %collective-permute-start.3 = (bf16[256,1152]{1,0:T(8,128)(2,1)S(1)}, bf16[256,1152]{1,0:T(8,128)(2,1)S(1)}, u32[]{:S(2)}, u32[]{:S(2)}) collective-permute-start(bf16[256,1152]{1,0:T(8,128)(2,1)S(1)} %get-tuple-element.59.in_own), channel_id=1, source_target_pairs={{0,1},{1,0},{2,3},{3,2},{4,5},{5,4},{6,7},{7,6},{8,9},{9,8},{10,11... | collective-permute-start | bytes 1769480 | tf_op jit(solution)/shard_map/ppermute | solution.py:467
  72.7 0.5 collective-permute-start.11
  73.2 0.6 collective-permute-done.3.in_got
  73.8 0.8 collective-permute-done.4.out_got
  74.7 0.8 collective-permute-done.7.got_ref
  75.5 2.8 %shard_map.131 = (bf16[288,1152]{1,0:T(8,128)(2,1)S(1)}, bf16[288,1152]{1,0:T(8,128)(2,1)S(1)}, bf16[288,1152]{1,0:T(8,128)(2,1)S(1)}, bf16[288,1152]{1,0:T(8,128)(2,1)S(1)}) custom-call(bf16[256,1152]{1,0:T(8,128)(2,1)S(1)} %get-tuple-element.59.in_own, bf16[256,1152]{1,0:T(8,128)(2,1)S(1)} %collective-permute-done.3.in_got, ...), custom_call_target="tpu_custom_call" | custom-call | flops 2000000 | bytes 6193 | tf_op jit(solution)/shard_map/pallas_call | solution.py:271
  78.7 1.2 collective-permute-start.8
  79.9 0.6 collective-permute-start.9
  80.4 4.1 %shard_map.135 = bf16[256,1152]{1,0:T(8,128)(2,1)} custom-call(bf16[256,1152]{1,0:T(8,128)(2,1)} %bitcast.27, bf16[256,576]{1,0:T(8,128)(2,1)} %get-tuple-element.57.attn_hbm, bf16[576,1152]{1,0:T(8,128)(2,1)} %bitcast.25, bf16[256,1728]{1,0:T(8,128)(2,1)} %bitcast.9.recv_hbm, bf16[576,1152]{1,0:T(8,128)(2,1)} %bitcast.16), custom_call_target="tpu_custom_call" | custom-call | flops 1000000 | bytes 5013 | tf_op jit(solution)/shard_map/pallas_call | solution.py:271
  84.6 4.8 %shard_map.134 = bf16[256,1152]{1,0:T(8,128)(2,1)} custom-call(bf16[256,1152]{1,0:T(8,128)(2,1)} %bitcast.28, bf16[1728,1152]{1,0:T(8,128)(2,1)} %bitcast.22, bf16[256,1152]{1,0:T(8,128)(2,1)S(1)} %get-tuple-element.60.out_own.dhidden_ref, bf16[256,1728]{1,0:T(8,128)(2,1)S(1)} %get-tuple-element.74.dqkv_ref), custom_call_target="tpu_custom_call" | custom-call | flops 1000000 | bytes 6635 | tf_op jit(solution)/shard_map/pallas_call | solution.py:271
  89.4 1.3 %shard_map.132.refs_4_ = bf16[256,2688]{1,0:T(8,128)(2,1)S(1)} custom-call(bf16[768,288]{1,0:T(8,128)(2,1)S(1)} %copy-done.3, bf16[288,1152]{1,0:T(8,128)(2,1)S(1)} %get-tuple-element.70.refs_0_, bf16[288,1152]{1,0:T(8,128)(2,1)S(1)} %collective-permute-done.5.refs_1_, bf16[288,1152]{1,0:T(8,128)(2,1)S(1)} %collective-permute-done.11.refs_2_, ...), custom_call_target="tpu_custom_call" | custom-call | flops 1000000 | bytes 4472 | tf_op jit(solution)/shard_map/pallas_call | solution.py:271
  90.7 0.4 collective-permute-done.8.refs_1_
  91.1 7.1 %collective-permute-done.9.refs_2_ = bf16[288,1152]{1,0:T(8,128)(2,1)S(1)} collective-permute-done((bf16[288,1152]{1,0:T(8,128)(2,1)S(1)}, bf16[288,1152]{1,0:T(8,128)(2,1)S(1)}, u32[]{:S(2)}, u32[]{:S(2)}) %collective-permute-start.9) | collective-permute-done | bytes 663584 | tf_op jit(solution)/shard_map/ppermute | solution.py:493
  98.3 1.3 %shard_map.133 = bf16[256,2688]{1,0:T(8,128)(2,1)S(1)} custom-call(bf16[768,288]{1,0:T(8,128)(2,1)S(1)} %copy-done.2, bf16[288,1152]{1,0:T(8,128)(2,1)S(1)} %get-tuple-element.66.refs_0_, bf16[288,1152]{1,0:T(8,128)(2,1)S(1)} %collective-permute-done.8.refs_1_, bf16[288,1152]{1,0:T(8,128)(2,1)S(1)} %collective-permute-done.9.refs_2_, ...), custom_call_target="tpu_custom_call" | custom-call | flops 1000000 | bytes 5849 | tf_op jit(solution)/shard_map/pallas_call | solution.py:271
  99.5 21.4 %all_to_all.16 = bf16[16,16,2688]{2,1,0:T(8,128)(2,1)S(1)} all-to-all(bf16[16,16,2688]{2,1,0:T(8,128)(2,1)S(1)} %bitcast.14), channel_id=1, replica_groups={{0,2,4,6,8,10,12,14,16,18,20,22,24,26,28,30},{32,34,36,38,40,42,44,46,4..., dimensions={0} | all-to-all | bytes 2752512 | tf_op jit(solution)/shard_map/all_to_all | solution.py:471
  121.1 1.7 %collective-permute-start.12 = (f32[2,9,1152]{2,1,0:T(8,128)S(1)}, f32[2,9,1152]{2,1,0:T(8,128)S(1)}, u32[]{:S(2)}, u32[]{:S(2)}) collective-permute-start(f32[2,9,1152]{2,1,0:T(8,128)S(1)} %get-tuple-element.79), channel_id=1, source_target_pairs={{0,1},{1,0},{2,3},{3,2},{4,5},{5,4},{6,7},{7,6},{8,9},{9,8},{10,11... | collective-permute-start | bytes 248840 | tf_op jit(solution)/shard_map/ppermute | solution.py:467
  122.9 1.0 collective-permute-done.12.got_ref
  123.9 0.7 shard_map.137
  (27 shorter events, 1.8 us)
Async XLA Ops:
  0.6 33.8 %copy-start.1 = (bf16[1152,1728]{0,1:T(8,128)(2,1)S(1)}, bf16[1152,1728]{0,1:T(8,128)(2,1)}, u32[]{:S(2)}) copy-start(bf16[1152,1728]{0,1:T(8,128)(2,1)} %param.12) | copy-start | bytes 11943940
  6.5 27.9 %copy-start = (bf16[1152,576]{0,1:T(8,128)(2,1)S(1)}, bf16[1152,576]{0,1:T(8,128)(2,1)}, u32[]{:S(2)}) copy-start(bf16[1152,576]{0,1:T(8,128)(2,1)} %param.13) | copy-start | bytes 3981316
  41.4 4.8 %copy-start.4 = (bf16[256,1152]{1,0:T(8,128)(2,1)S(1)}, bf16[256,1152]{1,0:T(8,128)(2,1)}, u32[]{:S(2)}) copy-start(bf16[256,1152]{1,0:T(8,128)(2,1)} %get-tuple-element.47.in_own) | copy-start | bytes 1769476
  41.5 7.0 %copy-start.5 = (bf16[256,1152]{1,0:T(8,128)(2,1)S(1)}, bf16[256,1152]{1,0:T(8,128)(2,1)}, u32[]{:S(2)}) copy-start(bf16[256,1152]{1,0:T(8,128)(2,1)} %get-tuple-element.48.out_own) | copy-start | bytes 1769476
  41.5 10.5 %copy-start.6 = (bf16[256,1152]{1,0:T(8,128)(2,1)S(1)}, bf16[256,1152]{1,0:T(8,128)(2,1)}, u32[]{:S(2)}) copy-start(bf16[256,1152]{1,0:T(8,128)(2,1)} %get-tuple-element.49.own_ref) | copy-start | bytes 1769476
  41.5 19.1 %all-to-all-start.1 = ((bf16[32,8,1728]{2,1,0:T(8,128)(2,1)}), bf16[32,8,1728]{2,1,0:T(8,128)(2,1)}, u32[]{:S(2)}, u32[]{:S(2)}) async-start(bf16[32,8,1728]{2,1,0:T(8,128)(2,1)} %bitcast.31), calls=%async_computation.1 | async-start | bytes 1835008 | tf_op jit(solution)/shard_map/all_to_all | solution.py:471
  46.3 3.8 %collective-permute-start = (bf16[256,1152]{1,0:T(8,128)(2,1)S(1)}, bf16[256,1152]{1,0:T(8,128)(2,1)S(1)}, u32[]{:S(2)}, u32[]{:S(2)}) collective-permute-start(bf16[256,1152]{1,0:T(8,128)(2,1)S(1)} %copy-done.4), channel_id=1, source_target_pairs={{0,1},{1,0},{2,3},{3,2},{4,5},{5,4},{6,7},{7,6},{8,9},{9,8},{10,11... | collective-permute-start | bytes 1769480 | tf_op jit(solution)/shard_map/ppermute | solution.py:467
  48.4 3.3 %collective-permute-start.1 = (bf16[256,1152]{1,0:T(8,128)(2,1)S(1)}, bf16[256,1152]{1,0:T(8,128)(2,1)S(1)}, u32[]{:S(2)}, u32[]{:S(2)}) collective-permute-start(bf16[256,1152]{1,0:T(8,128)(2,1)S(1)} %copy-done.5), channel_id=1, source_target_pairs={{0,1},{1,0},{2,3},{3,2},{4,5},{5,4},{6,7},{7,6},{8,9},{9,8},{10,11... | collective-permute-start | bytes 1769480 | tf_op jit(solution)/shard_map/ppermute | solution.py:467
  48.5 3.4 %collective-permute-start.2 = (bf16[256,1152]{1,0:T(8,128)(2,1)}, bf16[256,1152]{1,0:T(8,128)(2,1)S(1)}, u32[]{:S(2)}, u32[]{:S(2)}) collective-permute-start(bf16[256,1152]{1,0:T(8,128)(2,1)} %get-tuple-element.50), channel_id=1, source_target_pairs={{0,1},{1,0},{2,3},{3,2},{4,5},{5,4},{6,7},{7,6},{8,9},{9,8},{10,11... | collective-permute-start | bytes 1769480 | tf_op jit(solution)/shard_map/ppermute | solution.py:467
  54.7 0.8 copy-start.7
  55.6 0.8 copy-start.8
  60.6 12.2 %collective-permute-start.5 = (bf16[288,1152]{1,0:T(8,128)(2,1)}, bf16[288,1152]{1,0:T(8,128)(2,1)S(1)}, u32[]{:S(2)}, u32[]{:S(2)}) collective-permute-start(bf16[288,1152]{1,0:T(8,128)(2,1)} %copy-done.8), channel_id=1, source_target_pairs={{0,32},{1,9},{2,34},{3,11},{4,36},{5,13},{6,38},{7,15},{8,40},{9,1... | collective-permute-start | bytes 1990664 | tf_op jit(solution)/shard_map/ppermute | solution.py:493
  61.2 12.0 %collective-permute-start.6 = (bf16[288,1152]{1,0:T(8,128)(2,1)}, bf16[288,1152]{1,0:T(8,128)(2,1)S(1)}, u32[]{:S(2)}, u32[]{:S(2)}) collective-permute-start(bf16[288,1152]{1,0:T(8,128)(2,1)} %copy-done.7), channel_id=1, source_target_pairs={{0,96},{1,25},{2,98},{3,27},{4,100},{5,29},{6,102},{7,31},{8,104},... | collective-permute-start | bytes 1990664 | tf_op jit(solution)/shard_map/ppermute | solution.py:493
  68.4 5.4 %collective-permute-start.3 = (bf16[256,1152]{1,0:T(8,128)(2,1)S(1)}, bf16[256,1152]{1,0:T(8,128)(2,1)S(1)}, u32[]{:S(2)}, u32[]{:S(2)}) collective-permute-start(bf16[256,1152]{1,0:T(8,128)(2,1)S(1)} %get-tuple-element.59.in_own), channel_id=1, source_target_pairs={{0,1},{1,0},{2,3},{3,2},{4,5},{5,4},{6,7},{7,6},{8,9},{9,8},{10,11... | collective-permute-start | bytes 1769480 | tf_op jit(solution)/shard_map/ppermute | solution.py:467
  72.2 2.5 %collective-permute-start.4 = (bf16[256,1152]{1,0:T(8,128)(2,1)S(1)}, bf16[256,1152]{1,0:T(8,128)(2,1)S(1)}, u32[]{:S(2)}, u32[]{:S(2)}) collective-permute-start(bf16[256,1152]{1,0:T(8,128)(2,1)S(1)} %get-tuple-element.60.out_own.dhidden_ref), channel_id=1, source_target_pairs={{0,1},{1,0},{2,3},{3,2},{4,5},{5,4},{6,7},{7,6},{8,9},{9,8},{10,11... | collective-permute-start | bytes 1769480 | tf_op jit(solution)/shard_map/ppermute | solution.py:467
  72.3 3.2 %collective-permute-start.7 = (bf16[256,1152]{1,0:T(8,128)(2,1)S(1)}, bf16[256,1152]{1,0:T(8,128)(2,1)S(1)}, u32[]{:S(2)}, u32[]{:S(2)}) collective-permute-start(bf16[256,1152]{1,0:T(8,128)(2,1)S(1)} %get-tuple-element.65), channel_id=1, source_target_pairs={{0,1},{1,0},{2,3},{3,2},{4,5},{5,4},{6,7},{7,6},{8,9},{9,8},{10,11... | collective-permute-start | bytes 1769480 | tf_op jit(solution)/shard_map/ppermute | solution.py:467
  72.7 16.7 %collective-permute-start.11 = (bf16[288,1152]{1,0:T(8,128)(2,1)S(1)}, bf16[288,1152]{1,0:T(8,128)(2,1)S(1)}, u32[]{:S(2)}, u32[]{:S(2)}) collective-permute-start(bf16[288,1152]{1,0:T(8,128)(2,1)S(1)} %get-tuple-element.72), channel_id=1, source_target_pairs={{0,64},{1,17},{2,66},{3,19},{4,68},{5,21},{6,70},{7,23},{8,72},{9,... | collective-permute-start | bytes 1990664 | tf_op jit(solution)/shard_map/ppermute | solution.py:493
  78.3 12.4 %collective-permute-start.10 = (bf16[288,1152]{1,0:T(8,128)(2,1)S(1)}, bf16[288,1152]{1,0:T(8,128)(2,1)S(1)}, u32[]{:S(2)}, u32[]{:S(2)}) collective-permute-start(bf16[288,1152]{1,0:T(8,128)(2,1)S(1)} %get-tuple-element.69), channel_id=1, source_target_pairs={{0,96},{1,25},{2,98},{3,27},{4,100},{5,29},{6,102},{7,31},{8,104},... | collective-permute-start | bytes 1990664 | tf_op jit(solution)/shard_map/ppermute | solution.py:493
  78.7 12.5 %collective-permute-start.8 = (bf16[288,1152]{1,0:T(8,128)(2,1)S(1)}, bf16[288,1152]{1,0:T(8,128)(2,1)S(1)}, u32[]{:S(2)}, u32[]{:S(2)}) collective-permute-start(bf16[288,1152]{1,0:T(8,128)(2,1)S(1)} %get-tuple-element.67), channel_id=1, source_target_pairs={{0,32},{1,9},{2,34},{3,11},{4,36},{5,13},{6,38},{7,15},{8,40},{9,1... | collective-permute-start | bytes 1990664 | tf_op jit(solution)/shard_map/ppermute | solution.py:493
  79.9 18.4 %collective-permute-start.9 = (bf16[288,1152]{1,0:T(8,128)(2,1)S(1)}, bf16[288,1152]{1,0:T(8,128)(2,1)S(1)}, u32[]{:S(2)}, u32[]{:S(2)}) collective-permute-start(bf16[288,1152]{1,0:T(8,128)(2,1)S(1)} %get-tuple-element.68), channel_id=1, source_target_pairs={{0,64},{1,17},{2,66},{3,19},{4,68},{5,21},{6,70},{7,23},{8,72},{9,... | collective-permute-start | bytes 1990664 | tf_op jit(solution)/shard_map/ppermute | solution.py:493
  84.6 4.8 %copy-start.3 = (bf16[768,288]{1,0:T(8,128)(2,1)S(1)}, bf16[768,288]{1,0:T(8,128)(2,1)}, u32[]{:S(2)}) copy-start(bf16[768,288]{1,0:T(8,128)(2,1)} %constant.4.clone.table_ref) | copy-start | bytes 1327108
  89.4 8.9 %copy-start.2 = (bf16[768,288]{1,0:T(8,128)(2,1)S(1)}, bf16[768,288]{1,0:T(8,128)(2,1)}, u32[]{:S(2)}) copy-start(bf16[768,288]{1,0:T(8,128)(2,1)} %constant.5.clone.table_ref) | copy-start | bytes 1327108
  121.1 2.7 %collective-permute-start.12 = (f32[2,9,1152]{2,1,0:T(8,128)S(1)}, f32[2,9,1152]{2,1,0:T(8,128)S(1)}, u32[]{:S(2)}, u32[]{:S(2)}) collective-permute-start(f32[2,9,1152]{2,1,0:T(8,128)S(1)} %get-tuple-element.79), channel_id=1, source_target_pairs={{0,1},{1,0},{2,3},{3,2},{4,5},{5,4},{6,7},{7,6},{8,9},{9,8},{10,11... | collective-permute-start | bytes 248840 | tf_op jit(solution)/shard_map/ppermute | solution.py:467

commit v5 on v4

--- a/solution.py
+++ b/solution.py
@@ -199,10 +199,16 @@
     for source, target in ((keep_ref, keep_hbm), (give_ref, give_hbm)):
         copies.append(pltpu.make_async_copy(source, target, sems.at[len(copies)]))
         copies[-1].start()
-    dnormed = dot_nn(dqkv, w_qkv_ref[...]).astype(BF16).astype(F32)
-    back_ref[:, :width] = norm_back(dnormed, normed, rate).astype(BF16)
-    copies.append(pltpu.make_async_copy(back_ref, back_hbm, sems.at[4]))
-    copies[-1].start()
+    count = back_ref.shape[0]
+    for start in range(0, count, count // 2):
+        block = slice(start, start + count // 2)
+        dnormed = dot_nn(dqkv[block], w_qkv_ref[...]).astype(BF16).astype(F32)
+        back_ref[block, :width] = norm_back(dnormed, normed[block], rate[block]).astype(BF16)
+        rows = pl.ds(start, count // 2)
+        copies.append(
+            pltpu.make_async_copy(back_ref.at[rows, :], back_hbm.at[rows, :], sems.at[len(copies)])
+        )
+        copies[-1].start()
     for copy in copies:
         copy.wait()
 
@@ -517,7 +523,7 @@
         recv, w_qkv_time, w_out_time,
         flops=5 * 10**9,
         hbm_out=(0, 1, 2, 3, 4),
-        scratch=buffers(pack, half, half, half) + [pltpu.SemaphoreType.DMA((5,))],
+        scratch=buffers(pack, half, half, half) + [pltpu.SemaphoreType.DMA((6,))],
         grant=16,
     )
     terms_time = terms(

time: 125 us -> 125 us (level)
  no operation moved by 1% of the time
where the time goes in v5:
time: 125 us; the launch traced here: 124 us
  blocking collectives  49.3 us (39%)
  Pallas kernels  35.9 us (29%)
  starting transfers between devices  18.7 us (15%)
  waiting for transfers between devices  18.1 us (14%)
  local copies, waits for them, and re-layouts  1.71 us (1%)
    all_to_all x2, blocking collectives, exchange(): lax.all_to_all(array.reshape(parts, -1, lanes), axes, split_axis=0, conca...  49.3 us
    pallas_call x11, Pallas kernels, call(): pl.pallas_call(kernel, out_shape=[pltpu.HBM(*out) if place in hbm_out els...  35.9 us
    ppermute x7, starting transfers between devices, swap(): return lax.ppermute(array, 'c', [(0, 1), (1, 0)])  8.63 us
    ppermute x6, waiting for transfers between devices, along_lines(): lax.ppermute(part, ALL, line_pairs(step))  7.57 us
    ppermute x7, waiting for transfers between devices, swap(): return lax.ppermute(array, 'c', [(0, 1), (1, 0)])  6.34 us
    ppermute x6, starting transfers between devices, along_lines(): lax.ppermute(part, ALL, line_pairs(step))  5.26 us
    all_to_all x1, starting transfers between devices, exchange(): lax.all_to_all(array.reshape(parts, -1, lanes), axes, split_axis=0, conca...  4.78 us
    all_to_all x1, waiting for transfers between devices, exchange(): lax.all_to_all(array.reshape(parts, -1, lanes), axes, split_axis=0, conca...  4.16 us
  transfers between devices with their start and end apart: 14, of which 10 were waited for; matrix products, arithmetic and copies ran while one was open for 0% of the time, Pallas kernels for 17%

profile of v5, /device:TPU:1, one launch (start us, length us, event | category | flops | bytes accessed | tf_op | source)
XLA Modules:
  0.0 124.5 jit_solution(16887448829876737378)
XLA Ops:
  0.6 5.8 %shard_map.127 = (bf16[256,2304]{1,0:T(8,128)(2,1)S(1)}, bf16[256,1728]{1,0:T(8,128)(2,1)}, bf16[256,576]{1,0:T(8,128)(2,1)}, bf16[256,1152]{1,0:T(8,128)(2,1)}) custom-call(bf16[256,1152]{1,0:T(8,128)(2,1)} %bitcast.26, bf16[256,1152]{1,0:T(8,128)(2,1)} %bitcast.29, bf16[1728,1152]{1,0:T(8,128)(2,1)} %bitcast.21, bf16[576,1152]{1,0:T(8,128)(2,1)} %bitcast.23), custom_call_target="tpu_custom_call" | custom-call | flops 3000000 | bytes 9437 | tf_op jit(solution)/shard_map/pallas_call | solution.py:277
  6.5 27.9 %all_to_all.15 = bf16[32,8,2304]{2,1,0:T(8,128)(2,1)S(1)} all-to-all(bf16[32,8,2304]{2,1,0:T(8,128)(2,1)S(1)} %bitcast.20), channel_id=1, replica_groups=mesh['z'=4,'y'=4,'xl'=2,'xh'=2,'c'=2] {'z','y','xl'}, dimensions={0} | all-to-all | bytes 2359296 | tf_op jit(solution)/shard_map/all_to_all | solution.py:477
  34.4 6.8 %shard_map.128 = (bf16[256,1728]{1,0:T(8,128)(2,1)}, bf16[256,1152]{1,0:T(8,128)(2,1)}, bf16[256,1152]{1,0:T(8,128)(2,1)}, bf16[256,1152]{1,0:T(8,128)(2,1)}, bf16[256,1152]{1,0:T(8,128)(2,1)}) custom-call(bf16[256,2304]{1,0:T(8,128)(2,1)S(1)} %bitcast.18, bf16[1728,1152]{1,0:T(8,128)(2,1)S(1)} %bitcast.19, bf16[576,1152]{1,0:T(8,128)(2,1)S(1)} %bitcast.17), custom_call_target="tpu_custom_call" | custom-call | flops 5000000 | bytes 9732 | tf_op jit(solution)/shard_map/pallas_call | solution.py:277
  41.3 4.8 %all-to-all-start.1 = ((bf16[32,8,1728]{2,1,0:T(8,128)(2,1)}), bf16[32,8,1728]{2,1,0:T(8,128)(2,1)}, u32[]{:S(2)}, u32[]{:S(2)}) async-start(bf16[32,8,1728]{2,1,0:T(8,128)(2,1)} %bitcast.31), calls=%async_computation.1 | async-start | bytes 1835008 | tf_op jit(solution)/shard_map/all_to_all | solution.py:477
  46.1 2.1 %collective-permute-start = (bf16[256,1152]{1,0:T(8,128)(2,1)S(1)}, bf16[256,1152]{1,0:T(8,128)(2,1)S(1)}, u32[]{:S(2)}, u32[]{:S(2)}) collective-permute-start(bf16[256,1152]{1,0:T(8,128)(2,1)S(1)} %copy-done.4), channel_id=1, source_target_pairs={{0,1},{1,0},{2,3},{3,2},{4,5},{5,4},{6,7},{7,6},{8,9},{9,8},{10,11... | collective-permute-start | bytes 1769480 | tf_op jit(solution)/shard_map/ppermute | solution.py:473
  48.8 1.1 collective-permute-done.in_got
  49.9 1.7 %collective-permute-done.1.out_got = bf16[256,1152]{1,0:T(8,128)(2,1)S(1)} collective-permute-done((bf16[256,1152]{1,0:T(8,128)(2,1)S(1)}, bf16[256,1152]{1,0:T(8,128)(2,1)S(1)}, u32[]{:S(2)}, u32[]{:S(2)}) %collective-permute-start.1) | collective-permute-done | bytes 589856 | tf_op jit(solution)/shard_map/ppermute | solution.py:473
  51.8 2.8 %shard_map.129 = (bf16[288,1152]{1,0:T(8,128)(2,1)S(1)}, bf16[288,1152]{1,0:T(8,128)(2,1)S(1)}, bf16[288,1152]{1,0:T(8,128)(2,1)S(1)}, bf16[288,1152]{1,0:T(8,128)(2,1)S(1)}) custom-call(bf16[256,1152]{1,0:T(8,128)(2,1)S(1)} %copy-done.4, bf16[256,1152]{1,0:T(8,128)(2,1)S(1)} %collective-permute-done.in_got, bf16[256,1152]{1,0:T(8,128)(2,1)S(1)} %copy-done.5, ...), custom_call_target="tpu_custom_call" | custom-call | flops 2000000 | bytes 6193 | tf_op jit(solution)/shard_map/pallas_call | solution.py:277
  54.6 0.8 copy-done.7
  55.4 0.8 copy-done.8
  56.2 4.2 %all-to-all-done.1 = bf16[32,8,1728]{2,1,0:T(8,128)(2,1)} async-done(((bf16[32,8,1728]{2,1,0:T(8,128)(2,1)}), bf16[32,8,1728]{2,1,0:T(8,128)(2,1)}, u32[]{:S(2)}, u32[]{:S(2)}) %all-to-all-start.1) | async-done | bytes 884768 | tf_op jit(solution)/shard_map/all_to_all | solution.py:477
  60.4 0.6 collective-permute-start.5
  61.0 2.1 %collective-permute-start.6 = (bf16[288,1152]{1,0:T(8,128)(2,1)}, bf16[288,1152]{1,0:T(8,128)(2,1)S(1)}, u32[]{:S(2)}, u32[]{:S(2)}) collective-permute-start(bf16[288,1152]{1,0:T(8,128)(2,1)} %copy-done.7), channel_id=1, source_target_pairs={{0,96},{1,25},{2,98},{3,27},{4,100},{5,29},{6,102},{7,31},{8,104},... | collective-permute-start | bytes 1990664 | tf_op jit(solution)/shard_map/ppermute | solution.py:499
  63.1 5.2 %shard_map.130 = (bf16[256,1152]{1,0:T(8,128)(2,1)S(1)}, bf16[256,1728]{1,0:T(8,128)(2,1)S(1)}, bf16[256,1152]{1,0:T(8,128)(2,1)S(1)}, bf16[256,1152]{1,0:T(8,128)(2,1)S(1)}, bf16[256,1152]{1,0:T(8,128)(2,1)S(1)}) custom-call(bf16[256,1152]{1,0:T(8,128)(2,1)} %bitcast.30, bf16[256,1728]{1,0:T(8,128)(2,1)} %bitcast.9.recv_hbm, bf16[576,1152]{1,0:T(8,128)(2,1)} %bitcast.24, ...), custom_call_target="tpu_custom_call" | custom-call | flops 3000000 | bytes 7815 | tf_op jit(solution)/shard_map/pallas_call | solution.py:277
  68.3 3.8 %collective-permute-start.3 = (bf16[256,1152]{1,0:T(8,128)(2,1)S(1)}, bf16[256,1152]{1,0:T(8,128)(2,1)S(1)}, u32[]{:S(2)}, u32[]{:S(2)}) collective-permute-start(bf16[256,1152]{1,0:T(8,128)(2,1)S(1)} %get-tuple-element.59.in_own), channel_id=1, source_target_pairs={{0,1},{1,0},{2,3},{3,2},{4,5},{5,4},{6,7},{7,6},{8,9},{9,8},{10,11... | collective-permute-start | bytes 1769480 | tf_op jit(solution)/shard_map/ppermute | solution.py:473
  72.6 0.5 collective-permute-start.11
  73.0 0.6 collective-permute-done.3.in_got
  73.7 0.8 collective-permute-done.4.out_got
  74.5 0.8 collective-permute-done.7.got_ref
  75.4 2.8 %shard_map.131 = (bf16[288,1152]{1,0:T(8,128)(2,1)S(1)}, bf16[288,1152]{1,0:T(8,128)(2,1)S(1)}, bf16[288,1152]{1,0:T(8,128)(2,1)S(1)}, bf16[288,1152]{1,0:T(8,128)(2,1)S(1)}) custom-call(bf16[256,1152]{1,0:T(8,128)(2,1)S(1)} %get-tuple-element.59.in_own, bf16[256,1152]{1,0:T(8,128)(2,1)S(1)} %collective-permute-done.3.in_got, ...), custom_call_target="tpu_custom_call" | custom-call | flops 2000000 | bytes 6193 | tf_op jit(solution)/shard_map/pallas_call | solution.py:277
  78.5 1.2 collective-permute-start.8
  79.7 0.6 collective-permute-start.9
  80.3 4.1 %shard_map.135 = bf16[256,1152]{1,0:T(8,128)(2,1)} custom-call(bf16[256,1152]{1,0:T(8,128)(2,1)} %bitcast.27, bf16[256,576]{1,0:T(8,128)(2,1)} %get-tuple-element.57.attn_hbm, bf16[576,1152]{1,0:T(8,128)(2,1)} %bitcast.25, bf16[256,1728]{1,0:T(8,128)(2,1)} %bitcast.9.recv_hbm, bf16[576,1152]{1,0:T(8,128)(2,1)} %bitcast.16), custom_call_target="tpu_custom_call" | custom-call | flops 1000000 | bytes 5013 | tf_op jit(solution)/shard_map/pallas_call | solution.py:277
  84.4 4.8 %shard_map.134 = bf16[256,1152]{1,0:T(8,128)(2,1)} custom-call(bf16[256,1152]{1,0:T(8,128)(2,1)} %bitcast.28, bf16[1728,1152]{1,0:T(8,128)(2,1)} %bitcast.22, bf16[256,1152]{1,0:T(8,128)(2,1)S(1)} %get-tuple-element.60.out_own.dhidden_ref, bf16[256,1728]{1,0:T(8,128)(2,1)S(1)} %get-tuple-element.74.dqkv_ref), custom_call_target="tpu_custom_call" | custom-call | flops 1000000 | bytes 6635 | tf_op jit(solution)/shard_map/pallas_call | solution.py:277
  89.3 1.3 %shard_map.132.refs_4_ = bf16[256,2688]{1,0:T(8,128)(2,1)S(1)} custom-call(bf16[768,288]{1,0:T(8,128)(2,1)S(1)} %copy-done.3, bf16[288,1152]{1,0:T(8,128)(2,1)S(1)} %get-tuple-element.70.refs_0_, bf16[288,1152]{1,0:T(8,128)(2,1)S(1)} %collective-permute-done.5.refs_1_, bf16[288,1152]{1,0:T(8,128)(2,1)S(1)} %collective-permute-done.11.refs_2_, ...), custom_call_target="tpu_custom_call" | custom-call | flops 1000000 | bytes 4472 | tf_op jit(solution)/shard_map/pallas_call | solution.py:277
  90.5 0.4 collective-permute-done.8.refs_1_
  91.0 7.1 %collective-permute-done.9.refs_2_ = bf16[288,1152]{1,0:T(8,128)(2,1)S(1)} collective-permute-done((bf16[288,1152]{1,0:T(8,128)(2,1)S(1)}, bf16[288,1152]{1,0:T(8,128)(2,1)S(1)}, u32[]{:S(2)}, u32[]{:S(2)}) %collective-permute-start.9) | collective-permute-done | bytes 663584 | tf_op jit(solution)/shard_map/ppermute | solution.py:499
  98.1 1.3 %shard_map.133 = bf16[256,2688]{1,0:T(8,128)(2,1)S(1)} custom-call(bf16[768,288]{1,0:T(8,128)(2,1)S(1)} %copy-done.2, bf16[288,1152]{1,0:T(8,128)(2,1)S(1)} %get-tuple-element.66.refs_0_, bf16[288,1152]{1,0:T(8,128)(2,1)S(1)} %collective-permute-done.8.refs_1_, bf16[288,1152]{1,0:T(8,128)(2,1)S(1)} %collective-permute-done.9.refs_2_, ...), custom_call_target="tpu_custom_call" | custom-call | flops 1000000 | bytes 5849 | tf_op jit(solution)/shard_map/pallas_call | solution.py:277
  99.4 21.4 %all_to_all.16 = bf16[16,16,2688]{2,1,0:T(8,128)(2,1)S(1)} all-to-all(bf16[16,16,2688]{2,1,0:T(8,128)(2,1)S(1)} %bitcast.14), channel_id=1, replica_groups={{0,2,4,6,8,10,12,14,16,18,20,22,24,26,28,30},{32,34,36,38,40,42,44,46,4..., dimensions={0} | all-to-all | bytes 2752512 | tf_op jit(solution)/shard_map/all_to_all | solution.py:477
  121.0 1.7 %collective-permute-start.12 = (f32[2,9,1152]{2,1,0:T(8,128)S(1)}, f32[2,9,1152]{2,1,0:T(8,128)S(1)}, u32[]{:S(2)}, u32[]{:S(2)}) collective-permute-start(f32[2,9,1152]{2,1,0:T(8,128)S(1)} %get-tuple-element.79), channel_id=1, source_target_pairs={{0,1},{1,0},{2,3},{3,2},{4,5},{5,4},{6,7},{7,6},{8,9},{9,8},{10,11... | collective-permute-start | bytes 248840 | tf_op jit(solution)/shard_map/ppermute | solution.py:473
  122.7 1.0 collective-permute-done.12.got_ref
  123.7 0.7 shard_map.137
  (27 shorter events, 1.8 us)
Async XLA Ops:
  0.6 33.8 %copy-start.1 = (bf16[1152,1728]{0,1:T(8,128)(2,1)S(1)}, bf16[1152,1728]{0,1:T(8,128)(2,1)}, u32[]{:S(2)}) copy-start(bf16[1152,1728]{0,1:T(8,128)(2,1)} %param.12) | copy-start | bytes 11943940
  6.5 27.9 %copy-start = (bf16[1152,576]{0,1:T(8,128)(2,1)S(1)}, bf16[1152,576]{0,1:T(8,128)(2,1)}, u32[]{:S(2)}) copy-start(bf16[1152,576]{0,1:T(8,128)(2,1)} %param.13) | copy-start | bytes 3981316
  41.3 4.8 %copy-start.4 = (bf16[256,1152]{1,0:T(8,128)(2,1)S(1)}, bf16[256,1152]{1,0:T(8,128)(2,1)}, u32[]{:S(2)}) copy-start(bf16[256,1152]{1,0:T(8,128)(2,1)} %get-tuple-element.47.in_own) | copy-start | bytes 1769476
  41.3 7.0 %copy-start.5 = (bf16[256,1152]{1,0:T(8,128)(2,1)S(1)}, bf16[256,1152]{1,0:T(8,128)(2,1)}, u32[]{:S(2)}) copy-start(bf16[256,1152]{1,0:T(8,128)(2,1)} %get-tuple-element.48.out_own) | copy-start | bytes 1769476
  41.3 10.5 %copy-start.6 = (bf16[256,1152]{1,0:T(8,128)(2,1)S(1)}, bf16[256,1152]{1,0:T(8,128)(2,1)}, u32[]{:S(2)}) copy-start(bf16[256,1152]{1,0:T(8,128)(2,1)} %get-tuple-element.49.own_ref) | copy-start | bytes 1769476
  41.3 19.1 %all-to-all-start.1 = ((bf16[32,8,1728]{2,1,0:T(8,128)(2,1)}), bf16[32,8,1728]{2,1,0:T(8,128)(2,1)}, u32[]{:S(2)}, u32[]{:S(2)}) async-start(bf16[32,8,1728]{2,1,0:T(8,128)(2,1)} %bitcast.31), calls=%async_computation.1 | async-start | bytes 1835008 | tf_op jit(solution)/shard_map/all_to_all | solution.py:477
  46.1 3.8 %collective-permute-start = (bf16[256,1152]{1,0:T(8,128)(2,1)S(1)}, bf16[256,1152]{1,0:T(8,128)(2,1)S(1)}, u32[]{:S(2)}, u32[]{:S(2)}) collective-permute-start(bf16[256,1152]{1,0:T(8,128)(2,1)S(1)} %copy-done.4), channel_id=1, source_target_pairs={{0,1},{1,0},{2,3},{3,2},{4,5},{5,4},{6,7},{7,6},{8,9},{9,8},{10,11... | collective-permute-start | bytes 1769480 | tf_op jit(solution)/shard_map/ppermute | solution.py:473
  48.2 3.3 %collective-permute-start.1 = (bf16[256,1152]{1,0:T(8,128)(2,1)S(1)}, bf16[256,1152]{1,0:T(8,128)(2,1)S(1)}, u32[]{:S(2)}, u32[]{:S(2)}) collective-permute-start(bf16[256,1152]{1,0:T(8,128)(2,1)S(1)} %copy-done.5), channel_id=1, source_target_pairs={{0,1},{1,0},{2,3},{3,2},{4,5},{5,4},{6,7},{7,6},{8,9},{9,8},{10,11... | collective-permute-start | bytes 1769480 | tf_op jit(solution)/shard_map/ppermute | solution.py:473
  48.4 3.4 %collective-permute-start.2 = (bf16[256,1152]{1,0:T(8,128)(2,1)}, bf16[256,1152]{1,0:T(8,128)(2,1)S(1)}, u32[]{:S(2)}, u32[]{:S(2)}) collective-permute-start(bf16[256,1152]{1,0:T(8,128)(2,1)} %get-tuple-element.50), channel_id=1, source_target_pairs={{0,1},{1,0},{2,3},{3,2},{4,5},{5,4},{6,7},{7,6},{8,9},{9,8},{10,11... | collective-permute-start | bytes 1769480 | tf_op jit(solution)/shard_map/ppermute | solution.py:473
  54.6 0.8 copy-start.7
  55.4 0.8 copy-start.8
  60.4 12.1 %collective-permute-start.5 = (bf16[288,1152]{1,0:T(8,128)(2,1)}, bf16[288,1152]{1,0:T(8,128)(2,1)S(1)}, u32[]{:S(2)}, u32[]{:S(2)}) collective-permute-start(bf16[288,1152]{1,0:T(8,128)(2,1)} %copy-done.8), channel_id=1, source_target_pairs={{0,32},{1,9},{2,34},{3,11},{4,36},{5,13},{6,38},{7,15},{8,40},{9,1... | collective-permute-start | bytes 1990664 | tf_op jit(solution)/shard_map/ppermute | solution.py:499
  61.0 12.0 %collective-permute-start.6 = (bf16[288,1152]{1,0:T(8,128)(2,1)}, bf16[288,1152]{1,0:T(8,128)(2,1)S(1)}, u32[]{:S(2)}, u32[]{:S(2)}) collective-permute-start(bf16[288,1152]{1,0:T(8,128)(2,1)} %copy-done.7), channel_id=1, source_target_pairs={{0,96},{1,25},{2,98},{3,27},{4,100},{5,29},{6,102},{7,31},{8,104},... | collective-permute-start | bytes 1990664 | tf_op jit(solution)/shard_map/ppermute | solution.py:499
  68.3 5.4 %collective-permute-start.3 = (bf16[256,1152]{1,0:T(8,128)(2,1)S(1)}, bf16[256,1152]{1,0:T(8,128)(2,1)S(1)}, u32[]{:S(2)}, u32[]{:S(2)}) collective-permute-start(bf16[256,1152]{1,0:T(8,128)(2,1)S(1)} %get-tuple-element.59.in_own), channel_id=1, source_target_pairs={{0,1},{1,0},{2,3},{3,2},{4,5},{5,4},{6,7},{7,6},{8,9},{9,8},{10,11... | collective-permute-start | bytes 1769480 | tf_op jit(solution)/shard_map/ppermute | solution.py:473
  72.0 2.5 %collective-permute-start.4 = (bf16[256,1152]{1,0:T(8,128)(2,1)S(1)}, bf16[256,1152]{1,0:T(8,128)(2,1)S(1)}, u32[]{:S(2)}, u32[]{:S(2)}) collective-permute-start(bf16[256,1152]{1,0:T(8,128)(2,1)S(1)} %get-tuple-element.60.out_own.dhidden_ref), channel_id=1, source_target_pairs={{0,1},{1,0},{2,3},{3,2},{4,5},{5,4},{6,7},{7,6},{8,9},{9,8},{10,11... | collective-permute-start | bytes 1769480 | tf_op jit(solution)/shard_map/ppermute | solution.py:473
  72.1 3.2 %collective-permute-start.7 = (bf16[256,1152]{1,0:T(8,128)(2,1)S(1)}, bf16[256,1152]{1,0:T(8,128)(2,1)S(1)}, u32[]{:S(2)}, u32[]{:S(2)}) collective-permute-start(bf16[256,1152]{1,0:T(8,128)(2,1)S(1)} %get-tuple-element.65), channel_id=1, source_target_pairs={{0,1},{1,0},{2,3},{3,2},{4,5},{5,4},{6,7},{7,6},{8,9},{9,8},{10,11... | collective-permute-start | bytes 1769480 | tf_op jit(solution)/shard_map/ppermute | solution.py:473
  72.6 16.7 %collective-permute-start.11 = (bf16[288,1152]{1,0:T(8,128)(2,1)S(1)}, bf16[288,1152]{1,0:T(8,128)(2,1)S(1)}, u32[]{:S(2)}, u32[]{:S(2)}) collective-permute-start(bf16[288,1152]{1,0:T(8,128)(2,1)S(1)} %get-tuple-element.72), channel_id=1, source_target_pairs={{0,64},{1,17},{2,66},{3,19},{4,68},{5,21},{6,70},{7,23},{8,72},{9,... | collective-permute-start | bytes 1990664 | tf_op jit(solution)/shard_map/ppermute | solution.py:499
  78.2 12.4 %collective-permute-start.10 = (bf16[288,1152]{1,0:T(8,128)(2,1)S(1)}, bf16[288,1152]{1,0:T(8,128)(2,1)S(1)}, u32[]{:S(2)}, u32[]{:S(2)}) collective-permute-start(bf16[288,1152]{1,0:T(8,128)(2,1)S(1)} %get-tuple-element.69), channel_id=1, source_target_pairs={{0,96},{1,25},{2,98},{3,27},{4,100},{5,29},{6,102},{7,31},{8,104},... | collective-permute-start | bytes 1990664 | tf_op jit(solution)/shard_map/ppermute | solution.py:499
  78.5 12.5 %collective-permute-start.8 = (bf16[288,1152]{1,0:T(8,128)(2,1)S(1)}, bf16[288,1152]{1,0:T(8,128)(2,1)S(1)}, u32[]{:S(2)}, u32[]{:S(2)}) collective-permute-start(bf16[288,1152]{1,0:T(8,128)(2,1)S(1)} %get-tuple-element.67), channel_id=1, source_target_pairs={{0,32},{1,9},{2,34},{3,11},{4,36},{5,13},{6,38},{7,15},{8,40},{9,1... | collective-permute-start | bytes 1990664 | tf_op jit(solution)/shard_map/ppermute | solution.py:499
  79.7 18.4 %collective-permute-start.9 = (bf16[288,1152]{1,0:T(8,128)(2,1)S(1)}, bf16[288,1152]{1,0:T(8,128)(2,1)S(1)}, u32[]{:S(2)}, u32[]{:S(2)}) collective-permute-start(bf16[288,1152]{1,0:T(8,128)(2,1)S(1)} %get-tuple-element.68), channel_id=1, source_target_pairs={{0,64},{1,17},{2,66},{3,19},{4,68},{5,21},{6,70},{7,23},{8,72},{9,... | collective-permute-start | bytes 1990664 | tf_op jit(solution)/shard_map/ppermute | solution.py:499
  84.4 4.8 %copy-start.3 = (bf16[768,288]{1,0:T(8,128)(2,1)S(1)}, bf16[768,288]{1,0:T(8,128)(2,1)}, u32[]{:S(2)}) copy-start(bf16[768,288]{1,0:T(8,128)(2,1)} %constant.4.clone.table_ref) | copy-start | bytes 1327108
  89.2 8.9 %copy-start.2 = (bf16[768,288]{1,0:T(8,128)(2,1)S(1)}, bf16[768,288]{1,0:T(8,128)(2,1)}, u32[]{:S(2)}) copy-start(bf16[768,288]{1,0:T(8,128)(2,1)} %constant.5.clone.table_ref) | copy-start | bytes 1327108
  121.0 2.7 %collective-permute-start.12 = (f32[2,9,1152]{2,1,0:T(8,128)S(1)}, f32[2,9,1152]{2,1,0:T(8,128)S(1)}, u32[]{:S(2)}, u32[]{:S(2)}) collective-permute-start(f32[2,9,1152]{2,1,0:T(8,128)S(1)} %get-tuple-element.79), channel_id=1, source_target_pairs={{0,1},{1,0},{2,3},{3,2},{4,5},{5,4},{6,7},{7,6},{8,9},{9,8},{10,11... | collective-permute-start | bytes 248840 | tf_op jit(solution)/shard_map/ppermute | solution.py:473
